TPU v7x, 512 devices: a whole 4x4x16 slice. The times are simulated.
512 devices in a mesh: grp: 16 (over x, z_hi), blk: 32 (over y, z_lo, core).
Axes of the slice: x: 4, y: 4, z: 16 (z_hi: 4, z_lo: 4; z = z_hi * 4 + z_lo), core: 2. Of those that a mesh axis runs over, the one named last changes fastest.
Arguments:
- raw_blocks: bfloat16 [64, 96, 64, 256], P('blk', 'grp'), may hold values from -1.5 to 1.5
- metric_factor: bfloat16 [256, 256], replicated, may hold values from -0.375 to 0.375
- sig_list: int32 [64, 96], P('blk', 'grp'), may hold values from 0 to 15, as said below
- live_count: int32 [64, 16], P('blk', 'grp'), may hold values from 1 to 6, as said below
Outputs:
- exchange: float32 [4096, 4096], P('blk', 'grp')
Inputs may be any that keep to these rules, and one draw needn't show every extreme that they name: `sig_list`: the 6 slots of one row block in one group name distinct orbital blocks. `live_count`: for every group, each aligned run of 2 row blocks holds a row block with all 6 slots live.
All inputs are finite; a program needn't handle non-finite values.
Results may differ from a plain program's by a relative error of at most 0.0011.
Values may be sent and summed in bfloat16 or wider, within the bound.
No kernel may reach another device: no remote copies, remote signals or barrier semaphores. Data moves between devices by JAX's collectives and lax.ppermute only.
A program may use at most 64 MiB of HBM per device.

v0:
```python
import jax
import jax.numpy as jnp
from jax import lax
from jax.sharding import PartitionSpec as P

NOB_DEV = 16


def contract(raw_blocks, metric_factor, live_count):
    product = jnp.einsum(
        "msua,ab->msub", raw_blocks, metric_factor, preferred_element_type=jnp.float32
    )
    live_mask = jnp.arange(raw_blocks.shape[1], dtype=jnp.int32)[None, :] < live_count
    return (product * live_mask[:, :, None, None].astype(jnp.float32)).astype(jnp.bfloat16)


def dense_rows(contracted, sig_list):
    one_hot = (sig_list[:, :, None] == jnp.arange(NOB_DEV, dtype=jnp.int32)[None, None, :]).astype(
        jnp.bfloat16
    )
    return jnp.einsum(
        "msn,msua->mnua", one_hot, contracted, preferred_element_type=jnp.float32
    ).astype(jnp.bfloat16)


def pair_blocks(dense, other_x, other_ids):
    chosen = jnp.take(dense, other_ids, axis=1)
    blocks = jnp.einsum("mlsua,lsva->mulv", chosen, other_x, preferred_element_type=jnp.float32)
    return blocks.reshape(dense.shape[0] * dense.shape[2], other_x.shape[0] * other_x.shape[2])


def shards(raw_blocks, metric_factor, sig_list, live_count):
    contracted = contract(raw_blocks, metric_factor, live_count)
    dense = dense_rows(contracted, sig_list)
    row_blocks = raw_blocks.shape[0]
    width = raw_blocks.shape[2]
    rows_here = row_blocks * width
    cycle_size = lax.axis_size("blk")
    strip = jnp.zeros((rows_here, cycle_size * rows_here), jnp.float32)
    piece_x = lax.all_gather(contracted, "blk", axis=0, tiled=True)
    piece_ids = lax.all_gather(sig_list, "blk", axis=0, tiled=True)
    piece_rows = piece_x.shape[0]
    step_rows = max([divisor for divisor in range(1, 17) if piece_rows % divisor == 0])

    def one_turn(turn_index, current):
        block_x = lax.dynamic_slice_in_dim(piece_x, turn_index * step_rows, step_rows, 0)
        block_ids = lax.dynamic_slice_in_dim(piece_ids, turn_index * step_rows, step_rows, 0)
        values = pair_blocks(dense, block_x, block_ids)
        return lax.dynamic_update_slice(current, values, (0, turn_index * step_rows * width))

    strip = lax.fori_loop(0, piece_rows // step_rows, one_turn, strip)
    summed = lax.psum_scatter(strip, "grp", scatter_dimension=1, tiled=True)
    return 0.25 * summed


def solution(mesh):
    placed = (P("blk", "grp", None, None), P(), P("blk", "grp"), P("blk", "grp"))
    return jax.shard_map(
        shards, mesh=mesh, in_specs=placed, out_specs=P("blk", "grp"), check_vma=False
    )
```

profile of v0, /device:TPU:1, one launch (start us, length us, event | category | flops | bytes accessed | tf_op | source)
XLA Modules:
  0.0 296.7 jit_solution(10704077531473205670)
XLA Ops:
  6.5 0.8 compare_convert_fusion
  7.5 1.9 fusion.13
  9.6 1.7 convolution_convert_fusion
  11.2 0.3 copy.15
  11.6 48.6 %all-gather = s32[32,2,6]{2,1,0:T(2,128)} all-gather(s32[1,2,6]{2,1,0:T(2,128)} %bitcast.43), channel_id=1, replica_groups=mesh['grp'=16,'blk'=32] {'blk'}, dimensions={0}, use_global_device_ids=true | all-gather | bytes 1584 | tf_op jit(solution)/shard_map/all_gather | solution.py:41
  60.2 39.6 %all-gather.3.cloned.1.call-done = bf16[64,6,64,256]{3,2,1,0:T(8,128)(2,1)} async-done(((bf16[2,6,64,256]{3,2,1,0:T(8,128)(2,1)}), bf16[64,6,64,256]{3,2,1,0:T(8,128)(2,1)}) %all-gather.3.cloned.1.call-update) | async-done | bytes 12582928 | tf_op jit(solution)/shard_map/all_gather | solution.py:40
  99.9 1.5 broadcast_in_dim.40
  101.4 61.6 %while.15 = (s32[]{:T(128)}, f32[128,4096]{1,0:T(8,128)}, bf16[64,6,64,256]{3,2,1,0:T(8,128)(2,1)}, s32[64,6]{1,0:T(8,128)}, bf16[2,16,64,256]{3,2,1,0:T(8,128)(...) while((s32[]{:T(128)}, f32[128,4096]{1,0:T(8,128)}, ...), condition=%wide.region_1.0_spmd, body=%wide.region_0.1_spmd.sunk | while | flops 405800512 | bytes 25696916 | solution.py:51
  101.4 0.7 compare_and_fusion.2
  102.2 5.9 %gather_fusion = bf16[96,2,64,256]{3,2,1,0:T(8,128)(2,1)} fusion(bf16[2,16,64,256]{3,2,1,0:T(8,128)(2,1)S(1)} %get-tuple-element.226, s32[1024]{0:T(1024)S(1)} %pad_clamp_fusion.2), kind=kCustom, calls=%fused_computation.clone.1 | custom fusion | bytes 12583296 | tf_op jit(solution)/shard_map/while/body/eval_jaxpr/jit(_take)/gather | solution.py:27
  108.1 6.9 %fusion.25 = f32[2,64,16,64]{1,3,0,2:T(8,128)S(1)} fusion(bf16[16,6,2,64,256]{4,3,2,1,0:T(8,128)(2,1)} %bitcast.42, pred[16,6]{1,0:T(8,128)(4,1)S(1)} %get-tuple-element.199, bf16[64,6,64,256]{3,2,1,0:T(8,128)(2,1)} %get-tuple-element.224, s32[]{:T(128)S(6)} %select_n.57), kind=kOutput, calls=%fused_computation.8.clone.1 | convolution fusion | flops 405798912 | bytes 9961572 | tf_op jit(solution)/shard_map/while/body/eval_jaxpr/mlsua,lsva->mulv/dot_general | solution.py:28
  115.0 0.5 copy.31
  115.6 0.3 reshape.63
  115.9 0.9 constant_dynamic-update-slice_fusion.2
  116.8 0.7 compare_and_fusion.2
  117.6 5.9 %gather_fusion = bf16[96,2,64,256]{3,2,1,0:T(8,128)(2,1)} fusion(bf16[2,16,64,256]{3,2,1,0:T(8,128)(2,1)S(1)} %get-tuple-element.226, s32[1024]{0:T(1024)S(1)} %pad_clamp_fusion.2), kind=kCustom, calls=%fused_computation.clone.1 | custom fusion | bytes 12583296 | tf_op jit(solution)/shard_map/while/body/eval_jaxpr/jit(_take)/gather | solution.py:27
  123.5 6.9 %fusion.25 = f32[2,64,16,64]{1,3,0,2:T(8,128)S(1)} fusion(bf16[16,6,2,64,256]{4,3,2,1,0:T(8,128)(2,1)} %bitcast.42, pred[16,6]{1,0:T(8,128)(4,1)S(1)} %get-tuple-element.199, bf16[64,6,64,256]{3,2,1,0:T(8,128)(2,1)} %get-tuple-element.224, s32[]{:T(128)S(6)} %select_n.57), kind=kOutput, calls=%fused_computation.8.clone.1 | convolution fusion | flops 405798912 | bytes 9961572 | tf_op jit(solution)/shard_map/while/body/eval_jaxpr/mlsua,lsva->mulv/dot_general | solution.py:28
  130.4 0.5 copy.31
  131.0 0.3 reshape.63
  131.3 0.9 constant_dynamic-update-slice_fusion.2
  132.2 0.7 compare_and_fusion.2
  133.0 6.0 %gather_fusion = bf16[96,2,64,256]{3,2,1,0:T(8,128)(2,1)} fusion(bf16[2,16,64,256]{3,2,1,0:T(8,128)(2,1)S(1)} %get-tuple-element.226, s32[1024]{0:T(1024)S(1)} %pad_clamp_fusion.2), kind=kCustom, calls=%fused_computation.clone.1 | custom fusion | bytes 12583296 | tf_op jit(solution)/shard_map/while/body/eval_jaxpr/jit(_take)/gather | solution.py:27
  138.9 6.9 %fusion.25 = f32[2,64,16,64]{1,3,0,2:T(8,128)S(1)} fusion(bf16[16,6,2,64,256]{4,3,2,1,0:T(8,128)(2,1)} %bitcast.42, pred[16,6]{1,0:T(8,128)(4,1)S(1)} %get-tuple-element.199, bf16[64,6,64,256]{3,2,1,0:T(8,128)(2,1)} %get-tuple-element.224, s32[]{:T(128)S(6)} %select_n.57), kind=kOutput, calls=%fused_computation.8.clone.1 | convolution fusion | flops 405798912 | bytes 9961572 | tf_op jit(solution)/shard_map/while/body/eval_jaxpr/mlsua,lsva->mulv/dot_general | solution.py:28
  145.9 0.5 copy.31
  146.7 0.9 constant_dynamic-update-slice_fusion.2
  147.6 0.7 compare_and_fusion.2
  148.4 6.0 %gather_fusion = bf16[96,2,64,256]{3,2,1,0:T(8,128)(2,1)} fusion(bf16[2,16,64,256]{3,2,1,0:T(8,128)(2,1)S(1)} %get-tuple-element.226, s32[1024]{0:T(1024)S(1)} %pad_clamp_fusion.2), kind=kCustom, calls=%fused_computation.clone.1 | custom fusion | bytes 12583296 | tf_op jit(solution)/shard_map/while/body/eval_jaxpr/jit(_take)/gather | solution.py:27
  154.3 6.9 %fusion.25 = f32[2,64,16,64]{1,3,0,2:T(8,128)S(1)} fusion(bf16[16,6,2,64,256]{4,3,2,1,0:T(8,128)(2,1)} %bitcast.42, pred[16,6]{1,0:T(8,128)(4,1)S(1)} %get-tuple-element.199, bf16[64,6,64,256]{3,2,1,0:T(8,128)(2,1)} %get-tuple-element.224, s32[]{:T(128)S(6)} %select_n.57), kind=kOutput, calls=%fused_computation.8.clone.1 | convolution fusion | flops 405798912 | bytes 9961572 | tf_op jit(solution)/shard_map/while/body/eval_jaxpr/mlsua,lsva->mulv/dot_general | solution.py:28
  161.2 0.5 copy.31
  162.1 0.9 constant_dynamic-update-slice_fusion.2
  163.0 125.2 %reduce-scatter.2.cloned.1.call-done = f32[128,256]{1,0:T(8,128)} async-done(((f32[128,4096]{1,0:T(8,128)}), f32[128,256]{1,0:T(8,128)}) %reduce-scatter.2.cloned.1.call-update) | async-done | bytes 131088 | tf_op jit(solution)/shard_map/reduce_scatter | solution.py:52
  288.2 1.6 broadcast_multiply_fusion
  (16 shorter events, 1.3 us)
Async XLA Ops:
  6.5 1.0 copy-start
  6.5 93.3 %all-gather.3.cloned.1.call-start = ((), (), s32[]{:S(2)}) async-start(), calls=%async_computation.1 | async-start | bytes 12976128 | tf_op jit(solution)/shard_map/all_gather | solution.py:40
  9.5 278.7 %reduce-scatter.2.cloned.1.call-start = ((), (), s32[]{:S(2)}) async-start(), calls=%async_computation.2 | async-start | bytes 2228224 | tf_op jit(solution)/shard_map/reduce_scatter | solution.py:52
Sparse Core Ops, SparseCore 0:
  9.6 90.1 all-gather.2
  163.1 125.0 reduce-scatter.1
where the time goes:
time: 297 us
  waiting for transfers between devices  165 us (56%)
  blocking collectives  48.6 us (16%)
  local copies, waits for them, and re-layouts  33 us (11%)
  matrix products  31.3 us (11%)
  between operations  13.4 us (5%)
  other arithmetic  5.18 us (2%)
    reduce_scatter x1, waiting for transfers between devices, shards(): summed = lax.psum_scatter(strip, 'grp', scatter_dimension=1, tiled=True)  125 us
    all_gather x1, blocking collectives, shards(): piece_ids = lax.all_gather(sig_list, 'blk', axis=0, tiled=True)  48.6 us
    all_gather x1, waiting for transfers between devices, shards(): piece_x = lax.all_gather(contracted, 'blk', axis=0, tiled=True)  39.6 us
    dot_general x4, matrix products, pair_blocks(): jnp.einsum('mlsua,lsva->mulv', chosen, other_x, preferred_element_type=jn...  27.7 us
    gather x4, local copies, waits for them, and re-layouts, pair_blocks(): chosen = jnp.take(dense, other_ids, axis=1)  23.8 us
  transfers between devices with their start and end apart: 2, of which 2 were waited for; matrix products, arithmetic and copies ran while one was open for 1% of the time, Pallas kernels for 0%

commit v1 on v0

v1 whole, which is shorter than its diff:
```python
import jax
import jax.numpy as jnp
from jax import lax
from jax.experimental import pallas as pl
from jax.experimental.pallas import tpu as pltpu
from jax.sharding import Mesh, PartitionSpec as P

AXES = ("x", "zh", "y", "zl", "c")
NOB = 16
SLOTS = 6
BS = 64
AUX = 256
RB = 2
HALF = RB * BS
CHIP = 2 * HALF
BODY = RB * SLOTS * BS
PAY = BODY + 16
TILE = HALF + 16
LEVELS = 32000.0
CROSS = (3, 2, 0, 1)
VMEM = pl.BlockSpec(memory_space=pltpu.VMEM)
SMEM = pl.BlockSpec(memory_space=pltpu.SMEM)


def params(mib):
    return pltpu.CompilerParams(vmem_limit_bytes=mib * 1024 * 1024)


def contract_kernel(raw_ref, metric_ref, sig_ref, live_ref, out_ref):
    for m in range(RB):
        for s in range(SLOTS):
            block = m * SLOTS + s
            product = jnp.dot(
                raw_ref[m, s], metric_ref[...], preferred_element_type=jnp.float32
            )
            live = (s < live_ref[m, 0]).astype(jnp.float32)
            out_ref[block * BS : (block + 1) * BS, :] = (product * live).astype(jnp.bfloat16)
    lane = lax.broadcasted_iota(jnp.int32, (16, AUX), 1)
    ids = jnp.zeros((16, AUX), jnp.int32)
    for m in range(RB):
        for s in range(SLOTS):
            ids = jnp.where(lane == m * SLOTS + s, sig_ref[m, s], ids)
    out_ref[BODY:, :] = ids.astype(jnp.float32).astype(jnp.bfloat16)


def encode(values):
    top = jnp.max(jnp.abs(values), axis=0, keepdims=True)
    exponent = jnp.ceil(jnp.log2(jnp.maximum(top, 1e-30)) + 1e-3)
    coded = jnp.round(values * (LEVELS * jnp.exp2(-exponent)))
    return coded.astype(jnp.int32).astype(jnp.int16), exponent.astype(jnp.int32).astype(jnp.int16)


def decode(ref, index):
    exponent = ref[index + (slice(HALF, TILE), slice(None))].astype(jnp.int32).astype(jnp.float32)
    scale = jnp.exp2(exponent[0:1, :]) * (1.0 / LEVELS)
    return ref[index + (slice(0, HALF), slice(None))].astype(jnp.int32).astype(jnp.float32) * scale


def store_tile(ref, index, values, first, width):
    coded, exponent = encode(values)
    lanes = slice(first, first + width)
    ref[index + (slice(0, HALF), lanes)] = coded
    ref[index + (slice(HALF, TILE), lanes)] = jnp.broadcast_to(exponent, (16, width))


def pairs_kernel(place_ref, ids_ref, *refs):
    mine, other, out_ref, left, column, across = refs[:6], refs[6:11], *refs[11:]
    y, core = place_ref[0], place_ref[1]
    left[...] = jnp.zeros_like(left)
    column[...] = jnp.zeros_like(column)
    across[...] = jnp.zeros_like(across)

    def scatter(src, ids_row, targets):
        for m in range(RB):
            for s in range(SLOTS):
                block = m * SLOTS + s
                orbital = ids_ref[ids_row, block]
                values = src[block * BS : (block + 1) * BS, :]
                lanes = pl.ds(pl.multiple_of(orbital * AUX, AUX), AUX)
                for target, first in targets:
                    rows = pl.ds(pl.multiple_of(first + m * BS, BS), BS)
                    target[rows, lanes] = values

    for d in range(4):
        targets = [(column, core * 4 * HALF + d * HALF)]
        scatter(mine[d], d, targets + ([(left, 0)] if d == 0 else []))
        scatter(other[d], 6 + d, [(column, (1 - core) * 4 * HALF + d * HALF)])
    scatter(mine[4], 4, [(across, core * HALF), (left, HALF)])
    scatter(other[4], 10, [(across, (1 - core) * HALF)])
    scatter(mine[5], 5, [(left, 2 * HALF)])

    nt = (((1,), (1,)), ((), ()))
    for j in range(2):
        part = lax.dot_general(
            left[...], column[j * 4 * HALF : (j + 1) * 4 * HALF, :], nt,
            preferred_element_type=jnp.float32,
        )
        for d in range(4):
            at = lax.rem(y + d, 4)
            for t in range(3):
                tile = 2 if t == 1 else (0 if t == 0 else 1)
                store_tile(
                    out_ref, (at, tile),
                    part[t * HALF : (t + 1) * HALF, d * HALF : (d + 1) * HALF], j * HALF, HALF,
                )
    rows = pl.ds(pl.multiple_of(core * 4 * HALF, 4 * HALF), 4 * HALF)
    part = lax.dot_general(column[rows, :], across[...], nt, preferred_element_type=jnp.float32)
    for d in range(4):
        store_tile(
            out_ref, (lax.rem(y + d, 4), 3), part[d * HALF : (d + 1) * HALF, :], 0, CHIP
        )


def middle_kernel(place_ref, in_ref, *outs):
    for r in range(4):
        m = lax.rem(r + 4 - place_ref[2], 4)
        total = decode(in_ref, (0, m))
        for source in range(1, 4):
            total = total + decode(in_ref, (source, m))
        coded, exponent = encode(total)
        outs[r][:HALF, :] = coded
        outs[r][HALF:, :] = jnp.broadcast_to(exponent, (16, CHIP))


def last_kernel(a, b, c, d, out_ref):
    out_ref[...] = 0.25 * (decode(a, ()) + decode(b, ()) + (decode(c, ()) + decode(d, ())))


def index_of(x, zh, y, zl, c):
    return (((x * 4 + zh) * 4 + y) * 4 + zl) * 2 + c


def final_round(r):
    pairs = []
    for x in range(4):
        for s in range(4):
            for y in range(4):
                for z in range(4):
                    kind = (r - s) % 4
                    dest = (
                        (x, z, y, z), (x, z, y, z ^ 1), (x, z, y, CROSS[z]), (y, CROSS[z], x, z)
                    )[kind]
                    for c in range(2):
                        pairs.append((index_of(x, s, y, z, c), index_of(*dest, c)))
    return pairs


def shards(raw_blocks, metric_factor, sig_list, live_count):
    place = jnp.stack([lax.axis_index("y"), lax.axis_index("c"), lax.axis_index("zh")]).astype(jnp.int32)
    own = pl.pallas_call(
        contract_kernel,
        out_shape=jax.ShapeDtypeStruct((PAY, AUX), jnp.bfloat16),
        in_specs=[VMEM, VMEM, SMEM, SMEM],
        out_specs=VMEM,
        compiler_params=params(16),
        name="contract",
    )(raw_blocks, metric_factor, sig_list, live_count)

    across = lax.ppermute(own, "zl", [(CROSS[z], z) for z in range(4)])
    near = lax.ppermute(own, "zl", [(z ^ 1, z) for z in range(4)])
    column = [own] + [lax.ppermute(own, "y", [((i + d) % 4, i) for i in range(4)]) for d in (1, 2, 3)]
    mine = column + [across, near]
    other = [lax.ppermute(a, "c", [(0, 1), (1, 0)]) for a in column + [across]]
    ids = jnp.stack([a[BODY, : RB * SLOTS] for a in mine + other]).astype(jnp.int32)

    tiles = pl.pallas_call(
        pairs_kernel,
        out_shape=jax.ShapeDtypeStruct((4, 4, TILE, CHIP), jnp.int16),
        in_specs=[SMEM, SMEM] + [VMEM] * 11,
        out_specs=VMEM,
        scratch_shapes=[
            pltpu.VMEM((3 * HALF, NOB * AUX), jnp.bfloat16),
            pltpu.VMEM((8 * HALF, NOB * AUX), jnp.bfloat16),
            pltpu.VMEM((CHIP, NOB * AUX), jnp.bfloat16),
        ],
        compiler_params=params(48),
        name="pairs",
    )(place, ids, *mine, *other)
    arrived = lax.all_to_all(tiles, "x", 0, 0, tiled=True)
    coded = jax.ShapeDtypeStruct((TILE, CHIP), jnp.int16)
    messages = pl.pallas_call(
        middle_kernel,
        out_shape=[coded] * 4,
        in_specs=[SMEM, VMEM],
        out_specs=[VMEM] * 4,
        compiler_params=params(16),
        name="middle",
    )(place, arrived)
    received = [lax.ppermute(a, AXES, final_round(r)) for r, a in enumerate(messages)]
    return pl.pallas_call(
        last_kernel,
        out_shape=jax.ShapeDtypeStruct((HALF, CHIP), jnp.float32),
        in_specs=[VMEM] * 4,
        out_specs=VMEM,
        compiler_params=params(16),
        name="last",
    )(*received)


def solution(mesh):
    fine = Mesh(mesh.devices.reshape(4, 4, 4, 4, 2), AXES)
    blk, grp = ("y", "zl", "c"), ("x", "zh")
    placed = (P(blk, grp, None, None), P(), P(blk, grp), P(blk, grp))
    return jax.shard_map(shards, mesh=fine, in_specs=placed, out_specs=P(blk, grp), check_vma=False)
```

time: 297 us -> 110 us (0.37)
  the two profiles are of different devices: /device:TPU:1 before, /device:TPU:36 now
where the time goes in v1:
time: 110 us; the launch traced here: 109 us
  starting transfers between devices  57.6 us (52%)
  blocking collectives  18.9 us (17%)
  waiting for transfers between devices  17 us (15%)
  Pallas kernels  9.82 us (9%)
  local copies, waits for them, and re-layouts  5.39 us (5%)
    ppermute x4, starting transfers between devices, shards(): lax.ppermute(a, AXES, final_round(r))  28.3 us
    all_to_all x1, blocking collectives, shards(): arrived = lax.all_to_all(tiles, 'x', 0, 0, tiled=True)  18.9 us
    ppermute x3, starting transfers between devices, shards(): lax.ppermute(own, 'y', [((i + d) % 4, i) for i in range(4)])  11.6 us
    ppermute x4, waiting for transfers between devices, shards(): lax.ppermute(a, AXES, final_round(r))  10.6 us
    ppermute x5, starting transfers between devices, shards(): other = [lax.ppermute(a, 'c', [(0, 1), (1, 0)]) for a in column + [across]]  10.6 us
    pallas_call x1, Pallas kernels, shards(): pl.pallas_call(pairs_kernel, out_shape=jax.ShapeDtypeStruct((4, 4, TILE,...  7.23 us
    ppermute x1, starting transfers between devices, shards(): across = lax.ppermute(own, 'zl', [(CROSS[z], z) for z in range(4)])  5.18 us
    ppermute x1, waiting for transfers between devices, shards(): across = lax.ppermute(own, 'zl', [(CROSS[z], z) for z in range(4)])  3.79 us
  transfers between devices with their start and end apart: 14, of which 4 were waited for; matrix products, arithmetic and copies ran while one was open for 1% of the time, Pallas kernels for 0%

profile of v1, /device:TPU:36, one launch (start us, length us, event | category | flops | bytes accessed | tf_op | source)
XLA Modules:
  0.0 109.0 jit_solution(970996245230277235)
XLA Ops:
  0.0 0.7 copy.5.live_ref
  0.7 1.0 copy-done
  1.7 0.9 copy-done.1
  2.6 0.7 copy-done.2
  3.3 0.9 contract.1.refs_0_
  4.3 1.9 %collective-permute-start.5 = (bf16[784,256]{1,0:T(8,128)(2,1)S(1)}, bf16[784,256]{1,0:T(8,128)(2,1)S(1)}, u32[]{:S(2)}, u32[]{:S(2)}) collective-permute-start(bf16[784,256]{1,0:T(8,128)(2,1)S(1)} %contract.1.refs_0_), channel_id=1, source_target_pairs={{0,1},{1,0},{2,3},{3,2},{4,5},{5,4},{6,7},{7,6},{8,9},{9,8},{10,11... | collective-permute-start | bytes 1204232 | tf_op jit(solution)/shard_map/ppermute | solution.py:163
  6.2 5.2 %collective-permute-start.3 = (bf16[784,256]{1,0:T(8,128)(2,1)S(1)}, bf16[784,256]{1,0:T(8,128)(2,1)S(1)}, u32[]{:S(2)}, u32[]{:S(2)}) collective-permute-start(bf16[784,256]{1,0:T(8,128)(2,1)S(1)} %contract.1.refs_0_), channel_id=1, source_target_pairs={{6,0},{4,2},{0,4},{2,6},{7,1},{5,3},{1,5},{3,7},{14,8},{12,10},{8,... | collective-permute-start | bytes 1204232 | tf_op jit(solution)/shard_map/ppermute | solution.py:159
  11.4 3.5 %collective-permute-start.2 = (bf16[784,256]{1,0:T(8,128)(2,1)S(1)}, bf16[784,256]{1,0:T(8,128)(2,1)S(1)}, u32[]{:S(2)}, u32[]{:S(2)}) collective-permute-start(bf16[784,256]{1,0:T(8,128)(2,1)S(1)} %contract.1.refs_0_), channel_id=1, source_target_pairs={{24,0},{0,8},{8,16},{16,24},{25,1},{1,9},{9,17},{17,25},{26,2},{2,... | collective-permute-start | bytes 1204232 | tf_op jit(solution)/shard_map/ppermute | solution.py:161
  14.9 4.8 %collective-permute-start.1 = (bf16[784,256]{1,0:T(8,128)(2,1)S(1)}, bf16[784,256]{1,0:T(8,128)(2,1)S(1)}, u32[]{:S(2)}, u32[]{:S(2)}) collective-permute-start(bf16[784,256]{1,0:T(8,128)(2,1)S(1)} %contract.1.refs_0_), channel_id=1, source_target_pairs={{16,0},{24,8},{0,16},{8,24},{17,1},{25,9},{1,17},{9,25},{18,2},{26... | collective-permute-start | bytes 1204232 | tf_op jit(solution)/shard_map/ppermute | solution.py:161
  19.7 3.3 %collective-permute-start = (bf16[784,256]{1,0:T(8,128)(2,1)S(1)}, bf16[784,256]{1,0:T(8,128)(2,1)S(1)}, u32[]{:S(2)}, u32[]{:S(2)}) collective-permute-start(bf16[784,256]{1,0:T(8,128)(2,1)S(1)} %contract.1.refs_0_), channel_id=1, source_target_pairs={{8,0},{16,8},{24,16},{0,24},{9,1},{17,9},{25,17},{1,25},{10,2},{18... | collective-permute-start | bytes 1204232 | tf_op jit(solution)/shard_map/ppermute | solution.py:161
  23.0 2.0 %collective-permute-start.4 = (bf16[784,256]{1,0:T(8,128)(2,1)S(1)}, bf16[784,256]{1,0:T(8,128)(2,1)S(1)}, u32[]{:S(2)}, u32[]{:S(2)}) collective-permute-start(bf16[784,256]{1,0:T(8,128)(2,1)S(1)} %contract.1.refs_0_), channel_id=1, source_target_pairs={{2,0},{0,2},{6,4},{4,6},{3,1},{1,3},{7,5},{5,7},{10,8},{8,10},{14,... | collective-permute-start | bytes 1204232 | tf_op jit(solution)/shard_map/ppermute | solution.py:160
  25.0 3.8 %collective-permute-done.3.refs_4_ = bf16[784,256]{1,0:T(8,128)(2,1)S(1)} collective-permute-done((bf16[784,256]{1,0:T(8,128)(2,1)S(1)}, bf16[784,256]{1,0:T(8,128)(2,1)S(1)}, u32[]{:S(2)}, u32[]{:S(2)}) %collective-permute-start.3) | collective-permute-done | bytes 401440 | tf_op jit(solution)/shard_map/ppermute | solution.py:159
  28.8 1.9 %collective-permute-start.9 = (bf16[784,256]{1,0:T(8,128)(2,1)S(1)}, bf16[784,256]{1,0:T(8,128)(2,1)S(1)}, u32[]{:S(2)}, u32[]{:S(2)}) collective-permute-start(bf16[784,256]{1,0:T(8,128)(2,1)S(1)} %collective-permute-done.3.refs_4_), channel_id=1, source_target_pairs={{0,1},{1,0},{2,3},{3,2},{4,5},{5,4},{6,7},{7,6},{8,9},{9,8},{10,11... | collective-permute-start | bytes 1204232 | tf_op jit(solution)/shard_map/ppermute | solution.py:163
  30.8 2.4 %collective-permute-start.8 = (bf16[784,256]{1,0:T(8,128)(2,1)S(1)}, bf16[784,256]{1,0:T(8,128)(2,1)}, u32[]{:S(2)}, u32[]{:S(2)}) collective-permute-start(bf16[784,256]{1,0:T(8,128)(2,1)S(1)} %collective-permute-done.2.refs_3_), channel_id=1, source_target_pairs={{0,1},{1,0},{2,3},{3,2},{4,5},{5,4},{6,7},{7,6},{8,9},{9,8},{10,11... | collective-permute-start | bytes 1204232 | tf_op jit(solution)/shard_map/ppermute | solution.py:163
  33.1 2.6 %collective-permute-done.1.refs_2_ = bf16[784,256]{1,0:T(8,128)(2,1)S(1)} collective-permute-done((bf16[784,256]{1,0:T(8,128)(2,1)S(1)}, bf16[784,256]{1,0:T(8,128)(2,1)S(1)}, u32[]{:S(2)}, u32[]{:S(2)}) %collective-permute-start.1) | collective-permute-done | bytes 401440 | tf_op jit(solution)/shard_map/ppermute | solution.py:161
  35.7 1.9 %collective-permute-start.7 = (bf16[784,256]{1,0:T(8,128)(2,1)S(1)}, bf16[784,256]{1,0:T(8,128)(2,1)}, u32[]{:S(2)}, u32[]{:S(2)}) collective-permute-start(bf16[784,256]{1,0:T(8,128)(2,1)S(1)} %collective-permute-done.1.refs_2_), channel_id=1, source_target_pairs={{0,1},{1,0},{2,3},{3,2},{4,5},{5,4},{6,7},{7,6},{8,9},{9,8},{10,11... | collective-permute-start | bytes 1204232 | tf_op jit(solution)/shard_map/ppermute | solution.py:163
  37.7 2.4 %collective-permute-start.6 = (bf16[784,256]{1,0:T(8,128)(2,1)S(1)}, bf16[784,256]{1,0:T(8,128)(2,1)}, u32[]{:S(2)}, u32[]{:S(2)}) collective-permute-start(bf16[784,256]{1,0:T(8,128)(2,1)S(1)} %collective-permute-done.refs_1_), channel_id=1, source_target_pairs={{0,1},{1,0},{2,3},{3,2},{4,5},{5,4},{6,7},{7,6},{8,9},{9,8},{10,11... | collective-permute-start | bytes 1204232 | tf_op jit(solution)/shard_map/ppermute | solution.py:163
  40.1 0.1 pad_add_fusion.place_ref
  40.3 0.7 slice.53
  40.9 0.7 slice.52
  41.6 0.7 slice.51
  42.3 0.1 stack.19
  42.3 7.2 %pairs.1 = s16[4,4,144,256]{3,2,1,0:T(8,128)(2,1)S(1)} custom-call(s32[3]{0:T(128)S(1)} %pad_add_fusion.place_ref, s32[11,12]{1,0:T(8,128)S(1)} %convert_element_type.3.ids_ref, bf16[784,256]{1,0:T(8,128)(2,1)S(1)} %contract.1.refs_0_, bf16[784,256]{1,0:T(8,128)(2,1)S(1)} %collective-permute-done.refs_1_, ...), custom_call_target="tpu_custom_call" | custom-call | tf_op jit(solution)/shard_map/pairs/pallas_call | solution.py:166
  49.6 18.9 %all_to_all.5.in_ref = s16[4,4,144,256]{3,2,1,0:T(8,128)(2,1)S(1)} all-to-all(s16[4,4,144,256]{3,2,1,0:T(8,128)(2,1)S(1)} %pairs.1), channel_id=1, replica_groups=mesh['x'=4,'zh'=4,'y'=4,'zl'=4,'c'=2] {'x'}, dimensions={0} | all-to-all | bytes 2359296 | tf_op jit(solution)/shard_map/all_to_all | solution.py:179
  68.4 0.9 middle.1
  69.4 9.1 %collective-permute-start.10 = (s16[144,256]{1,0:T(8,128)(2,1)S(1)}, s16[144,256]{1,0:T(8,128)(2,1)S(1)}, u32[]{:S(2)}, u32[]{:S(2)}) collective-permute-start(s16[144,256]{1,0:T(8,128)(2,1)S(1)} %get-tuple-element.9), channel_id=1, source_target_pairs={{0,0},{1,1},{2,34},{3,35},{4,68},{5,69},{6,102},{7,103},{8,8},{9,9... | collective-permute-start | bytes 221192 | tf_op jit(solution)/shard_map/ppermute | solution.py:189
  78.5 12.2 %collective-permute-start.11 = (s16[144,256]{1,0:T(8,128)(2,1)S(1)}, s16[144,256]{1,0:T(8,128)(2,1)S(1)}, u32[]{:S(2)}, u32[]{:S(2)}) collective-permute-start(s16[144,256]{1,0:T(8,128)(2,1)S(1)} %get-tuple-element.10), channel_id=1, source_target_pairs={{0,2},{1,3},{2,32},{3,33},{4,70},{5,71},{6,100},{7,101},{8,10},{9,... | collective-permute-start | bytes 221192 | tf_op jit(solution)/shard_map/ppermute | solution.py:189
  90.7 1.9 %collective-permute-start.12 = (s16[144,256]{1,0:T(8,128)(2,1)S(1)}, s16[144,256]{1,0:T(8,128)(2,1)S(1)}, u32[]{:S(2)}, u32[]{:S(2)}) collective-permute-start(s16[144,256]{1,0:T(8,128)(2,1)S(1)} %get-tuple-element.11), channel_id=1, source_target_pairs={{0,6},{1,7},{2,36},{3,37},{4,64},{5,65},{6,98},{7,99},{8,14},{9,15... | collective-permute-start | bytes 221192 | tf_op jit(solution)/shard_map/ppermute | solution.py:189
  92.6 5.0 %collective-permute-start.13 = (s16[144,256]{1,0:T(8,128)(2,1)S(1)}, s16[144,256]{1,0:T(8,128)(2,1)S(1)}, u32[]{:S(2)}, u32[]{:S(2)}) collective-permute-start(s16[144,256]{1,0:T(8,128)(2,1)S(1)} %get-tuple-element.12), channel_id=1, source_target_pairs={{0,96},{1,97},{2,66},{3,67},{4,4},{5,5},{6,38},{7,39},{8,224},{9,2... | collective-permute-start | bytes 221192 | tf_op jit(solution)/shard_map/ppermute | solution.py:189
  97.7 2.3 %collective-permute-done.12.c = s16[144,256]{1,0:T(8,128)(2,1)S(1)} collective-permute-done((s16[144,256]{1,0:T(8,128)(2,1)S(1)}, s16[144,256]{1,0:T(8,128)(2,1)S(1)}, u32[]{:S(2)}, u32[]{:S(2)}) %collective-permute-start.12) | collective-permute-done | bytes 73760 | tf_op jit(solution)/shard_map/ppermute | solution.py:189
  99.9 8.3 %collective-permute-done.13.d = s16[144,256]{1,0:T(8,128)(2,1)S(1)} collective-permute-done((s16[144,256]{1,0:T(8,128)(2,1)S(1)}, s16[144,256]{1,0:T(8,128)(2,1)S(1)}, u32[]{:S(2)}, u32[]{:S(2)}) %collective-permute-start.13) | collective-permute-done | bytes 73760 | tf_op jit(solution)/shard_map/ppermute | solution.py:189
  108.3 0.7 last.1
  (22 shorter events, 0.1 us)
Async XLA Ops:
  0.7 1.0 copy-start
  1.7 0.9 copy-start.1
  2.6 0.7 copy-start.2
  4.3 18.7 %collective-permute-start.5 = (bf16[784,256]{1,0:T(8,128)(2,1)S(1)}, bf16[784,256]{1,0:T(8,128)(2,1)S(1)}, u32[]{:S(2)}, u32[]{:S(2)}) collective-permute-start(bf16[784,256]{1,0:T(8,128)(2,1)S(1)} %contract.1.refs_0_), channel_id=1, source_target_pairs={{0,1},{1,0},{2,3},{3,2},{4,5},{5,4},{6,7},{7,6},{8,9},{9,8},{10,11... | collective-permute-start | bytes 1204232 | tf_op jit(solution)/shard_map/ppermute | solution.py:163
  6.2 22.6 %collective-permute-start.3 = (bf16[784,256]{1,0:T(8,128)(2,1)S(1)}, bf16[784,256]{1,0:T(8,128)(2,1)S(1)}, u32[]{:S(2)}, u32[]{:S(2)}) collective-permute-start(bf16[784,256]{1,0:T(8,128)(2,1)S(1)} %contract.1.refs_0_), channel_id=1, source_target_pairs={{6,0},{4,2},{0,4},{2,6},{7,1},{5,3},{1,5},{3,7},{14,8},{12,10},{8,... | collective-permute-start | bytes 1204232 | tf_op jit(solution)/shard_map/ppermute | solution.py:159
  11.4 19.4 %collective-permute-start.2 = (bf16[784,256]{1,0:T(8,128)(2,1)S(1)}, bf16[784,256]{1,0:T(8,128)(2,1)S(1)}, u32[]{:S(2)}, u32[]{:S(2)}) collective-permute-start(bf16[784,256]{1,0:T(8,128)(2,1)S(1)} %contract.1.refs_0_), channel_id=1, source_target_pairs={{24,0},{0,8},{8,16},{16,24},{25,1},{1,9},{9,17},{17,25},{26,2},{2,... | collective-permute-start | bytes 1204232 | tf_op jit(solution)/shard_map/ppermute | solution.py:161
  14.9 20.9 %collective-permute-start.1 = (bf16[784,256]{1,0:T(8,128)(2,1)S(1)}, bf16[784,256]{1,0:T(8,128)(2,1)S(1)}, u32[]{:S(2)}, u32[]{:S(2)}) collective-permute-start(bf16[784,256]{1,0:T(8,128)(2,1)S(1)} %contract.1.refs_0_), channel_id=1, source_target_pairs={{16,0},{24,8},{0,16},{8,24},{17,1},{25,9},{1,17},{9,25},{18,2},{26... | collective-permute-start | bytes 1204232 | tf_op jit(solution)/shard_map/ppermute | solution.py:161
  19.7 18.0 %collective-permute-start = (bf16[784,256]{1,0:T(8,128)(2,1)S(1)}, bf16[784,256]{1,0:T(8,128)(2,1)S(1)}, u32[]{:S(2)}, u32[]{:S(2)}) collective-permute-start(bf16[784,256]{1,0:T(8,128)(2,1)S(1)} %contract.1.refs_0_), channel_id=1, source_target_pairs={{8,0},{16,8},{24,16},{0,24},{9,1},{17,9},{25,17},{1,25},{10,2},{18... | collective-permute-start | bytes 1204232 | tf_op jit(solution)/shard_map/ppermute | solution.py:161
  23.0 17.2 %collective-permute-start.4 = (bf16[784,256]{1,0:T(8,128)(2,1)S(1)}, bf16[784,256]{1,0:T(8,128)(2,1)S(1)}, u32[]{:S(2)}, u32[]{:S(2)}) collective-permute-start(bf16[784,256]{1,0:T(8,128)(2,1)S(1)} %contract.1.refs_0_), channel_id=1, source_target_pairs={{2,0},{0,2},{6,4},{4,6},{3,1},{1,3},{7,5},{5,7},{10,8},{8,10},{14,... | collective-permute-start | bytes 1204232 | tf_op jit(solution)/shard_map/ppermute | solution.py:160
  28.8 11.4 %collective-permute-start.9 = (bf16[784,256]{1,0:T(8,128)(2,1)S(1)}, bf16[784,256]{1,0:T(8,128)(2,1)S(1)}, u32[]{:S(2)}, u32[]{:S(2)}) collective-permute-start(bf16[784,256]{1,0:T(8,128)(2,1)S(1)} %collective-permute-done.3.refs_4_), channel_id=1, source_target_pairs={{0,1},{1,0},{2,3},{3,2},{4,5},{5,4},{6,7},{7,6},{8,9},{9,8},{10,11... | collective-permute-start | bytes 1204232 | tf_op jit(solution)/shard_map/ppermute | solution.py:163
  30.8 9.5 %collective-permute-start.8 = (bf16[784,256]{1,0:T(8,128)(2,1)S(1)}, bf16[784,256]{1,0:T(8,128)(2,1)}, u32[]{:S(2)}, u32[]{:S(2)}) collective-permute-start(bf16[784,256]{1,0:T(8,128)(2,1)S(1)} %collective-permute-done.2.refs_3_), channel_id=1, source_target_pairs={{0,1},{1,0},{2,3},{3,2},{4,5},{5,4},{6,7},{7,6},{8,9},{9,8},{10,11... | collective-permute-start | bytes 1204232 | tf_op jit(solution)/shard_map/ppermute | solution.py:163
  35.7 5.2 %collective-permute-start.7 = (bf16[784,256]{1,0:T(8,128)(2,1)S(1)}, bf16[784,256]{1,0:T(8,128)(2,1)}, u32[]{:S(2)}, u32[]{:S(2)}) collective-permute-start(bf16[784,256]{1,0:T(8,128)(2,1)S(1)} %collective-permute-done.1.refs_2_), channel_id=1, source_target_pairs={{0,1},{1,0},{2,3},{3,2},{4,5},{5,4},{6,7},{7,6},{8,9},{9,8},{10,11... | collective-permute-start | bytes 1204232 | tf_op jit(solution)/shard_map/ppermute | solution.py:163
  37.7 3.9 %collective-permute-start.6 = (bf16[784,256]{1,0:T(8,128)(2,1)S(1)}, bf16[784,256]{1,0:T(8,128)(2,1)}, u32[]{:S(2)}, u32[]{:S(2)}) collective-permute-start(bf16[784,256]{1,0:T(8,128)(2,1)S(1)} %collective-permute-done.refs_1_), channel_id=1, source_target_pairs={{0,1},{1,0},{2,3},{3,2},{4,5},{5,4},{6,7},{7,6},{8,9},{9,8},{10,11... | collective-permute-start | bytes 1204232 | tf_op jit(solution)/shard_map/ppermute | solution.py:163
  69.4 28.3 %collective-permute-start.10 = (s16[144,256]{1,0:T(8,128)(2,1)S(1)}, s16[144,256]{1,0:T(8,128)(2,1)S(1)}, u32[]{:S(2)}, u32[]{:S(2)}) collective-permute-start(s16[144,256]{1,0:T(8,128)(2,1)S(1)} %get-tuple-element.9), channel_id=1, source_target_pairs={{0,0},{1,1},{2,34},{3,35},{4,68},{5,69},{6,102},{7,103},{8,8},{9,9... | collective-permute-start | bytes 221192 | tf_op jit(solution)/shard_map/ppermute | solution.py:189
  78.5 19.2 %collective-permute-start.11 = (s16[144,256]{1,0:T(8,128)(2,1)S(1)}, s16[144,256]{1,0:T(8,128)(2,1)S(1)}, u32[]{:S(2)}, u32[]{:S(2)}) collective-permute-start(s16[144,256]{1,0:T(8,128)(2,1)S(1)} %get-tuple-element.10), channel_id=1, source_target_pairs={{0,2},{1,3},{2,32},{3,33},{4,70},{5,71},{6,100},{7,101},{8,10},{9,... | collective-permute-start | bytes 221192 | tf_op jit(solution)/shard_map/ppermute | solution.py:189
  90.7 9.3 %collective-permute-start.12 = (s16[144,256]{1,0:T(8,128)(2,1)S(1)}, s16[144,256]{1,0:T(8,128)(2,1)S(1)}, u32[]{:S(2)}, u32[]{:S(2)}) collective-permute-start(s16[144,256]{1,0:T(8,128)(2,1)S(1)} %get-tuple-element.11), channel_id=1, source_target_pairs={{0,6},{1,7},{2,36},{3,37},{4,64},{5,65},{6,98},{7,99},{8,14},{9,15... | collective-permute-start | bytes 221192 | tf_op jit(solution)/shard_map/ppermute | solution.py:189
  92.6 15.7 %collective-permute-start.13 = (s16[144,256]{1,0:T(8,128)(2,1)S(1)}, s16[144,256]{1,0:T(8,128)(2,1)S(1)}, u32[]{:S(2)}, u32[]{:S(2)}) collective-permute-start(s16[144,256]{1,0:T(8,128)(2,1)S(1)} %get-tuple-element.12), channel_id=1, source_target_pairs={{0,96},{1,97},{2,66},{3,67},{4,4},{5,5},{6,38},{7,39},{8,224},{9,2... | collective-permute-start | bytes 221192 | tf_op jit(solution)/shard_map/ppermute | solution.py:189

commit v2 on v0

v2 whole, which is shorter than its diff:
```python
import jax
import jax.numpy as jnp
from jax import lax
from jax.experimental import pallas as pl
from jax.experimental.pallas import tpu as pltpu
from jax.sharding import Mesh, PartitionSpec as P

AXES = ("x", "zh", "y", "zl", "c")
NOB = 16
SLOTS = 6
BS = 64
AUX = 256
RB = 2
HALF = RB * BS
CHIP = 2 * HALF
BODY = RB * SLOTS * BS
PAY = BODY + 16
TILE = HALF + 16
LEVELS = 32000.0
CROSS = (3, 2, 0, 1)
VMEM = pl.BlockSpec(memory_space=pltpu.VMEM)
SMEM = pl.BlockSpec(memory_space=pltpu.SMEM)
ANY = pl.BlockSpec(memory_space=pl.ANY)


def params(mib):
    return pltpu.CompilerParams(vmem_limit_bytes=mib * 1024 * 1024)


def contract_kernel(raw_hbm, metric_hbm, sig_ref, live_ref, out_ref, raw_ref, metric_ref, sems):
    copies = [
        pltpu.make_async_copy(metric_hbm, metric_ref, sems.at[0]),
        pltpu.make_async_copy(raw_hbm, raw_ref, sems.at[1]),
    ]
    for copy in copies:
        copy.start()
    lane = lax.broadcasted_iota(jnp.int32, (16, AUX), 1)
    ids = jnp.zeros((16, AUX), jnp.int32)
    for m in range(RB):
        for s in range(SLOTS):
            ids = jnp.where(lane == m * SLOTS + s, sig_ref[m, s], ids)
    out_ref[BODY:, :] = ids.astype(jnp.float32).astype(jnp.bfloat16)
    for copy in copies:
        copy.wait()
    for m in range(RB):
        for s in range(SLOTS):
            block = m * SLOTS + s
            product = jnp.dot(
                raw_ref[m, s], metric_ref[...], preferred_element_type=jnp.float32
            )
            live = (s < live_ref[m, 0]).astype(jnp.float32)
            out_ref[block * BS : (block + 1) * BS, :] = (product * live).astype(jnp.bfloat16)


def encode(values):
    top = jnp.max(jnp.abs(values), axis=0, keepdims=True)
    exponent = jnp.ceil(jnp.log2(jnp.maximum(top, 1e-30)) + 1e-3)
    coded = jnp.round(values * (LEVELS * jnp.exp2(-exponent)))
    return coded.astype(jnp.int32).astype(jnp.int16), exponent.astype(jnp.int32)


def decode(coded, exponents, row):
    scale = jnp.exp2(exponents[row : row + 1, :].astype(jnp.float32)) * (1.0 / LEVELS)
    return coded.astype(jnp.int32).astype(jnp.float32) * scale


def pick_rows(rows, width):
    at = lax.broadcasted_iota(jnp.int32, (16, width), 0)
    block = jnp.zeros((16, width), jnp.int32)
    for i, row in enumerate(rows):
        block = jnp.where(at == i, jnp.broadcast_to(row, (16, width)), block)
    return block


def load_ids(sources, ids_vmem, ids_smem, sem):
    for i, src in enumerate(sources):
        ids = src[BODY:PAY, 0:128].astype(jnp.float32).astype(jnp.int32)
        ids_vmem[i] = ids[0:8, :]
    return pltpu.make_async_copy(ids_vmem, ids_smem, sem)


def scatter(src, ids, row, target, first):
    for m in range(RB):
        for s in range(SLOTS):
            block = m * SLOTS + s
            orbital = ids[row, 0, block]
            lanes = pl.ds(pl.multiple_of(orbital * AUX, AUX), AUX)
            rows = pl.ds(pl.multiple_of(first + m * BS, BS), BS)
            target[rows, lanes] = src[block * BS : (block + 1) * BS, :]


NT = (((1,), (1,)), ((), ()))


def early_kernel(place_ref, *refs):
    column, mine, other = refs[:4], refs[4:6], refs[6:9]
    out_ref, exp_ref, rows, cols, ids_vmem, ids, sem = refs[9:]
    core = place_ref[1]
    copy = load_ids([*column, *mine, *other], ids_vmem, ids, sem)
    copy.start()
    rows[...] = jnp.zeros_like(rows)
    cols[...] = jnp.zeros_like(cols)
    copy.wait()
    for d in range(4):
        scatter(column[d], ids, d, rows, d * HALF)
    for t in range(3):
        at = t * CHIP
        src, row = (column[0], 0) if t == 0 else (mine[t - 1], 3 + t)
        scatter(src, ids, row, cols, at + core * HALF)
        scatter(other[t], ids, 6 + t, cols, at + (1 - core) * HALF)
    for t in range(3):
        part = lax.dot_general(
            rows[...], cols[t * CHIP : (t + 1) * CHIP, :], NT, preferred_element_type=jnp.float32
        )
        for d in range(4):
            coded, exponent = encode(part[d * HALF : (d + 1) * HALF, :])
            out_ref[d, t * HALF : (t + 1) * HALF, :] = coded
            exp_ref[d, t * 8 : (t + 1) * 8, :] = jnp.broadcast_to(exponent, (8, CHIP))


def late_kernel(place_ref, *refs):
    column, far, far_other, early, early_exp = refs[:4], *refs[4:8]
    outs, (rows, cols, ids_vmem, ids, sem) = refs[8:12], refs[12:]
    y, core, x = place_ref[0], place_ref[1], place_ref[2]
    copy = load_ids([*column, far, far_other], ids_vmem, ids, sem)
    copy.start()
    rows[...] = jnp.zeros_like(rows)
    cols[...] = jnp.zeros_like(cols)
    copy.wait()
    for i in range(4):
        scatter(column[i], ids, i, rows, i * HALF)
    scatter(far, ids, 4, cols, core * HALF)
    scatter(far_other, ids, 5, cols, (1 - core) * HALF)
    for r in range(4):
        d = lax.rem(r + 8 - x - y, 4)
        part = lax.dot_general(
            rows[pl.ds(pl.multiple_of(d * HALF, HALF), HALF), :], cols[...], NT,
            preferred_element_type=jnp.float32,
        )
        coded, exponent = encode(part)
        outs[r][: 3 * HALF, :] = early[d]
        outs[r][3 * HALF : 4 * HALF, :] = coded
        before = early_exp[d]
        block = pick_rows([before[0:1], before[8:9], before[16:17], exponent], CHIP)
        outs[r][4 * HALF :, :] = block.astype(jnp.int16)


def middle_kernel(place_ref, *refs):
    sources, out_ref = refs[:4], refs[4]
    exponents = [src[4 * HALF :, :].astype(jnp.int32) for src in sources]
    for t in range(4):
        total = None
        for src, exps in zip(sources, exponents):
            value = decode(src[t * HALF : (t + 1) * HALF, :], exps, t)
            total = value if total is None else total + value
        coded, exponent = encode(total)
        at = place_ref[3 + t]
        out_ref[at, :HALF, :] = coded
        out_ref[at, HALF:, :] = jnp.broadcast_to(exponent, (16, CHIP)).astype(jnp.int16)


def last_kernel(in_ref, out_ref):
    total = None
    for s in range(4):
        value = decode(in_ref[s, :HALF, :], in_ref[s, HALF:, :].astype(jnp.int32), 0)
        total = value if total is None else total + value
    out_ref[...] = 0.25 * total


def index_of(x, y, c):
    return (x * 4 + y) * 2 + c


def plane_round(r):
    pairs = []
    for x in range(4):
        for y in range(4):
            for c in range(2):
                pairs.append((index_of(x, y, c), index_of(y, (r - x) % 4, c)))
    return pairs


def shards(raw_blocks, metric_factor, sig_list, live_count):
    z = lax.axis_index("zl")
    order = jnp.array([[t, t ^ 1, CROSS[t], CROSS[t ^ 1]] for t in range(4)], jnp.int32)[z]
    first = [lax.axis_index("y"), lax.axis_index("c"), lax.axis_index("x")]
    place = jnp.concatenate([jnp.stack(first).astype(jnp.int32), order])
    own = pl.pallas_call(
        contract_kernel,
        out_shape=jax.ShapeDtypeStruct((PAY, AUX), jnp.bfloat16),
        in_specs=[ANY, ANY, SMEM, SMEM],
        out_specs=VMEM,
        scratch_shapes=[
            pltpu.VMEM(raw_blocks.shape, jnp.bfloat16),
            pltpu.VMEM((AUX, AUX), jnp.bfloat16),
            pltpu.SemaphoreType.DMA((2,)),
        ],
        compiler_params=params(56),
        name="contract",
    )(raw_blocks, metric_factor, sig_list, live_count)

    def swap(a):
        return lax.ppermute(a, "c", [(0, 1), (1, 0)])

    flip = [(i ^ 1, i) for i in range(4)]
    across = lax.ppermute(own, "zl", [(CROSS[i], i) for i in range(4)])
    near = lax.ppermute(own, "zl", flip)
    column = [own] + [lax.ppermute(own, "y", [((i + d) % 4, i) for i in range(4)]) for d in (1, 2, 3)]
    far = lax.ppermute(across, "zl", flip)

    def dense(rows):
        return pltpu.VMEM((rows, NOB * AUX), jnp.bfloat16)

    def ids_scratch(count):
        return [
            pltpu.VMEM((count, 8, 128), jnp.int32),
            pltpu.SMEM((count, 8, 128), jnp.int32),
            pltpu.SemaphoreType.DMA,
        ]

    early = pl.pallas_call(
        early_kernel,
        out_shape=[
            jax.ShapeDtypeStruct((4, 3 * HALF, CHIP), jnp.int16),
            jax.ShapeDtypeStruct((4, 24, CHIP), jnp.int32),
        ],
        in_specs=[SMEM] + [VMEM] * 9,
        out_specs=[VMEM] * 2,
        scratch_shapes=[dense(4 * HALF), dense(3 * CHIP)] + ids_scratch(9),
        compiler_params=params(40),
        cost_estimate=pl.CostEstimate(flops=2 * 512 * 768 * 4096, bytes_accessed=4_000_000, transcendentals=0),
        name="early",
    )(place, *column, near, across, swap(own), swap(near), swap(across))
    message = jax.ShapeDtypeStruct((4 * HALF + 16, CHIP), jnp.int16)
    messages = pl.pallas_call(
        late_kernel,
        out_shape=[message] * 4,
        in_specs=[SMEM] + [VMEM] * 8,
        out_specs=[VMEM] * 4,
        scratch_shapes=[dense(4 * HALF), dense(CHIP)] + ids_scratch(6),
        compiler_params=params(40),
        cost_estimate=pl.CostEstimate(flops=2 * 512 * 256 * 4096, bytes_accessed=4_000_000, transcendentals=0),
        name="late",
    )(place, *column, far, swap(far), *early)
    summed = pl.pallas_call(
        middle_kernel,
        out_shape=jax.ShapeDtypeStruct((4, TILE, CHIP), jnp.int16),
        in_specs=[SMEM] + [VMEM] * 4,
        out_specs=VMEM,
        compiler_params=params(16),
        name="middle",
    )(place, *[lax.ppermute(a, ("x", "y", "c"), plane_round(r)) for r, a in enumerate(messages)])
    arrived = lax.all_to_all(summed, "zh", 0, 0, tiled=True)
    return pl.pallas_call(
        last_kernel,
        out_shape=jax.ShapeDtypeStruct((HALF, CHIP), jnp.float32),
        in_specs=[VMEM],
        out_specs=VMEM,
        compiler_params=params(16),
        name="last",
    )(arrived)


def solution(mesh):
    fine = Mesh(mesh.devices.reshape(4, 4, 4, 4, 2), AXES)
    blk, grp = ("y", "zl", "c"), ("x", "zh")
    placed = (P(blk, grp, None, None), P(), P(blk, grp), P(blk, grp))
    return jax.shard_map(shards, mesh=fine, in_specs=placed, out_specs=P(blk, grp), check_vma=False)
```

time: 297 us -> 149 us (0.50)
  the two profiles are of different devices: /device:TPU:1 before, /device:TPU:32 now
where the time goes in v2:
time: 149 us
  waiting for transfers between devices  51.5 us (35%)
  starting transfers between devices  42.4 us (28%)
  blocking collectives  35.3 us (24%)
  Pallas kernels  16.2 us (11%)
  local copies, waits for them, and re-layouts  2.98 us (2%)
    ppermute x4, waiting for transfers between devices, shards(): lax.ppermute(a, ('x', 'y', 'c'), plane_round(r))  41.8 us
    all_to_all x1, blocking collectives, shards(): arrived = lax.all_to_all(summed, 'zh', 0, 0, tiled=True)  35.3 us
    ppermute x4, starting transfers between devices, shards(): lax.ppermute(a, ('x', 'y', 'c'), plane_round(r))  14.2 us
    ppermute x3, starting transfers between devices, shards(): lax.ppermute(own, 'y', [((i + d) % 4, i) for i in range(4)])  8.83 us
    ppermute x4, starting transfers between devices, swap(): return lax.ppermute(a, 'c', [(0, 1), (1, 0)])  8.16 us
    ppermute x1, waiting for transfers between devices, shards(): across = lax.ppermute(own, 'zl', [(CROSS[i], i) for i in range(4)])  7.53 us
    pallas_call x1, Pallas kernels, shards(): pl.pallas_call(early_kernel, out_shape=[jax.ShapeDtypeStruct((4, 3 * HALF...  6.74 us
    ppermute x1, starting transfers between devices, shards(): across = lax.ppermute(own, 'zl', [(CROSS[i], i) for i in range(4)])  5.18 us
  transfers between devices with their start and end apart: 14, of which 6 were waited for; matrix products, arithmetic and copies ran while one was open for 1% of the time, Pallas kernels for 5%

profile of v2, /device:TPU:32, one launch (start us, length us, event | category | flops | bytes accessed | tf_op | source)
XLA Modules:
  0.0 148.8 jit_solution(9979171821481322582)
XLA Ops:
  0.0 1.3 copy.6.live_ref
  1.3 2.9 %contract.1.refs_0_ = bf16[784,256]{1,0:T(8,128)(2,1)} custom-call(bf16[2,6,64,256]{3,2,1,0:T(8,128)(2,1)} %raw_hbm.1, bf16[256,256]{1,0:T(8,128)(2,1)} %metric_hbm.1, s32[2,6]{1,0:T(2,128)} %sig_ref.1, s32[2,1]{1,0:T(2,128)} %copy.6.live_ref), custom_call_target="tpu_custom_call" | custom-call | tf_op jit(solution)/shard_map/contract/pallas_call | solution.py:188
  4.2 5.2 %collective-permute-start.3 = (bf16[784,256]{1,0:T(8,128)(2,1)}, bf16[784,256]{1,0:T(8,128)(2,1)S(1)}, u32[]{:S(2)}, u32[]{:S(2)}) collective-permute-start(bf16[784,256]{1,0:T(8,128)(2,1)} %contract.1.refs_0_), channel_id=1, source_target_pairs={{6,0},{4,2},{0,4},{2,6},{7,1},{5,3},{1,5},{3,7},{14,8},{12,10},{8,... | collective-permute-start | bytes 1204232 | tf_op jit(solution)/shard_map/ppermute | solution.py:206
  9.4 4.1 %collective-permute-start.6 = (bf16[784,256]{1,0:T(8,128)(2,1)}, bf16[784,256]{1,0:T(8,128)(2,1)S(1)}, u32[]{:S(2)}, u32[]{:S(2)}) collective-permute-start(bf16[784,256]{1,0:T(8,128)(2,1)} %contract.1.refs_0_), channel_id=1, source_target_pairs={{2,0},{0,2},{6,4},{4,6},{3,1},{1,3},{7,5},{5,7},{10,8},{8,10},{14,... | collective-permute-start | bytes 1204232 | tf_op jit(solution)/shard_map/ppermute | solution.py:207
  13.6 2.8 %collective-permute-start = (bf16[784,256]{1,0:T(8,128)(2,1)}, bf16[784,256]{1,0:T(8,128)(2,1)S(1)}, u32[]{:S(2)}, u32[]{:S(2)}) collective-permute-start(bf16[784,256]{1,0:T(8,128)(2,1)} %contract.1.refs_0_), channel_id=1, source_target_pairs={{8,0},{16,8},{24,16},{0,24},{9,1},{17,9},{25,17},{1,25},{10,2},{18... | collective-permute-start | bytes 1204232 | tf_op jit(solution)/shard_map/ppermute | solution.py:208
  16.4 2.5 %collective-permute-start.1 = (bf16[784,256]{1,0:T(8,128)(2,1)}, bf16[784,256]{1,0:T(8,128)(2,1)S(1)}, u32[]{:S(2)}, u32[]{:S(2)}) collective-permute-start(bf16[784,256]{1,0:T(8,128)(2,1)} %contract.1.refs_0_), channel_id=1, source_target_pairs={{16,0},{24,8},{0,16},{8,24},{17,1},{25,9},{1,17},{9,25},{18,2},{26... | collective-permute-start | bytes 1204232 | tf_op jit(solution)/shard_map/ppermute | solution.py:208
  18.9 7.5 %collective-permute-done.3.refs_5_ = bf16[784,256]{1,0:T(8,128)(2,1)S(1)} collective-permute-done((bf16[784,256]{1,0:T(8,128)(2,1)}, bf16[784,256]{1,0:T(8,128)(2,1)S(1)}, u32[]{:S(2)}, u32[]{:S(2)}) %collective-permute-start.3) | collective-permute-done | bytes 401440 | tf_op jit(solution)/shard_map/ppermute | solution.py:206
  26.5 1.9 %collective-permute-start.4 = (bf16[784,256]{1,0:T(8,128)(2,1)S(1)}, bf16[784,256]{1,0:T(8,128)(2,1)S(1)}, u32[]{:S(2)}, u32[]{:S(2)}) collective-permute-start(bf16[784,256]{1,0:T(8,128)(2,1)S(1)} %collective-permute-done.3.refs_5_), channel_id=1, source_target_pairs={{2,0},{0,2},{6,4},{4,6},{3,1},{1,3},{7,5},{5,7},{10,8},{8,10},{14,... | collective-permute-start | bytes 1204232 | tf_op jit(solution)/shard_map/ppermute | solution.py:209
  28.4 3.5 %collective-permute-start.2 = (bf16[784,256]{1,0:T(8,128)(2,1)}, bf16[784,256]{1,0:T(8,128)(2,1)S(1)}, u32[]{:S(2)}, u32[]{:S(2)}) collective-permute-start(bf16[784,256]{1,0:T(8,128)(2,1)} %contract.1.refs_0_), channel_id=1, source_target_pairs={{24,0},{0,8},{8,16},{16,24},{25,1},{1,9},{9,17},{17,25},{26,2},{2,... | collective-permute-start | bytes 1204232 | tf_op jit(solution)/shard_map/ppermute | solution.py:208
  31.9 1.9 %collective-permute-start.7 = (bf16[784,256]{1,0:T(8,128)(2,1)}, bf16[784,256]{1,0:T(8,128)(2,1)S(1)}, u32[]{:S(2)}, u32[]{:S(2)}) collective-permute-start(bf16[784,256]{1,0:T(8,128)(2,1)} %contract.1.refs_0_), channel_id=1, source_target_pairs={{0,1},{1,0},{2,3},{3,2},{4,5},{5,4},{6,7},{7,6},{8,9},{9,8},{10,11... | collective-permute-start | bytes 1204232 | tf_op jit(solution)/shard_map/ppermute | solution.py:203
  33.8 2.4 %collective-permute-start.9 = (bf16[784,256]{1,0:T(8,128)(2,1)S(1)}, bf16[784,256]{1,0:T(8,128)(2,1)S(1)}, u32[]{:S(2)}, u32[]{:S(2)}) collective-permute-start(bf16[784,256]{1,0:T(8,128)(2,1)S(1)} %collective-permute-done.3.refs_5_), channel_id=1, source_target_pairs={{0,1},{1,0},{2,3},{3,2},{4,5},{5,4},{6,7},{7,6},{8,9},{9,8},{10,11... | collective-permute-start | bytes 1204232 | tf_op jit(solution)/shard_map/ppermute | solution.py:203
  36.2 1.9 %collective-permute-start.8 = (bf16[784,256]{1,0:T(8,128)(2,1)S(1)}, bf16[784,256]{1,0:T(8,128)(2,1)}, u32[]{:S(2)}, u32[]{:S(2)}) collective-permute-start(bf16[784,256]{1,0:T(8,128)(2,1)S(1)} %collective-permute-done.6.refs_4_), channel_id=1, source_target_pairs={{0,1},{1,0},{2,3},{3,2},{4,5},{5,4},{6,7},{7,6},{8,9},{9,8},{10,11... | collective-permute-start | bytes 1204232 | tf_op jit(solution)/shard_map/ppermute | solution.py:203
  38.2 0.7 dynamic-slice_bitcast_fusion
  38.9 0.7 collective-permute-done.4.refs_4_
  39.6 1.9 %collective-permute-start.5 = (bf16[784,256]{1,0:T(8,128)(2,1)S(1)}, bf16[784,256]{1,0:T(8,128)(2,1)S(1)}, u32[]{:S(2)}, u32[]{:S(2)}) collective-permute-start(bf16[784,256]{1,0:T(8,128)(2,1)S(1)} %collective-permute-done.4.refs_4_), channel_id=1, source_target_pairs={{0,1},{1,0},{2,3},{3,2},{4,5},{5,4},{6,7},{7,6},{8,9},{9,8},{10,11... | collective-permute-start | bytes 1204232 | tf_op jit(solution)/shard_map/ppermute | solution.py:203
  41.5 0.1 pad_add_fusion.place_ref
  41.5 1.4 collective-permute-done.2.refs_3_
  43.0 1.0 copy-done
  44.0 6.7 %early.1 = (s16[4,384,256]{2,1,0:T(8,128)(2,1)S(1)}, s32[4,24,256]{2,1,0:T(8,128)S(1)}) custom-call(s32[7]{0:T(128)S(1)} %pad_add_fusion.place_ref, bf16[784,256]{1,0:T(8,128)(2,1)S(1)} %copy-done, bf16[784,256]{1,0:T(8,128)(2,1)S(1)} %collective-permute-done.refs_1_, bf16[784,256]{1,0:T(8,128)(2,1)S(1)} %collective-permute-done.1.refs_2_, ...), custom_call_target="tpu_custom_call" | custom-call | flops 3221225472 | bytes 4000000 | tf_op jit(solution)/shard_map/early/pallas_call | solution.py:221
  50.7 0.0 collective-permute-done.5.refs_5_
  50.8 4.9 %late.1 = (s16[528,256]{1,0:T(8,128)(2,1)S(1)}, s16[528,256]{1,0:T(8,128)(2,1)S(1)}, s16[528,256]{1,0:T(8,128)(2,1)S(1)}, s16[528,256]{1,0:T(8,128)(2,1)S(1)}) custom-call(s32[7]{0:T(128)S(1)} %pad_add_fusion.place_ref, bf16[784,256]{1,0:T(8,128)(2,1)S(1)} %copy-done.1, bf16[784,256]{1,0:T(8,128)(2,1)S(1)} %collective-permute-done.refs_1_, ...), custom_call_target="tpu_custom_call" | custom-call | flops 1073741824 | bytes 4000000 | tf_op jit(solution)/shard_map/late/pallas_call | solution.py:235
  55.7 0.7 collective-permute-start.10
  56.4 6.1 %collective-permute-start.11 = (s16[528,256]{1,0:T(8,128)(2,1)S(1)}, s16[528,256]{1,0:T(8,128)(2,1)S(1)}, u32[]{:S(2)}, u32[]{:S(2)}) collective-permute-start(s16[528,256]{1,0:T(8,128)(2,1)S(1)} %get-tuple-element.14), channel_id=1, source_target_pairs={{0,8},{1,9},{8,136},{9,137},{16,264},{17,265},{24,392},{25,393},{1... | collective-permute-start | bytes 811016 | tf_op jit(solution)/shard_map/ppermute | solution.py:252
  62.4 5.4 %collective-permute-start.12 = (s16[528,256]{1,0:T(8,128)(2,1)S(1)}, s16[528,256]{1,0:T(8,128)(2,1)S(1)}, u32[]{:S(2)}, u32[]{:S(2)}) collective-permute-start(s16[528,256]{1,0:T(8,128)(2,1)S(1)} %get-tuple-element.15), channel_id=1, source_target_pairs={{0,16},{1,17},{8,144},{9,145},{16,272},{17,273},{24,400},{25,401},... | collective-permute-start | bytes 811016 | tf_op jit(solution)/shard_map/ppermute | solution.py:252
  67.8 2.1 %collective-permute-start.13 = (s16[528,256]{1,0:T(8,128)(2,1)S(1)}, s16[528,256]{1,0:T(8,128)(2,1)S(1)}, u32[]{:S(2)}, u32[]{:S(2)}) collective-permute-start(s16[528,256]{1,0:T(8,128)(2,1)S(1)} %get-tuple-element.16), channel_id=1, source_target_pairs={{0,24},{1,25},{8,152},{9,153},{16,280},{17,281},{24,408},{25,409},... | collective-permute-start | bytes 811016 | tf_op jit(solution)/shard_map/ppermute | solution.py:252
  69.9 0.0 collective-permute-done.10.refs_0_
  69.9 31.2 %collective-permute-done.11.refs_1_ = s16[528,256]{1,0:T(8,128)(2,1)S(1)} collective-permute-done((s16[528,256]{1,0:T(8,128)(2,1)S(1)}, s16[528,256]{1,0:T(8,128)(2,1)S(1)}, u32[]{:S(2)}, u32[]{:S(2)}) %collective-permute-start.11) | collective-permute-done | bytes 270368 | tf_op jit(solution)/shard_map/ppermute | solution.py:252
  101.1 5.7 %collective-permute-done.12.refs_2_ = s16[528,256]{1,0:T(8,128)(2,1)S(1)} collective-permute-done((s16[528,256]{1,0:T(8,128)(2,1)S(1)}, s16[528,256]{1,0:T(8,128)(2,1)S(1)}, u32[]{:S(2)}, u32[]{:S(2)}) %collective-permute-start.12) | collective-permute-done | bytes 270368 | tf_op jit(solution)/shard_map/ppermute | solution.py:252
  106.8 5.0 %collective-permute-done.13.refs_3_ = s16[528,256]{1,0:T(8,128)(2,1)S(1)} collective-permute-done((s16[528,256]{1,0:T(8,128)(2,1)S(1)}, s16[528,256]{1,0:T(8,128)(2,1)S(1)}, u32[]{:S(2)}, u32[]{:S(2)}) %collective-permute-start.13) | collective-permute-done | bytes 270368 | tf_op jit(solution)/shard_map/ppermute | solution.py:252
  111.8 0.9 middle.1
  112.7 35.3 %all_to_all.5.in_ref = s16[4,144,256]{2,1,0:T(8,128)(2,1)S(1)} all-to-all(s16[4,144,256]{2,1,0:T(8,128)(2,1)S(1)} %middle.1), channel_id=1, replica_groups=mesh['x'=4,'zh'=4,'y'=4,'zl'=4,'c'=2] {'zh'}, dimensions={0} | all-to-all | bytes 589824 | tf_op jit(solution)/shard_map/all_to_all | solution.py:253
  148.0 0.7 last.1
  (9 shorter events, 0.0 us)
Async XLA Ops:
  4.2 22.2 %collective-permute-start.3 = (bf16[784,256]{1,0:T(8,128)(2,1)}, bf16[784,256]{1,0:T(8,128)(2,1)S(1)}, u32[]{:S(2)}, u32[]{:S(2)}) collective-permute-start(bf16[784,256]{1,0:T(8,128)(2,1)} %contract.1.refs_0_), channel_id=1, source_target_pairs={{6,0},{4,2},{0,4},{2,6},{7,1},{5,3},{1,5},{3,7},{14,8},{12,10},{8,... | collective-permute-start | bytes 1204232 | tf_op jit(solution)/shard_map/ppermute | solution.py:206
  9.4 22.4 %collective-permute-start.6 = (bf16[784,256]{1,0:T(8,128)(2,1)}, bf16[784,256]{1,0:T(8,128)(2,1)S(1)}, u32[]{:S(2)}, u32[]{:S(2)}) collective-permute-start(bf16[784,256]{1,0:T(8,128)(2,1)} %contract.1.refs_0_), channel_id=1, source_target_pairs={{2,0},{0,2},{6,4},{4,6},{3,1},{1,3},{7,5},{5,7},{10,8},{8,10},{14,... | collective-permute-start | bytes 1204232 | tf_op jit(solution)/shard_map/ppermute | solution.py:207
  13.6 20.2 %collective-permute-start = (bf16[784,256]{1,0:T(8,128)(2,1)}, bf16[784,256]{1,0:T(8,128)(2,1)S(1)}, u32[]{:S(2)}, u32[]{:S(2)}) collective-permute-start(bf16[784,256]{1,0:T(8,128)(2,1)} %contract.1.refs_0_), channel_id=1, source_target_pairs={{8,0},{16,8},{24,16},{0,24},{9,1},{17,9},{25,17},{1,25},{10,2},{18... | collective-permute-start | bytes 1204232 | tf_op jit(solution)/shard_map/ppermute | solution.py:208
  16.4 19.9 %collective-permute-start.1 = (bf16[784,256]{1,0:T(8,128)(2,1)}, bf16[784,256]{1,0:T(8,128)(2,1)S(1)}, u32[]{:S(2)}, u32[]{:S(2)}) collective-permute-start(bf16[784,256]{1,0:T(8,128)(2,1)} %contract.1.refs_0_), channel_id=1, source_target_pairs={{16,0},{24,8},{0,16},{8,24},{17,1},{25,9},{1,17},{9,25},{18,2},{26... | collective-permute-start | bytes 1204232 | tf_op jit(solution)/shard_map/ppermute | solution.py:208
  26.5 13.1 %collective-permute-start.4 = (bf16[784,256]{1,0:T(8,128)(2,1)S(1)}, bf16[784,256]{1,0:T(8,128)(2,1)S(1)}, u32[]{:S(2)}, u32[]{:S(2)}) collective-permute-start(bf16[784,256]{1,0:T(8,128)(2,1)S(1)} %collective-permute-done.3.refs_5_), channel_id=1, source_target_pairs={{2,0},{0,2},{6,4},{4,6},{3,1},{1,3},{7,5},{5,7},{10,8},{8,10},{14,... | collective-permute-start | bytes 1204232 | tf_op jit(solution)/shard_map/ppermute | solution.py:209
  28.4 14.6 %collective-permute-start.2 = (bf16[784,256]{1,0:T(8,128)(2,1)}, bf16[784,256]{1,0:T(8,128)(2,1)S(1)}, u32[]{:S(2)}, u32[]{:S(2)}) collective-permute-start(bf16[784,256]{1,0:T(8,128)(2,1)} %contract.1.refs_0_), channel_id=1, source_target_pairs={{24,0},{0,8},{8,16},{16,24},{25,1},{1,9},{9,17},{17,25},{26,2},{2,... | collective-permute-start | bytes 1204232 | tf_op jit(solution)/shard_map/ppermute | solution.py:208
  31.9 11.1 %collective-permute-start.7 = (bf16[784,256]{1,0:T(8,128)(2,1)}, bf16[784,256]{1,0:T(8,128)(2,1)S(1)}, u32[]{:S(2)}, u32[]{:S(2)}) collective-permute-start(bf16[784,256]{1,0:T(8,128)(2,1)} %contract.1.refs_0_), channel_id=1, source_target_pairs={{0,1},{1,0},{2,3},{3,2},{4,5},{5,4},{6,7},{7,6},{8,9},{9,8},{10,11... | collective-permute-start | bytes 1204232 | tf_op jit(solution)/shard_map/ppermute | solution.py:203
  33.8 9.2 %collective-permute-start.9 = (bf16[784,256]{1,0:T(8,128)(2,1)S(1)}, bf16[784,256]{1,0:T(8,128)(2,1)S(1)}, u32[]{:S(2)}, u32[]{:S(2)}) collective-permute-start(bf16[784,256]{1,0:T(8,128)(2,1)S(1)} %collective-permute-done.3.refs_5_), channel_id=1, source_target_pairs={{0,1},{1,0},{2,3},{3,2},{4,5},{5,4},{6,7},{7,6},{8,9},{9,8},{10,11... | collective-permute-start | bytes 1204232 | tf_op jit(solution)/shard_map/ppermute | solution.py:203
  36.2 6.7 %collective-permute-start.8 = (bf16[784,256]{1,0:T(8,128)(2,1)S(1)}, bf16[784,256]{1,0:T(8,128)(2,1)}, u32[]{:S(2)}, u32[]{:S(2)}) collective-permute-start(bf16[784,256]{1,0:T(8,128)(2,1)S(1)} %collective-permute-done.6.refs_4_), channel_id=1, source_target_pairs={{0,1},{1,0},{2,3},{3,2},{4,5},{5,4},{6,7},{7,6},{8,9},{9,8},{10,11... | collective-permute-start | bytes 1204232 | tf_op jit(solution)/shard_map/ppermute | solution.py:203
  39.6 11.2 %collective-permute-start.5 = (bf16[784,256]{1,0:T(8,128)(2,1)S(1)}, bf16[784,256]{1,0:T(8,128)(2,1)S(1)}, u32[]{:S(2)}, u32[]{:S(2)}) collective-permute-start(bf16[784,256]{1,0:T(8,128)(2,1)S(1)} %collective-permute-done.4.refs_4_), channel_id=1, source_target_pairs={{0,1},{1,0},{2,3},{3,2},{4,5},{5,4},{6,7},{7,6},{8,9},{9,8},{10,11... | collective-permute-start | bytes 1204232 | tf_op jit(solution)/shard_map/ppermute | solution.py:203
  43.0 1.0 copy-start
  44.0 6.8 %copy-start.1 = (bf16[784,256]{1,0:T(8,128)(2,1)S(1)}, bf16[784,256]{1,0:T(8,128)(2,1)}, u32[]{:S(2)}) copy-start(bf16[784,256]{1,0:T(8,128)(2,1)} %contract.1.refs_0_) | copy-start | bytes 1204228
  55.7 14.3 %collective-permute-start.10 = (s16[528,256]{1,0:T(8,128)(2,1)S(1)}, s16[528,256]{1,0:T(8,128)(2,1)S(1)}, u32[]{:S(2)}, u32[]{:S(2)}) collective-permute-start(s16[528,256]{1,0:T(8,128)(2,1)S(1)} %get-tuple-element.13), channel_id=1, source_target_pairs={{0,0},{1,1},{8,128},{9,129},{16,256},{17,257},{24,384},{25,385},{1... | collective-permute-start | bytes 811016 | tf_op jit(solution)/shard_map/ppermute | solution.py:252
  56.4 44.7 %collective-permute-start.11 = (s16[528,256]{1,0:T(8,128)(2,1)S(1)}, s16[528,256]{1,0:T(8,128)(2,1)S(1)}, u32[]{:S(2)}, u32[]{:S(2)}) collective-permute-start(s16[528,256]{1,0:T(8,128)(2,1)S(1)} %get-tuple-element.14), channel_id=1, source_target_pairs={{0,8},{1,9},{8,136},{9,137},{16,264},{17,265},{24,392},{25,393},{1... | collective-permute-start | bytes 811016 | tf_op jit(solution)/shard_map/ppermute | solution.py:252
  62.4 44.4 %collective-permute-start.12 = (s16[528,256]{1,0:T(8,128)(2,1)S(1)}, s16[528,256]{1,0:T(8,128)(2,1)S(1)}, u32[]{:S(2)}, u32[]{:S(2)}) collective-permute-start(s16[528,256]{1,0:T(8,128)(2,1)S(1)} %get-tuple-element.15), channel_id=1, source_target_pairs={{0,16},{1,17},{8,144},{9,145},{16,272},{17,273},{24,400},{25,401},... | collective-permute-start | bytes 811016 | tf_op jit(solution)/shard_map/ppermute | solution.py:252
  67.8 44.0 %collective-permute-start.13 = (s16[528,256]{1,0:T(8,128)(2,1)S(1)}, s16[528,256]{1,0:T(8,128)(2,1)S(1)}, u32[]{:S(2)}, u32[]{:S(2)}) collective-permute-start(s16[528,256]{1,0:T(8,128)(2,1)S(1)} %get-tuple-element.16), channel_id=1, source_target_pairs={{0,24},{1,25},{8,152},{9,153},{16,280},{17,281},{24,408},{25,409},... | collective-permute-start | bytes 811016 | tf_op jit(solution)/shard_map/ppermute | solution.py:252

commit v3 on v2

v3 whole, which is shorter than its diff:
```python
import jax
import jax.numpy as jnp
from jax import lax
from jax.experimental import pallas as pl
from jax.experimental.pallas import tpu as pltpu
from jax.sharding import Mesh, PartitionSpec as P

AXES = ("x", "zh", "y", "zl", "c")
NOB = 16
SLOTS = 6
BS = 64
AUX = 256
RB = 2
HALF = RB * BS
CHIP = 2 * HALF
BODY = RB * SLOTS * BS
PAY = BODY + 16
TILE = HALF + 16
LEVELS = 32000.0
CROSS = (3, 2, 0, 1)
VMEM = pl.BlockSpec(memory_space=pltpu.VMEM)
SMEM = pl.BlockSpec(memory_space=pltpu.SMEM)
ANY = pl.BlockSpec(memory_space=pl.ANY)


def params(mib):
    return pltpu.CompilerParams(vmem_limit_bytes=mib * 1024 * 1024)


def contract_kernel(raw_hbm, metric_hbm, sig_ref, live_ref, out_ref, raw_ref, metric_ref, sems):
    copies = [
        pltpu.make_async_copy(metric_hbm, metric_ref, sems.at[0]),
        pltpu.make_async_copy(raw_hbm, raw_ref, sems.at[1]),
    ]
    for copy in copies:
        copy.start()
    lane = lax.broadcasted_iota(jnp.int32, (16, AUX), 1)
    ids = jnp.zeros((16, AUX), jnp.int32)
    for m in range(RB):
        for s in range(SLOTS):
            ids = jnp.where(lane == m * SLOTS + s, sig_ref[m, s], ids)
    out_ref[BODY:, :] = ids.astype(jnp.float32).astype(jnp.bfloat16)
    for copy in copies:
        copy.wait()
    for m in range(RB):
        for s in range(SLOTS):
            block = m * SLOTS + s
            product = jnp.dot(
                raw_ref[m, s], metric_ref[...], preferred_element_type=jnp.float32
            )
            live = (s < live_ref[m]).astype(jnp.float32)
            out_ref[block * BS : (block + 1) * BS, :] = (product * live).astype(jnp.bfloat16)


def encode(values):
    top = jnp.max(jnp.abs(values), axis=0, keepdims=True)
    exponent = jnp.ceil(jnp.log2(jnp.maximum(top, 1e-30)) + 1e-3)
    coded = jnp.round(values * (LEVELS * jnp.exp2(-exponent)))
    return coded.astype(jnp.int32).astype(jnp.int16), exponent.astype(jnp.int32)


def decode(coded, exponents, row):
    scale = jnp.exp2(exponents[row : row + 1, :].astype(jnp.float32)) * (1.0 / LEVELS)
    return coded.astype(jnp.int32).astype(jnp.float32) * scale


def pick_rows(rows, width):
    at = lax.broadcasted_iota(jnp.int32, (16, width), 0)
    block = jnp.zeros((16, width), jnp.int32)
    for i, row in enumerate(rows):
        block = jnp.where(at == i, jnp.broadcast_to(row, (16, width)), block)
    return block


def load_ids(sources, ids_vmem, ids_smem, sem):
    for i, src in enumerate(sources):
        ids = src[BODY:PAY, 0:128].astype(jnp.float32).astype(jnp.int32)
        ids_vmem[i] = ids[0:8, :]
    return pltpu.make_async_copy(ids_vmem, ids_smem, sem)


def scatter(src, ids, row, target, first):
    for m in range(RB):
        for s in range(SLOTS):
            block = m * SLOTS + s
            orbital = ids[row, 0, block]
            lanes = pl.ds(pl.multiple_of(orbital * AUX, AUX), AUX)
            rows = pl.ds(pl.multiple_of(first + m * BS, BS), BS)
            target[rows, lanes] = src[block * BS : (block + 1) * BS, :]


NT = (((1,), (1,)), ((), ()))


TYPES = 3
CHUNK = TYPES * HALF + 16


def pairs_kernel(place_ref, *refs):
    column, mine, other = refs[:4], (refs[0], *refs[4:6]), refs[6:9]
    out_ref, rows, cols, ids_vmem, ids, sem = refs[9:]
    y, core = place_ref[0], place_ref[1]
    copy = load_ids([*column, *mine[1:], *other], ids_vmem, ids, sem)
    copy.start()
    rows[...] = jnp.zeros_like(rows)
    cols[...] = jnp.zeros_like(cols)
    copy.wait()
    for d in range(4):
        scatter(column[d], ids, d, cols, lax.rem(y + d, 4) * HALF)
    for t in range(TYPES):
        scatter(mine[t], ids, 0 if t == 0 else 3 + t, rows, t * CHIP + core * HALF)
        scatter(other[t], ids, 6 + t, rows, t * CHIP + (1 - core) * HALF)
    exponents = {}
    for t in range(TYPES):
        part = lax.dot_general(
            rows[t * CHIP : (t + 1) * CHIP, :], cols[...], NT, preferred_element_type=jnp.float32
        )
        for i in range(4):
            for k in range(2):
                coded, exponent = encode(
                    part[k * HALF : (k + 1) * HALF, i * HALF : (i + 1) * HALF]
                )
                out_ref[i * 2 + k, t * HALF : (t + 1) * HALF, :] = coded
                exponents[i, k, t] = exponent
    for i in range(4):
        for k in range(2):
            block = pick_rows([exponents[i, k, t] for t in range(TYPES)], HALF)
            out_ref[i * 2 + k, TYPES * HALF :, :] = block.astype(jnp.int16)


def put(ref, values):
    coded, exponent = encode(values)
    ref[:HALF, :] = coded
    ref[HALF:, :] = jnp.broadcast_to(exponent, (16, values.shape[1])).astype(jnp.int16)


def middle_kernel(place_ref, in_ref, own_ref, near_ref, across_ref, same_ref, swapped_ref):
    core = place_ref[1]
    for t, ref in enumerate((own_ref, near_ref, across_ref)):
        halves = []
        for k in range(2):
            total = None
            for x in range(4):
                exps = in_ref[x * 2 + k, TYPES * HALF :, :].astype(jnp.int32)
                value = decode(in_ref[x * 2 + k, t * HALF : (t + 1) * HALF, :], exps, t)
                total = value if total is None else total + value
            halves.append(total)
        put(ref, jnp.concatenate(halves, axis=1))
        if t == 2:
            first = core == 0
            put(same_ref, jnp.where(first, halves[0], halves[1]).T)
            put(swapped_ref, jnp.where(first, halves[1], halves[0]).T)


def cross(z):
    return jnp.where(z < 2, 3 - z, z - 2)


def assemble_kernel(place_ref, own_ref, near_ref, across_ref, same_ref, swapped_ref, out_ref):
    core, z = place_ref[1], place_ref[2]
    flipped = z + 1 - 2 * lax.rem(z, 2)
    out_ref[z] = own_ref[...]
    out_ref[flipped] = near_ref[...]
    out_ref[cross(flipped)] = across_ref[...]
    here = pl.ds(pl.multiple_of(core * HALF, HALF), HALF)
    there = pl.ds(pl.multiple_of((1 - core) * HALF, HALF), HALF)
    out_ref[cross(z), :, here] = same_ref[...]
    out_ref[cross(z), :, there] = swapped_ref[...]


def last_kernel(in_ref, out_ref):
    total = None
    for s in range(4):
        value = decode(in_ref[s, :HALF, :], in_ref[s, HALF:, :].astype(jnp.int32), 0)
        total = value if total is None else total + value
    out_ref[...] = 0.25 * total


def mirror(swap_cores):
    return [
        ((x * 4 + y) * 2 + c, (y * 4 + x) * 2 + (c ^ swap_cores))
        for x in range(4) for y in range(4) for c in range(2)
    ]


def shards(raw_blocks, metric_factor, sig_list, live_count):
    place = jnp.stack([lax.axis_index("y"), lax.axis_index("c"), lax.axis_index("zl")]).astype(jnp.int32)
    own = pl.pallas_call(
        contract_kernel,
        out_shape=jax.ShapeDtypeStruct((PAY, AUX), jnp.bfloat16),
        in_specs=[ANY, ANY, SMEM, SMEM],
        out_specs=VMEM,
        scratch_shapes=[
            pltpu.VMEM(raw_blocks.shape, jnp.bfloat16),
            pltpu.VMEM((AUX, AUX), jnp.bfloat16),
            pltpu.SemaphoreType.DMA((2,)),
        ],
        compiler_params=params(24),
        name="contract",
    )(raw_blocks, metric_factor, sig_list, live_count.reshape(RB))

    def swap(a):
        return lax.ppermute(a, "c", [(0, 1), (1, 0)])

    flip = [(i ^ 1, i) for i in range(4)]
    across = lax.ppermute(own, "zl", [(CROSS[i], i) for i in range(4)])
    near = lax.ppermute(own, "zl", flip)
    column = [own] + [lax.ppermute(own, "y", [((i + d) % 4, i) for i in range(4)]) for d in (1, 2, 3)]
    tiles = pl.pallas_call(
        pairs_kernel,
        out_shape=jax.ShapeDtypeStruct((8, CHUNK, HALF), jnp.int16),
        in_specs=[SMEM] + [VMEM] * 9,
        out_specs=VMEM,
        scratch_shapes=[
            pltpu.VMEM((TYPES * CHIP, NOB * AUX), jnp.bfloat16),
            pltpu.VMEM((4 * HALF, NOB * AUX), jnp.bfloat16),
            pltpu.VMEM((9, 8, 128), jnp.int32),
            pltpu.SMEM((9, 8, 128), jnp.int32),
            pltpu.SemaphoreType.DMA,
        ],
        compiler_params=params(40),
        name="pairs",
    )(place, *column, near, across, swap(own), swap(near), swap(across))
    arrived = lax.all_to_all(tiles, ("x", "c"), 0, 0, tiled=True)
    wide = jax.ShapeDtypeStruct((TILE, CHIP), jnp.int16)
    narrow = jax.ShapeDtypeStruct((TILE, HALF), jnp.int16)
    own_tile, near_tile, across_tile, same, swapped = pl.pallas_call(
        middle_kernel,
        out_shape=[wide] * 3 + [narrow] * 2,
        in_specs=[SMEM, VMEM],
        out_specs=[VMEM] * 5,
        compiler_params=params(16),
        name="middle",
    )(place, arrived)
    ordered = pl.pallas_call(
        assemble_kernel,
        out_shape=jax.ShapeDtypeStruct((4, TILE, CHIP), jnp.int16),
        in_specs=[SMEM] + [VMEM] * 5,
        out_specs=VMEM,
        compiler_params=params(16),
        name="assemble",
    )(
        place,
        own_tile,
        lax.ppermute(near_tile, "zl", flip),
        lax.ppermute(across_tile, "zl", [(i, CROSS[i]) for i in range(4)]),
        lax.ppermute(same, ("x", "y", "c"), mirror(0)),
        lax.ppermute(swapped, ("x", "y", "c"), mirror(1)),
    )
    arrived = lax.all_to_all(ordered, "zh", 0, 0, tiled=True)
    return pl.pallas_call(
        last_kernel,
        out_shape=jax.ShapeDtypeStruct((HALF, CHIP), jnp.float32),
        in_specs=[VMEM],
        out_specs=VMEM,
        compiler_params=params(16),
        name="last",
    )(arrived)


def solution(mesh):
    fine = Mesh(mesh.devices.reshape(4, 4, 4, 4, 2), AXES)
    blk, grp = ("y", "zl", "c"), ("x", "zh")
    placed = (P(blk, grp, None, None), P(), P(blk, grp), P(blk, grp))
    return jax.shard_map(shards, mesh=fine, in_specs=placed, out_specs=P(blk, grp), check_vma=False)
```

time: 149 us -> 121 us (0.81)
  the two profiles are of different devices: /device:TPU:32 before, /device:TPU:36 now
where the time goes in v3:
time: 121 us
  blocking collectives  51.9 us (43%)
  starting transfers between devices  40 us (33%)
  waiting for transfers between devices  15.8 us (13%)
  Pallas kernels  10.1 us (8%)
  local copies, waits for them, and re-layouts  2.59 us (2%)
    all_to_all x1, blocking collectives, shards(): arrived = lax.all_to_all(ordered, 'zh', 0, 0, tiled=True)  35.7 us
    all_to_all x1, blocking collectives, shards(): arrived = lax.all_to_all(tiles, ('x', 'c'), 0, 0, tiled=True)  16.2 us
    ppermute x3, starting transfers between devices, shards(): lax.ppermute(own, 'y', [((i + d) % 4, i) for i in range(4)])  11.6 us
    pallas_call x1, Pallas kernels, shards(): pl.pallas_call(pairs_kernel, out_shape=jax.ShapeDtypeStruct((8, CHUNK, HA...  6.66 us
    ppermute x3, starting transfers between devices, swap(): return lax.ppermute(a, 'c', [(0, 1), (1, 0)])  6.24 us
    ppermute x3, waiting for transfers between devices, shards(): lax.ppermute(own, 'y', [((i + d) % 4, i) for i in range(4)])  5.82 us
    ppermute x1, starting transfers between devices, shards(): lax.ppermute(same, ('x', 'y', 'c'), mirror(0))  5.32 us
    ppermute x1, starting transfers between devices, shards(): across = lax.ppermute(own, 'zl', [(CROSS[i], i) for i in range(4)])  5.18 us
  transfers between devices with their start and end apart: 12, of which 5 were waited for; matrix products, arithmetic and copies ran while one was open for 0% of the time, Pallas kernels for 0%

profile of v3, /device:TPU:36, one launch (start us, length us, event | category | flops | bytes accessed | tf_op | source)
XLA Modules:
  0.0 120.8 jit_solution(8620759206136022195)
XLA Ops:
  0.0 0.7 copy-done.3
  0.7 0.0 copy-done.2
  0.7 1.0 copy-done
  1.7 0.9 copy-done.1
  2.6 1.3 %contract.1.refs_0_ = bf16[784,256]{1,0:T(8,128)(2,1)S(1)} custom-call(bf16[2,6,64,256]{3,2,1,0:T(8,128)(2,1)S(1)} %copy-done, bf16[256,256]{1,0:T(8,128)(2,1)S(1)} %copy-done.1, s32[2,6]{1,0:T(2,128)S(1)} %copy-done.2, s32[2]{0:T(128)S(1)} %bitcast.4), custom_call_target="tpu_custom_call" | custom-call | tf_op jit(solution)/shard_map/contract/pallas_call | solution.py:188
  3.9 1.9 %collective-permute-start.5 = (bf16[784,256]{1,0:T(8,128)(2,1)S(1)}, bf16[784,256]{1,0:T(8,128)(2,1)S(1)}, u32[]{:S(2)}, u32[]{:S(2)}) collective-permute-start(bf16[784,256]{1,0:T(8,128)(2,1)S(1)} %contract.1.refs_0_), channel_id=1, source_target_pairs={{0,1},{1,0},{2,3},{3,2},{4,5},{5,4},{6,7},{7,6},{8,9},{9,8},{10,11... | collective-permute-start | bytes 1204232 | tf_op jit(solution)/shard_map/ppermute | solution.py:203
  5.9 5.2 %collective-permute-start.4 = (bf16[784,256]{1,0:T(8,128)(2,1)S(1)}, bf16[784,256]{1,0:T(8,128)(2,1)S(1)}, u32[]{:S(2)}, u32[]{:S(2)}) collective-permute-start(bf16[784,256]{1,0:T(8,128)(2,1)S(1)} %contract.1.refs_0_), channel_id=1, source_target_pairs={{6,0},{4,2},{0,4},{2,6},{7,1},{5,3},{1,5},{3,7},{14,8},{12,10},{8,... | collective-permute-start | bytes 1204232 | tf_op jit(solution)/shard_map/ppermute | solution.py:206
  11.0 2.0 %collective-permute-start.3 = (bf16[784,256]{1,0:T(8,128)(2,1)S(1)}, bf16[784,256]{1,0:T(8,128)(2,1)S(1)}, u32[]{:S(2)}, u32[]{:S(2)}) collective-permute-start(bf16[784,256]{1,0:T(8,128)(2,1)S(1)} %contract.1.refs_0_), channel_id=1, source_target_pairs={{2,0},{0,2},{6,4},{4,6},{3,1},{1,3},{7,5},{5,7},{10,8},{8,10},{14,... | collective-permute-start | bytes 1204232 | tf_op jit(solution)/shard_map/ppermute | solution.py:207
  13.1 3.5 %collective-permute-start.2 = (bf16[784,256]{1,0:T(8,128)(2,1)S(1)}, bf16[784,256]{1,0:T(8,128)(2,1)S(1)}, u32[]{:S(2)}, u32[]{:S(2)}) collective-permute-start(bf16[784,256]{1,0:T(8,128)(2,1)S(1)} %contract.1.refs_0_), channel_id=1, source_target_pairs={{24,0},{0,8},{8,16},{16,24},{25,1},{1,9},{9,17},{17,25},{26,2},{2,... | collective-permute-start | bytes 1204232 | tf_op jit(solution)/shard_map/ppermute | solution.py:208
  16.6 4.8 %collective-permute-start.1 = (bf16[784,256]{1,0:T(8,128)(2,1)S(1)}, bf16[784,256]{1,0:T(8,128)(2,1)S(1)}, u32[]{:S(2)}, u32[]{:S(2)}) collective-permute-start(bf16[784,256]{1,0:T(8,128)(2,1)S(1)} %contract.1.refs_0_), channel_id=1, source_target_pairs={{16,0},{24,8},{0,16},{8,24},{17,1},{25,9},{1,17},{9,25},{18,2},{26... | collective-permute-start | bytes 1204232 | tf_op jit(solution)/shard_map/ppermute | solution.py:208
  21.4 0.0 collective-permute-done.5.refs_6_
  21.4 3.3 %collective-permute-start = (bf16[784,256]{1,0:T(8,128)(2,1)S(1)}, bf16[784,256]{1,0:T(8,128)(2,1)S(1)}, u32[]{:S(2)}, u32[]{:S(2)}) collective-permute-start(bf16[784,256]{1,0:T(8,128)(2,1)S(1)} %contract.1.refs_0_), channel_id=1, source_target_pairs={{8,0},{16,8},{24,16},{0,24},{9,1},{17,9},{25,17},{1,25},{10,2},{18... | collective-permute-start | bytes 1204232 | tf_op jit(solution)/shard_map/ppermute | solution.py:208
  24.7 3.8 %collective-permute-done.4.refs_5_ = bf16[784,256]{1,0:T(8,128)(2,1)S(1)} collective-permute-done((bf16[784,256]{1,0:T(8,128)(2,1)S(1)}, bf16[784,256]{1,0:T(8,128)(2,1)S(1)}, u32[]{:S(2)}, u32[]{:S(2)}) %collective-permute-start.4) | collective-permute-done | bytes 401440 | tf_op jit(solution)/shard_map/ppermute | solution.py:206
  28.5 1.9 %collective-permute-start.7 = (bf16[784,256]{1,0:T(8,128)(2,1)S(1)}, bf16[784,256]{1,0:T(8,128)(2,1)S(1)}, u32[]{:S(2)}, u32[]{:S(2)}) collective-permute-start(bf16[784,256]{1,0:T(8,128)(2,1)S(1)} %collective-permute-done.4.refs_5_), channel_id=1, source_target_pairs={{0,1},{1,0},{2,3},{3,2},{4,5},{5,4},{6,7},{7,6},{8,9},{9,8},{10,11... | collective-permute-start | bytes 1204232 | tf_op jit(solution)/shard_map/ppermute | solution.py:203
  30.4 0.0 collective-permute-done.3.refs_4_
  30.4 2.4 %collective-permute-start.6 = (bf16[784,256]{1,0:T(8,128)(2,1)S(1)}, bf16[784,256]{1,0:T(8,128)(2,1)}, u32[]{:S(2)}, u32[]{:S(2)}) collective-permute-start(bf16[784,256]{1,0:T(8,128)(2,1)S(1)} %collective-permute-done.3.refs_4_), channel_id=1, source_target_pairs={{0,1},{1,0},{2,3},{3,2},{4,5},{5,4},{6,7},{7,6},{8,9},{9,8},{10,11... | collective-permute-start | bytes 1204232 | tf_op jit(solution)/shard_map/ppermute | solution.py:203
  32.8 0.1 pad_add_fusion.place_ref
  32.9 0.0 collective-permute-done.2.refs_3_
  32.9 4.5 %collective-permute-done.1.refs_2_ = bf16[784,256]{1,0:T(8,128)(2,1)S(1)} collective-permute-done((bf16[784,256]{1,0:T(8,128)(2,1)S(1)}, bf16[784,256]{1,0:T(8,128)(2,1)S(1)}, u32[]{:S(2)}, u32[]{:S(2)}) %collective-permute-start.1) | collective-permute-done | bytes 401440 | tf_op jit(solution)/shard_map/ppermute | solution.py:208
  37.3 1.4 %collective-permute-done.refs_1_ = bf16[784,256]{1,0:T(8,128)(2,1)S(1)} collective-permute-done((bf16[784,256]{1,0:T(8,128)(2,1)S(1)}, bf16[784,256]{1,0:T(8,128)(2,1)S(1)}, u32[]{:S(2)}, u32[]{:S(2)}) %collective-permute-start) | collective-permute-done | bytes 401440 | tf_op jit(solution)/shard_map/ppermute | solution.py:208
  38.7 6.7 %pairs.1 = s16[8,400,128]{2,1,0:T(8,128)(2,1)S(1)} custom-call(s32[3]{0:T(128)S(1)} %pad_add_fusion.place_ref, bf16[784,256]{1,0:T(8,128)(2,1)S(1)} %contract.1.refs_0_, bf16[784,256]{1,0:T(8,128)(2,1)S(1)} %collective-permute-done.refs_1_, bf16[784,256]{1,0:T(8,128)(2,1)S(1)} %collective-permute-done.1.refs_2_, ...), custom_call_target="tpu_custom_call" | custom-call | tf_op jit(solution)/shard_map/pairs/pallas_call | solution.py:209
  45.4 16.2 %all_to_all.10.in_ref = s16[8,400,128]{2,1,0:T(8,128)(2,1)S(1)} all-to-all(s16[8,400,128]{2,1,0:T(8,128)(2,1)S(1)} %pairs.1), channel_id=1, replica_groups=mesh['x'=4,'zh'=4,'y'=4,'zl'=4,'c'=2] {'x','c'}, dimensions={0} | all-to-all | bytes 1638400 | tf_op jit(solution)/shard_map/all_to_all | solution.py:224
  61.6 0.8 middle.1
  62.4 3.2 %collective-permute-start.8 = (s16[144,256]{1,0:T(8,128)(2,1)S(1)}, s16[144,256]{1,0:T(8,128)(2,1)S(1)}, u32[]{:S(2)}, u32[]{:S(2)}) collective-permute-start(s16[144,256]{1,0:T(8,128)(2,1)S(1)} %get-tuple-element.11), channel_id=1, source_target_pairs={{2,0},{0,2},{6,4},{4,6},{3,1},{1,3},{7,5},{5,7},{10,8},{8,10},{14,... | collective-permute-start | bytes 221192 | tf_op jit(solution)/shard_map/ppermute | solution.py:245
  65.6 3.5 %collective-permute-start.9 = (s16[144,256]{1,0:T(8,128)(2,1)S(1)}, s16[144,256]{1,0:T(8,128)(2,1)S(1)}, u32[]{:S(2)}, u32[]{:S(2)}) collective-permute-start(s16[144,256]{1,0:T(8,128)(2,1)S(1)} %get-tuple-element.12), channel_id=1, source_target_pairs={{0,6},{2,4},{4,0},{6,2},{1,7},{3,5},{5,1},{7,3},{8,14},{10,12},{12... | collective-permute-start | bytes 221192 | tf_op jit(solution)/shard_map/ppermute | solution.py:246
  69.2 5.3 %collective-permute-start.10 = (s16[144,128]{1,0:T(8,128)(2,1)S(1)}, s16[144,128]{1,0:T(8,128)(2,1)S(1)}, u32[]{:S(2)}, u32[]{:S(2)}) collective-permute-start(s16[144,128]{1,0:T(8,128)(2,1)S(1)} %get-tuple-element.13), channel_id=1, source_target_pairs={{0,0},{1,1},{8,128},{9,129},{16,256},{17,257},{24,384},{25,385},{1... | collective-permute-start | bytes 110600 | tf_op jit(solution)/shard_map/ppermute | solution.py:247
  74.5 3.0 %collective-permute-start.11 = (s16[144,128]{1,0:T(8,128)(2,1)S(1)}, s16[144,128]{1,0:T(8,128)(2,1)S(1)}, u32[]{:S(2)}, u32[]{:S(2)}) collective-permute-start(s16[144,128]{1,0:T(8,128)(2,1)S(1)} %get-tuple-element.14), channel_id=1, source_target_pairs={{0,1},{1,0},{8,129},{9,128},{16,257},{17,256},{24,385},{25,384},{1... | collective-permute-start | bytes 110600 | tf_op jit(solution)/shard_map/ppermute | solution.py:248
  77.5 1.5 %collective-permute-done.10.same_ref = s16[144,128]{1,0:T(8,128)(2,1)S(1)} collective-permute-done((s16[144,128]{1,0:T(8,128)(2,1)S(1)}, s16[144,128]{1,0:T(8,128)(2,1)S(1)}, u32[]{:S(2)}, u32[]{:S(2)}) %collective-permute-start.10) | collective-permute-done | bytes 36896 | tf_op jit(solution)/shard_map/ppermute | solution.py:247
  78.9 4.7 %collective-permute-done.11.swapped_ref = s16[144,128]{1,0:T(8,128)(2,1)S(1)} collective-permute-done((s16[144,128]{1,0:T(8,128)(2,1)S(1)}, s16[144,128]{1,0:T(8,128)(2,1)S(1)}, u32[]{:S(2)}, u32[]{:S(2)}) %collective-permute-start.11) | collective-permute-done | bytes 36896 | tf_op jit(solution)/shard_map/ppermute | solution.py:248
  83.7 0.6 assemble.1
  84.3 35.7 %all_to_all.11.in_ref = s16[4,144,256]{2,1,0:T(8,128)(2,1)S(1)} all-to-all(s16[4,144,256]{2,1,0:T(8,128)(2,1)S(1)} %assemble.1), channel_id=1, replica_groups=mesh['x'=4,'zh'=4,'y'=4,'zl'=4,'c'=2] {'zh'}, dimensions={0} | all-to-all | bytes 589824 | tf_op jit(solution)/shard_map/all_to_all | solution.py:250
  120.0 0.7 last.1
  (8 shorter events, 0.0 us)
Async XLA Ops:
  0.0 0.7 copy-start.3
  0.0 0.7 copy-start.2
  0.7 1.0 copy-start
  1.7 0.9 copy-start.1
  3.9 17.5 %collective-permute-start.5 = (bf16[784,256]{1,0:T(8,128)(2,1)S(1)}, bf16[784,256]{1,0:T(8,128)(2,1)S(1)}, u32[]{:S(2)}, u32[]{:S(2)}) collective-permute-start(bf16[784,256]{1,0:T(8,128)(2,1)S(1)} %contract.1.refs_0_), channel_id=1, source_target_pairs={{0,1},{1,0},{2,3},{3,2},{4,5},{5,4},{6,7},{7,6},{8,9},{9,8},{10,11... | collective-permute-start | bytes 1204232 | tf_op jit(solution)/shard_map/ppermute | solution.py:203
  5.9 22.6 %collective-permute-start.4 = (bf16[784,256]{1,0:T(8,128)(2,1)S(1)}, bf16[784,256]{1,0:T(8,128)(2,1)S(1)}, u32[]{:S(2)}, u32[]{:S(2)}) collective-permute-start(bf16[784,256]{1,0:T(8,128)(2,1)S(1)} %contract.1.refs_0_), channel_id=1, source_target_pairs={{6,0},{4,2},{0,4},{2,6},{7,1},{5,3},{1,5},{3,7},{14,8},{12,10},{8,... | collective-permute-start | bytes 1204232 | tf_op jit(solution)/shard_map/ppermute | solution.py:206
  11.0 19.4 %collective-permute-start.3 = (bf16[784,256]{1,0:T(8,128)(2,1)S(1)}, bf16[784,256]{1,0:T(8,128)(2,1)S(1)}, u32[]{:S(2)}, u32[]{:S(2)}) collective-permute-start(bf16[784,256]{1,0:T(8,128)(2,1)S(1)} %contract.1.refs_0_), channel_id=1, source_target_pairs={{2,0},{0,2},{6,4},{4,6},{3,1},{1,3},{7,5},{5,7},{10,8},{8,10},{14,... | collective-permute-start | bytes 1204232 | tf_op jit(solution)/shard_map/ppermute | solution.py:207
  13.1 19.8 %collective-permute-start.2 = (bf16[784,256]{1,0:T(8,128)(2,1)S(1)}, bf16[784,256]{1,0:T(8,128)(2,1)S(1)}, u32[]{:S(2)}, u32[]{:S(2)}) collective-permute-start(bf16[784,256]{1,0:T(8,128)(2,1)S(1)} %contract.1.refs_0_), channel_id=1, source_target_pairs={{24,0},{0,8},{8,16},{16,24},{25,1},{1,9},{9,17},{17,25},{26,2},{2,... | collective-permute-start | bytes 1204232 | tf_op jit(solution)/shard_map/ppermute | solution.py:208
  16.6 20.8 %collective-permute-start.1 = (bf16[784,256]{1,0:T(8,128)(2,1)S(1)}, bf16[784,256]{1,0:T(8,128)(2,1)S(1)}, u32[]{:S(2)}, u32[]{:S(2)}) collective-permute-start(bf16[784,256]{1,0:T(8,128)(2,1)S(1)} %contract.1.refs_0_), channel_id=1, source_target_pairs={{16,0},{24,8},{0,16},{8,24},{17,1},{25,9},{1,17},{9,25},{18,2},{26... | collective-permute-start | bytes 1204232 | tf_op jit(solution)/shard_map/ppermute | solution.py:208
  21.4 17.3 %collective-permute-start = (bf16[784,256]{1,0:T(8,128)(2,1)S(1)}, bf16[784,256]{1,0:T(8,128)(2,1)S(1)}, u32[]{:S(2)}, u32[]{:S(2)}) collective-permute-start(bf16[784,256]{1,0:T(8,128)(2,1)S(1)} %contract.1.refs_0_), channel_id=1, source_target_pairs={{8,0},{16,8},{24,16},{0,24},{9,1},{17,9},{25,17},{1,25},{10,2},{18... | collective-permute-start | bytes 1204232 | tf_op jit(solution)/shard_map/ppermute | solution.py:208
  28.5 10.2 %collective-permute-start.7 = (bf16[784,256]{1,0:T(8,128)(2,1)S(1)}, bf16[784,256]{1,0:T(8,128)(2,1)S(1)}, u32[]{:S(2)}, u32[]{:S(2)}) collective-permute-start(bf16[784,256]{1,0:T(8,128)(2,1)S(1)} %collective-permute-done.4.refs_5_), channel_id=1, source_target_pairs={{0,1},{1,0},{2,3},{3,2},{4,5},{5,4},{6,7},{7,6},{8,9},{9,8},{10,11... | collective-permute-start | bytes 1204232 | tf_op jit(solution)/shard_map/ppermute | solution.py:203
  30.4 8.3 %collective-permute-start.6 = (bf16[784,256]{1,0:T(8,128)(2,1)S(1)}, bf16[784,256]{1,0:T(8,128)(2,1)}, u32[]{:S(2)}, u32[]{:S(2)}) collective-permute-start(bf16[784,256]{1,0:T(8,128)(2,1)S(1)} %collective-permute-done.3.refs_4_), channel_id=1, source_target_pairs={{0,1},{1,0},{2,3},{3,2},{4,5},{5,4},{6,7},{7,6},{8,9},{9,8},{10,11... | collective-permute-start | bytes 1204232 | tf_op jit(solution)/shard_map/ppermute | solution.py:203
  62.4 21.3 %collective-permute-start.8 = (s16[144,256]{1,0:T(8,128)(2,1)S(1)}, s16[144,256]{1,0:T(8,128)(2,1)S(1)}, u32[]{:S(2)}, u32[]{:S(2)}) collective-permute-start(s16[144,256]{1,0:T(8,128)(2,1)S(1)} %get-tuple-element.11), channel_id=1, source_target_pairs={{2,0},{0,2},{6,4},{4,6},{3,1},{1,3},{7,5},{5,7},{10,8},{8,10},{14,... | collective-permute-start | bytes 221192 | tf_op jit(solution)/shard_map/ppermute | solution.py:245
  65.6 18.1 %collective-permute-start.9 = (s16[144,256]{1,0:T(8,128)(2,1)S(1)}, s16[144,256]{1,0:T(8,128)(2,1)S(1)}, u32[]{:S(2)}, u32[]{:S(2)}) collective-permute-start(s16[144,256]{1,0:T(8,128)(2,1)S(1)} %get-tuple-element.12), channel_id=1, source_target_pairs={{0,6},{2,4},{4,0},{6,2},{1,7},{3,5},{5,1},{7,3},{8,14},{10,12},{12... | collective-permute-start | bytes 221192 | tf_op jit(solution)/shard_map/ppermute | solution.py:246
  69.2 9.8 %collective-permute-start.10 = (s16[144,128]{1,0:T(8,128)(2,1)S(1)}, s16[144,128]{1,0:T(8,128)(2,1)S(1)}, u32[]{:S(2)}, u32[]{:S(2)}) collective-permute-start(s16[144,128]{1,0:T(8,128)(2,1)S(1)} %get-tuple-element.13), channel_id=1, source_target_pairs={{0,0},{1,1},{8,128},{9,129},{16,256},{17,257},{24,384},{25,385},{1... | collective-permute-start | bytes 110600 | tf_op jit(solution)/shard_map/ppermute | solution.py:247
  74.5 9.2 %collective-permute-start.11 = (s16[144,128]{1,0:T(8,128)(2,1)S(1)}, s16[144,128]{1,0:T(8,128)(2,1)S(1)}, u32[]{:S(2)}, u32[]{:S(2)}) collective-permute-start(s16[144,128]{1,0:T(8,128)(2,1)S(1)} %get-tuple-element.14), channel_id=1, source_target_pairs={{0,1},{1,0},{8,129},{9,128},{16,257},{17,256},{24,385},{25,384},{1... | collective-permute-start | bytes 110600 | tf_op jit(solution)/shard_map/ppermute | solution.py:248

commit v4 on v3

v4 whole, which is shorter than its diff:
```python
import jax
import jax.numpy as jnp
from jax import lax
from jax.experimental import pallas as pl
from jax.experimental.pallas import tpu as pltpu
from jax.sharding import Mesh, PartitionSpec as P

AXES = ("x", "zh", "y", "zl", "c")
NOB = 16
SLOTS = 6
BS = 64
AUX = 256
RB = 2
HALF = RB * BS
CHIP = 2 * HALF
BODY = RB * SLOTS * BS
PAY = BODY + 16
TILE = HALF + 16
LEVELS = 32000.0
CROSS = (3, 2, 0, 1)
VMEM = pl.BlockSpec(memory_space=pltpu.VMEM)
SMEM = pl.BlockSpec(memory_space=pltpu.SMEM)
ANY = pl.BlockSpec(memory_space=pl.ANY)


def params(mib):
    return pltpu.CompilerParams(vmem_limit_bytes=mib * 1024 * 1024)


def contract_kernel(raw_hbm, metric_hbm, sig_ref, live_ref, out_ref, raw_ref, metric_ref, sems):
    copies = [
        pltpu.make_async_copy(metric_hbm, metric_ref, sems.at[0]),
        pltpu.make_async_copy(raw_hbm, raw_ref, sems.at[1]),
    ]
    for copy in copies:
        copy.start()
    lane = lax.broadcasted_iota(jnp.int32, (16, AUX), 1)
    ids = jnp.zeros((16, AUX), jnp.int32)
    for m in range(RB):
        for s in range(SLOTS):
            ids = jnp.where(lane == m * SLOTS + s, sig_ref[m, s], ids)
    out_ref[BODY:, :] = ids.astype(jnp.float32).astype(jnp.bfloat16)
    for copy in copies:
        copy.wait()
    for m in range(RB):
        for s in range(SLOTS):
            block = m * SLOTS + s
            product = jnp.dot(
                raw_ref[m, s], metric_ref[...], preferred_element_type=jnp.float32
            )
            live = (s < live_ref[m]).astype(jnp.float32)
            out_ref[block * BS : (block + 1) * BS, :] = (product * live).astype(jnp.bfloat16)


def encode(values):
    top = jnp.max(jnp.abs(values), axis=0, keepdims=True)
    exponent = jnp.ceil(jnp.log2(jnp.maximum(top, 1e-30)) + 1e-3)
    coded = jnp.round(values * (LEVELS * jnp.exp2(-exponent)))
    return coded.astype(jnp.int32).astype(jnp.int16), exponent.astype(jnp.int32)


def decode(coded, exponents, row):
    scale = jnp.exp2(exponents[row : row + 1, :].astype(jnp.float32)) * (1.0 / LEVELS)
    return coded.astype(jnp.int32).astype(jnp.float32) * scale


def pick_rows(rows, width):
    at = lax.broadcasted_iota(jnp.int32, (16, width), 0)
    block = jnp.zeros((16, width), jnp.int32)
    for i, row in enumerate(rows):
        block = jnp.where(at == i, jnp.broadcast_to(row, (16, width)), block)
    return block


def load_ids(sources, ids_vmem, ids_smem, sem):
    for i, src in enumerate(sources):
        ids = src[BODY:PAY, 0:128].astype(jnp.float32).astype(jnp.int32)
        ids_vmem[i] = ids[0:8, :]
    return pltpu.make_async_copy(ids_vmem, ids_smem, sem)


def scatter(src, ids, row, target, first):
    for m in range(RB):
        for s in range(SLOTS):
            block = m * SLOTS + s
            orbital = ids[row, 0, block]
            lanes = pl.ds(pl.multiple_of(orbital * AUX, AUX), AUX)
            rows = pl.ds(pl.multiple_of(first + m * BS, BS), BS)
            target[rows, lanes] = src[block * BS : (block + 1) * BS, :]


NT = (((1,), (1,)), ((), ()))


TYPES = 3
CHUNK = 2 * CHIP + 16
WIDE = CHIP + 16


def column_kernel(place_ref, *refs):
    column, (out_ref, ids_vmem, ids, sem) = refs[:4], refs[4:]
    copy = load_ids(column, ids_vmem, ids, sem)
    copy.start()
    out_ref[...] = jnp.zeros_like(out_ref)
    copy.wait()
    for i, d in enumerate((0, 2, 1, 3)):
        scatter(column[i], ids, i, out_ref, lax.rem(place_ref[0] + d, 4) * HALF)


def pairs_kernel(place_ref, *refs):
    cols, *wide = refs[:4]
    out_ref, rows, ids_vmem, ids, sem = refs[4:]
    core = place_ref[1]
    halves = [src.at[k] for src in wide for k in range(2)]
    copy = load_ids(halves, ids_vmem, ids, sem)
    copy.start()
    rows[...] = jnp.zeros_like(rows)
    copy.wait()
    for i, t in enumerate((0, 2 - core, 1 + core)):
        for k in range(2):
            scatter(halves[i * 2 + k], ids, i * 2 + k, rows, t * CHIP + k * HALF)
    exponents = {}
    for t in range(TYPES):
        part = lax.dot_general(
            rows[t * CHIP : (t + 1) * CHIP, :], cols[...], NT, preferred_element_type=jnp.float32
        )
        for i in range(4):
            coded, exponents[t, i] = encode(part[:, i * HALF : (i + 1) * HALF])
            chunk, first = i * 2 + t // 2, (t % 2) * CHIP
            out_ref[chunk, first : first + CHIP, :] = coded
    for i in range(4):
        out_ref[i * 2 + 1, CHIP : 2 * CHIP, :] = jnp.zeros((CHIP, HALF), jnp.int16)
        for k in range(2):
            block = pick_rows([exponents[k * 2, i], exponents[1, i]], HALF)
            out_ref[i * 2 + k, 2 * CHIP :, :] = block.astype(jnp.int16)


def middle_kernel(place_ref, in_ref, even_ref, odd_ref):
    tiles = []
    for u in range(2):
        halves = []
        for k in range(2):
            total = None
            for x in range(4):
                exps = in_ref[x * 2 + k, 2 * CHIP :, :].astype(jnp.int32)
                value = decode(in_ref[x * 2 + k, u * CHIP : (u + 1) * CHIP, :], exps, u)
                total = value if total is None else total + value
            halves.append(total)
        tiles.append(jnp.concatenate(halves, axis=1))
    first = encode(tiles[0])
    second = encode(jnp.where(place_ref[1] == 0, tiles[1], tiles[0].T))

    def write(ref, pair):
        ref[:CHIP, :] = pair[0]
        ref[CHIP:, :] = jnp.broadcast_to(pair[1], (16, CHIP)).astype(jnp.int16)

    even = lax.rem(place_ref[2], 2) == 0

    @pl.when(even)
    def _():
        write(even_ref, first)
        write(odd_ref, second)

    @pl.when(jnp.logical_not(even))
    def _():
        write(even_ref, second)
        write(odd_ref, first)


def join_kernel(place_ref, a_ref, b_ref, keep_ref, send_ref):
    core = place_ref[1]
    for ref, half in ((keep_ref, core), (send_ref, 1 - core)):
        rows = pl.ds(pl.multiple_of(half * HALF, HALF), HALF)
        ref[...] = sum(
            decode(src[rows, :], src[CHIP:, :].astype(jnp.int32), 0) for src in (a_ref, b_ref)
        )


def last_kernel(keep_ref, come_ref, out_ref):
    out_ref[...] = 0.25 * (keep_ref[...] + come_ref[...])


def index_of(x, zh, y, zl, c):
    return (((x * 4 + zh) * 4 + y) * 4 + zl) * 2 + c


def far_round(r):
    pairs = []
    for x in range(4):
        for s in range(4):
            for y in range(4):
                for z in range(4):
                    kinds = (
                        ((x, z, y, z), (x, z, y, z ^ 1)),
                        ((x, z, y, CROSS[z]), (y, CROSS[z], x, z)),
                    )
                    for c in range(2):
                        dest = kinds[c][(s + r) % 2]
                        pairs.append((index_of(x, s, y, z, c), index_of(*dest, s // 2)))
    return pairs


def shards(raw_blocks, metric_factor, sig_list, live_count):
    place = jnp.stack([lax.axis_index("y"), lax.axis_index("c"), lax.axis_index("zh")]).astype(jnp.int32)
    own = pl.pallas_call(
        contract_kernel,
        out_shape=jax.ShapeDtypeStruct((PAY, AUX), jnp.bfloat16),
        in_specs=[ANY, ANY, SMEM, SMEM],
        out_specs=VMEM,
        scratch_shapes=[
            pltpu.VMEM(raw_blocks.shape, jnp.bfloat16),
            pltpu.VMEM((AUX, AUX), jnp.bfloat16),
            pltpu.SemaphoreType.DMA((2,)),
        ],
        compiler_params=params(24),
        name="contract",
    )(raw_blocks, metric_factor, sig_list, live_count.reshape(RB))

    def swap(a):
        return lax.ppermute(a, "c", [(0, 1), (1, 0)])

    both = lax.all_gather(own, "c")
    along = lax.ppermute(
        both,
        ("zl", "c"),
        [(CROSS[i] * 2, i * 2) for i in range(4)] + [((i ^ 1) * 2 + 1, i * 2 + 1) for i in range(4)],
    )
    column = [own] + [lax.ppermute(own, "y", [((i + d) % 4, i) for i in range(4)]) for d in (2, 1, 3)]
    dense = pl.pallas_call(
        column_kernel,
        out_shape=jax.ShapeDtypeStruct((4 * HALF, NOB * AUX), jnp.bfloat16),
        in_specs=[SMEM] + [VMEM] * 4,
        out_specs=VMEM,
        scratch_shapes=[
            pltpu.VMEM((4, 8, 128), jnp.int32),
            pltpu.SMEM((4, 8, 128), jnp.int32),
            pltpu.SemaphoreType.DMA,
        ],
        compiler_params=params(16),
        cost_estimate=pl.CostEstimate(flops=20_000_000_000, bytes_accessed=6_000_000, transcendentals=0),
        name="column",
    )(place, *column)
    tiles = pl.pallas_call(
        pairs_kernel,
        out_shape=jax.ShapeDtypeStruct((8, CHUNK, HALF), jnp.int16),
        in_specs=[SMEM] + [VMEM] * 4,
        out_specs=VMEM,
        scratch_shapes=[
            pltpu.VMEM((TYPES * CHIP, NOB * AUX), jnp.bfloat16),
            pltpu.VMEM((6, 8, 128), jnp.int32),
            pltpu.SMEM((6, 8, 128), jnp.int32),
            pltpu.SemaphoreType.DMA,
        ],
        compiler_params=params(24),
        name="pairs",
    )(place, dense, both, along, swap(along))
    arrived = lax.all_to_all(tiles, ("x", "c"), 0, 0, tiled=True)
    wide = jax.ShapeDtypeStruct((WIDE, CHIP), jnp.int16)
    messages = pl.pallas_call(
        middle_kernel,
        out_shape=[wide] * 2,
        in_specs=[SMEM, VMEM],
        out_specs=[VMEM] * 2,
        compiler_params=params(24),
        name="middle",
    )(place, arrived)
    half = jax.ShapeDtypeStruct((HALF, CHIP), jnp.float32)
    keep, send = pl.pallas_call(
        join_kernel,
        out_shape=[half] * 2,
        in_specs=[SMEM, VMEM, VMEM],
        out_specs=[VMEM] * 2,
        compiler_params=params(16),
        name="join",
    )(place, *[lax.ppermute(a, AXES, far_round(r)) for r, a in enumerate(messages)])
    return pl.pallas_call(
        last_kernel,
        out_shape=half,
        in_specs=[VMEM] * 2,
        out_specs=VMEM,
        compiler_params=params(16),
        name="last",
    )(keep, swap(send))


def solution(mesh):
    fine = Mesh(mesh.devices.reshape(4, 4, 4, 4, 2), AXES)
    blk, grp = ("y", "zl", "c"), ("x", "zh")
    placed = (P(blk, grp, None, None), P(), P(blk, grp), P(blk, grp))
    return jax.shard_map(shards, mesh=fine, in_specs=placed, out_specs=P(blk, grp), check_vma=False)
```

time: 121 us -> 103 us (0.85)
  the two profiles are of different devices: /device:TPU:36 before, /device:TPU:81 now
where the time goes in v4:
time: 103 us
  waiting for transfers between devices  32.9 us (32%)
  starting transfers between devices  32.7 us (32%)
  blocking collectives  23.1 us (22%)
  Pallas kernels  10.9 us (11%)
  local copies, waits for them, and re-layouts  3.23 us (3%)
    all_to_all x1, blocking collectives, shards(): arrived = lax.all_to_all(tiles, ('x', 'c'), 0, 0, tiled=True)  20.4 us
    ppermute x2, waiting for transfers between devices, shards(): lax.ppermute(a, AXES, far_round(r))  19.3 us
    ppermute x2, starting transfers between devices, shards(): lax.ppermute(a, AXES, far_round(r))  17.1 us
    ppermute x1, waiting for transfers between devices, shards(): lax.ppermute(both, ('zl', 'c'), [(CROSS[i] * 2, i * 2) for i in range(4)]...  9.92 us
    ppermute x3, starting transfers between devices, shards(): lax.ppermute(own, 'y', [((i + d) % 4, i) for i in range(4)])  7.92 us
    pallas_call x1, Pallas kernels, shards(): pl.pallas_call(pairs_kernel, out_shape=jax.ShapeDtypeStruct((8, CHUNK, HA...  5.65 us
    ppermute x2, starting transfers between devices, swap(): return lax.ppermute(a, 'c', [(0, 1), (1, 0)])  4.16 us
    ppermute x1, starting transfers between devices, shards(): lax.ppermute(both, ('zl', 'c'), [(CROSS[i] * 2, i * 2) for i in range(4)]...  3.53 us
  transfers between devices with their start and end apart: 8, of which 6 were waited for; matrix products, arithmetic and copies ran while one was open for 0% of the time, Pallas kernels for 2%

profile of v4, /device:TPU:81, one launch (start us, length us, event | category | flops | bytes accessed | tf_op | source)
XLA Modules:
  0.0 103.0 jit_solution(8916846760773132776)
XLA Ops:
  0.0 1.0 copy-done
  1.0 0.0 copy-start.1
  1.0 0.9 copy-done.1
  1.9 0.0 copy-start.2
  1.9 0.7 copy-done.2
  2.6 0.0 copy-start.3
  2.6 0.7 copy-done.3
  3.2 1.3 %contract.1.refs_0_ = bf16[784,256]{1,0:T(8,128)(2,1)S(1)} custom-call(bf16[2,6,64,256]{3,2,1,0:T(8,128)(2,1)S(1)} %copy-done, bf16[256,256]{1,0:T(8,128)(2,1)S(1)} %copy-done.1, s32[2,6]{1,0:T(2,128)S(1)} %copy-done.2, s32[2]{0:T(128)S(1)} %bitcast.7), custom_call_target="tpu_custom_call" | custom-call | tf_op jit(solution)/shard_map/contract/pallas_call | solution.py:205
  4.6 2.7 %all-gather = bf16[1568,256]{1,0:T(8,128)(2,1)S(1)} all-gather(bf16[784,256]{1,0:T(8,128)(2,1)S(1)} %contract.1.refs_0_), channel_id=2, replica_groups=mesh['x'=4,'zh'=4,'y'=4,'zl'=4,'c'=2] {'c'}, dimensions={0}, use_global_device_ids=true | all-gather | bytes 1204224 | tf_op jit(solution)/shard_map/all_gather | solution.py:222
  7.3 3.5 %collective-permute-start.3 = (bf16[2,784,256]{2,1,0:T(8,128)(2,1)S(1)}, bf16[2,784,256]{2,1,0:T(8,128)(2,1)S(1)}, u32[]{:S(2)}, u32[]{:S(2)}) collective-permute-start(bf16[2,784,256]{2,1,0:T(8,128)(2,1)S(1)} %bitcast.5), channel_id=1, source_target_pairs={{6,0},{4,2},{0,4},{2,6},{3,1},{1,3},{7,5},{5,7},{14,8},{12,10},{8,... | collective-permute-start | bytes 2408456 | tf_op jit(solution)/shard_map/ppermute | solution.py:223
  10.8 2.0 %collective-permute-start = (bf16[784,256]{1,0:T(8,128)(2,1)S(1)}, bf16[784,256]{1,0:T(8,128)(2,1)S(1)}, u32[]{:S(2)}, u32[]{:S(2)}) collective-permute-start(bf16[784,256]{1,0:T(8,128)(2,1)S(1)} %contract.1.refs_0_), channel_id=1, source_target_pairs={{16,0},{24,8},{0,16},{8,24},{17,1},{25,9},{1,17},{9,25},{18,2},{26... | collective-permute-start | bytes 1204232 | tf_op jit(solution)/shard_map/ppermute | solution.py:228
  12.8 4.0 %collective-permute-start.1 = (bf16[784,256]{1,0:T(8,128)(2,1)S(1)}, bf16[784,256]{1,0:T(8,128)(2,1)S(1)}, u32[]{:S(2)}, u32[]{:S(2)}) collective-permute-start(bf16[784,256]{1,0:T(8,128)(2,1)S(1)} %contract.1.refs_0_), channel_id=1, source_target_pairs={{8,0},{16,8},{24,16},{0,24},{9,1},{17,9},{25,17},{1,25},{10,2},{18... | collective-permute-start | bytes 1204232 | tf_op jit(solution)/shard_map/ppermute | solution.py:228
  16.8 1.9 %collective-permute-start.2 = (bf16[784,256]{1,0:T(8,128)(2,1)S(1)}, bf16[784,256]{1,0:T(8,128)(2,1)S(1)}, u32[]{:S(2)}, u32[]{:S(2)}) collective-permute-start(bf16[784,256]{1,0:T(8,128)(2,1)S(1)} %contract.1.refs_0_), channel_id=1, source_target_pairs={{24,0},{0,8},{8,16},{16,24},{25,1},{1,9},{9,17},{17,25},{26,2},{2,... | collective-permute-start | bytes 1204232 | tf_op jit(solution)/shard_map/ppermute | solution.py:228
  18.8 0.1 pad_add_fusion.place_ref
  18.8 9.9 %collective-permute-done.3.refs_2_ = bf16[2,784,256]{2,1,0:T(8,128)(2,1)S(1)} collective-permute-done((bf16[2,784,256]{2,1,0:T(8,128)(2,1)S(1)}, bf16[2,784,256]{2,1,0:T(8,128)(2,1)S(1)}, u32[]{:S(2)}, u32[]{:S(2)}) %collective-permute-start.3) | collective-permute-done | bytes 802848 | tf_op jit(solution)/shard_map/ppermute | solution.py:223
  28.7 2.2 %collective-permute-start.4 = (bf16[2,784,256]{2,1,0:T(8,128)(2,1)S(1)}, bf16[2,784,256]{2,1,0:T(8,128)(2,1)S(1)}, u32[]{:S(2)}, u32[]{:S(2)}) collective-permute-start(bf16[2,784,256]{2,1,0:T(8,128)(2,1)S(1)} %collective-permute-done.3.refs_2_), channel_id=1, source_target_pairs={{0,1},{1,0},{2,3},{3,2},{4,5},{5,4},{6,7},{7,6},{8,9},{9,8},{10,11... | collective-permute-start | bytes 2408456 | tf_op jit(solution)/shard_map/ppermute | solution.py:220
  31.0 0.0 collective-permute-done.refs_1_
  31.0 1.4 %collective-permute-done.1.refs_2_ = bf16[784,256]{1,0:T(8,128)(2,1)S(1)} collective-permute-done((bf16[784,256]{1,0:T(8,128)(2,1)S(1)}, bf16[784,256]{1,0:T(8,128)(2,1)S(1)}, u32[]{:S(2)}, u32[]{:S(2)}) %collective-permute-start.1) | collective-permute-done | bytes 401440 | tf_op jit(solution)/shard_map/ppermute | solution.py:228
  32.4 1.0 collective-permute-done.2.refs_3_
  33.4 1.8 %column.1.refs_0_ = bf16[512,4096]{1,0:T(8,128)(2,1)S(1)} custom-call(s32[3]{0:T(128)S(1)} %pad_add_fusion.place_ref, bf16[784,256]{1,0:T(8,128)(2,1)S(1)} %contract.1.refs_0_, bf16[784,256]{1,0:T(8,128)(2,1)S(1)} %collective-permute-done.refs_1_, bf16[784,256]{1,0:T(8,128)(2,1)S(1)} %collective-permute-done.1.refs_2_, ...), custom_call_target="tpu_custom_call" | custom-call | flops 20000000000 | bytes 6000000 | tf_op jit(solution)/shard_map/column/pallas_call | solution.py:229
  35.2 0.0 collective-permute-done.4.refs_3_
  35.2 5.7 %pairs.1 = s16[8,528,128]{2,1,0:T(8,128)(2,1)S(1)} custom-call(s32[3]{0:T(128)S(1)} %pad_add_fusion.place_ref, bf16[512,4096]{1,0:T(8,128)(2,1)S(1)} %column.1.refs_0_, bf16[2,784,256]{2,1,0:T(8,128)(2,1)S(1)} %bitcast.6, bf16[2,784,256]{2,1,0:T(8,128)(2,1)S(1)} %collective-permute-done.3.refs_2_, bf16[2,784,256]{2,1,0:T(8,128)(2,1)S(1)} %collective-permute-done.4.refs_3_), custom_call_target="tpu_custom_call" | custom-call | tf_op jit(solution)/shard_map/pairs/pallas_call | solution.py:243
  40.9 20.4 %all_to_all.5.in_ref = s16[8,528,128]{2,1,0:T(8,128)(2,1)S(1)} all-to-all(s16[8,528,128]{2,1,0:T(8,128)(2,1)S(1)} %pairs.1), channel_id=1, replica_groups=mesh['x'=4,'zh'=4,'y'=4,'zl'=4,'c'=2] {'x','c'}, dimensions={0} | all-to-all | bytes 2162688 | tf_op jit(solution)/shard_map/all_to_all | solution.py:257
  61.2 0.9 middle.1
  62.1 13.0 %collective-permute-start.5 = (s16[272,256]{1,0:T(8,128)(2,1)S(1)}, s16[272,256]{1,0:T(8,128)(2,1)S(1)}, u32[]{:S(2)}, u32[]{:S(2)}) collective-permute-start(s16[272,256]{1,0:T(8,128)(2,1)S(1)} %get-tuple-element.9), channel_id=1, source_target_pairs={{0,0},{1,6},{2,34},{3,36},{4,68},{5,64},{6,102},{7,98},{8,8},{9,14... | collective-permute-start | bytes 417800 | tf_op jit(solution)/shard_map/ppermute | solution.py:275
  75.1 4.1 %collective-permute-start.6 = (s16[272,256]{1,0:T(8,128)(2,1)S(1)}, s16[272,256]{1,0:T(8,128)(2,1)S(1)}, u32[]{:S(2)}, u32[]{:S(2)}) collective-permute-start(s16[272,256]{1,0:T(8,128)(2,1)S(1)} %get-tuple-element.10), channel_id=1, source_target_pairs={{0,2},{1,96},{2,32},{3,66},{4,70},{5,4},{6,100},{7,38},{8,10},{9,2... | collective-permute-start | bytes 417800 | tf_op jit(solution)/shard_map/ppermute | solution.py:275
  79.2 3.9 %collective-permute-done.5.a_ref = s16[272,256]{1,0:T(8,128)(2,1)S(1)} collective-permute-done((s16[272,256]{1,0:T(8,128)(2,1)S(1)}, s16[272,256]{1,0:T(8,128)(2,1)S(1)}, u32[]{:S(2)}, u32[]{:S(2)}) %collective-permute-start.5) | collective-permute-done | bytes 139296 | tf_op jit(solution)/shard_map/ppermute | solution.py:275
  83.1 15.4 %collective-permute-done.6.b_ref = s16[272,256]{1,0:T(8,128)(2,1)S(1)} collective-permute-done((s16[272,256]{1,0:T(8,128)(2,1)S(1)}, s16[272,256]{1,0:T(8,128)(2,1)S(1)}, u32[]{:S(2)}, u32[]{:S(2)}) %collective-permute-start.6) | collective-permute-done | bytes 139296 | tf_op jit(solution)/shard_map/ppermute | solution.py:275
  98.5 0.6 join.1
  99.1 1.9 %collective-permute-start.7 = (f32[128,256]{1,0:T(8,128)S(1)}, f32[128,256]{1,0:T(8,128)S(1)}, u32[]{:S(2)}, u32[]{:S(2)}) collective-permute-start(f32[128,256]{1,0:T(8,128)S(1)} %get-tuple-element.12), channel_id=1, source_target_pairs={{0,1},{1,0},{2,3},{3,2},{4,5},{5,4},{6,7},{7,6},{8,9},{9,8},{10,11... | collective-permute-start | bytes 393224 | tf_op jit(solution)/shard_map/ppermute | solution.py:220
  101.0 1.3 %collective-permute-done.7.come_ref = f32[128,256]{1,0:T(8,128)S(1)} collective-permute-done((f32[128,256]{1,0:T(8,128)S(1)}, f32[128,256]{1,0:T(8,128)S(1)}, u32[]{:S(2)}, u32[]{:S(2)}) %collective-permute-start.7) | collective-permute-done | bytes 131104 | tf_op jit(solution)/shard_map/ppermute | solution.py:220
  102.3 0.7 last.1
  (1 shorter events, 0.0 us)
Async XLA Ops:
  0.0 1.0 copy-start
  1.0 0.9 copy-start.1
  1.9 0.7 copy-start.2
  2.6 0.7 copy-start.3
  7.3 21.5 %collective-permute-start.3 = (bf16[2,784,256]{2,1,0:T(8,128)(2,1)S(1)}, bf16[2,784,256]{2,1,0:T(8,128)(2,1)S(1)}, u32[]{:S(2)}, u32[]{:S(2)}) collective-permute-start(bf16[2,784,256]{2,1,0:T(8,128)(2,1)S(1)} %bitcast.5), channel_id=1, source_target_pairs={{6,0},{4,2},{0,4},{2,6},{3,1},{1,3},{7,5},{5,7},{14,8},{12,10},{8,... | collective-permute-start | bytes 2408456 | tf_op jit(solution)/shard_map/ppermute | solution.py:223
  10.8 20.2 %collective-permute-start = (bf16[784,256]{1,0:T(8,128)(2,1)S(1)}, bf16[784,256]{1,0:T(8,128)(2,1)S(1)}, u32[]{:S(2)}, u32[]{:S(2)}) collective-permute-start(bf16[784,256]{1,0:T(8,128)(2,1)S(1)} %contract.1.refs_0_), channel_id=1, source_target_pairs={{16,0},{24,8},{0,16},{8,24},{17,1},{25,9},{1,17},{9,25},{18,2},{26... | collective-permute-start | bytes 1204232 | tf_op jit(solution)/shard_map/ppermute | solution.py:228
  12.8 19.7 %collective-permute-start.1 = (bf16[784,256]{1,0:T(8,128)(2,1)S(1)}, bf16[784,256]{1,0:T(8,128)(2,1)S(1)}, u32[]{:S(2)}, u32[]{:S(2)}) collective-permute-start(bf16[784,256]{1,0:T(8,128)(2,1)S(1)} %contract.1.refs_0_), channel_id=1, source_target_pairs={{8,0},{16,8},{24,16},{0,24},{9,1},{17,9},{25,17},{1,25},{10,2},{18... | collective-permute-start | bytes 1204232 | tf_op jit(solution)/shard_map/ppermute | solution.py:228
  16.8 16.6 %collective-permute-start.2 = (bf16[784,256]{1,0:T(8,128)(2,1)S(1)}, bf16[784,256]{1,0:T(8,128)(2,1)S(1)}, u32[]{:S(2)}, u32[]{:S(2)}) collective-permute-start(bf16[784,256]{1,0:T(8,128)(2,1)S(1)} %contract.1.refs_0_), channel_id=1, source_target_pairs={{24,0},{0,8},{8,16},{16,24},{25,1},{1,9},{9,17},{17,25},{26,2},{2,... | collective-permute-start | bytes 1204232 | tf_op jit(solution)/shard_map/ppermute | solution.py:228
  28.7 6.4 %collective-permute-start.4 = (bf16[2,784,256]{2,1,0:T(8,128)(2,1)S(1)}, bf16[2,784,256]{2,1,0:T(8,128)(2,1)S(1)}, u32[]{:S(2)}, u32[]{:S(2)}) collective-permute-start(bf16[2,784,256]{2,1,0:T(8,128)(2,1)S(1)} %collective-permute-done.3.refs_2_), channel_id=1, source_target_pairs={{0,1},{1,0},{2,3},{3,2},{4,5},{5,4},{6,7},{7,6},{8,9},{9,8},{10,11... | collective-permute-start | bytes 2408456 | tf_op jit(solution)/shard_map/ppermute | solution.py:220
  62.1 21.0 %collective-permute-start.5 = (s16[272,256]{1,0:T(8,128)(2,1)S(1)}, s16[272,256]{1,0:T(8,128)(2,1)S(1)}, u32[]{:S(2)}, u32[]{:S(2)}) collective-permute-start(s16[272,256]{1,0:T(8,128)(2,1)S(1)} %get-tuple-element.9), channel_id=1, source_target_pairs={{0,0},{1,6},{2,34},{3,36},{4,68},{5,64},{6,102},{7,98},{8,8},{9,14... | collective-permute-start | bytes 417800 | tf_op jit(solution)/shard_map/ppermute | solution.py:275
  75.1 23.3 %collective-permute-start.6 = (s16[272,256]{1,0:T(8,128)(2,1)S(1)}, s16[272,256]{1,0:T(8,128)(2,1)S(1)}, u32[]{:S(2)}, u32[]{:S(2)}) collective-permute-start(s16[272,256]{1,0:T(8,128)(2,1)S(1)} %get-tuple-element.10), channel_id=1, source_target_pairs={{0,2},{1,96},{2,32},{3,66},{4,70},{5,4},{6,100},{7,38},{8,10},{9,2... | collective-permute-start | bytes 417800 | tf_op jit(solution)/shard_map/ppermute | solution.py:275
  99.1 3.2 %collective-permute-start.7 = (f32[128,256]{1,0:T(8,128)S(1)}, f32[128,256]{1,0:T(8,128)S(1)}, u32[]{:S(2)}, u32[]{:S(2)}) collective-permute-start(f32[128,256]{1,0:T(8,128)S(1)} %get-tuple-element.12), channel_id=1, source_target_pairs={{0,1},{1,0},{2,3},{3,2},{4,5},{5,4},{6,7},{7,6},{8,9},{9,8},{10,11... | collective-permute-start | bytes 393224 | tf_op jit(solution)/shard_map/ppermute | solution.py:220

commit v5 on v4

--- a/solution.py
+++ b/solution.py
@@ -107,32 +107,35 @@
         scatter(column[i], ids, i, out_ref, lax.rem(place_ref[0] + d, 4) * HALF)
 
 
-def pairs_kernel(place_ref, *refs):
-    cols, *wide = refs[:4]
-    out_ref, rows, ids_vmem, ids, sem = refs[4:]
-    core = place_ref[1]
-    halves = [src.at[k] for src in wide for k in range(2)]
+def rows_kernel(src, out_ref, ids_vmem, ids, sem):
+    halves = [src.at[k] for k in range(2)]
     copy = load_ids(halves, ids_vmem, ids, sem)
     copy.start()
-    rows[...] = jnp.zeros_like(rows)
+    out_ref[...] = jnp.zeros_like(out_ref)
     copy.wait()
-    for i, t in enumerate((0, 2 - core, 1 + core)):
-        for k in range(2):
-            scatter(halves[i * 2 + k], ids, i * 2 + k, rows, t * CHIP + k * HALF)
+    for k in range(2):
+        scatter(halves[k], ids, k, out_ref, k * HALF)
+
+
+def pairs_kernel(place_ref, cols, own_rows, first_rows, src, out_ref, rows, ids_vmem, ids, sem):
+    core = place_ref[1]
+    rows_kernel(src, rows, ids_vmem, ids, sem)
     exponents = {}
-    for t in range(TYPES):
-        part = lax.dot_general(
-            rows[t * CHIP : (t + 1) * CHIP, :], cols[...], NT, preferred_element_type=jnp.float32
-        )
+    places = ((0, 0), (1 - core, core * CHIP), (core, (1 - core) * CHIP))
+    for t, block in enumerate((own_rows, first_rows, rows)):
+        part = lax.dot_general(block[...], cols[...], NT, preferred_element_type=jnp.float32)
+        chunk, first = places[t]
         for i in range(4):
             coded, exponents[t, i] = encode(part[:, i * HALF : (i + 1) * HALF])
-            chunk, first = i * 2 + t // 2, (t % 2) * CHIP
-            out_ref[chunk, first : first + CHIP, :] = coded
+            at = pl.ds(first if t == 0 else pl.multiple_of(first, CHIP), CHIP)
+            out_ref[i * 2 + chunk, at, :] = coded
+    zero = core == 0
     for i in range(4):
         out_ref[i * 2 + 1, CHIP : 2 * CHIP, :] = jnp.zeros((CHIP, HALF), jnp.int16)
-        for k in range(2):
-            block = pick_rows([exponents[k * 2, i], exponents[1, i]], HALF)
-            out_ref[i * 2 + k, 2 * CHIP :, :] = block.astype(jnp.int16)
+        near = jnp.where(zero, exponents[2, i], exponents[1, i])
+        across = jnp.where(zero, exponents[1, i], exponents[2, i])
+        out_ref[i * 2, 2 * CHIP :, :] = pick_rows([exponents[0, i], near], HALF).astype(jnp.int16)
+        out_ref[i * 2 + 1, 2 * CHIP :, :] = pick_rows([across], HALF).astype(jnp.int16)
 
 
 def middle_kernel(place_ref, in_ref, even_ref, odd_ref):
@@ -212,7 +215,7 @@
             pltpu.VMEM((AUX, AUX), jnp.bfloat16),
             pltpu.SemaphoreType.DMA((2,)),
         ],
-        compiler_params=params(24),
+        compiler_params=params(56),
         name="contract",
     )(raw_blocks, metric_factor, sig_list, live_count.reshape(RB))
 
@@ -226,16 +229,31 @@
         [(CROSS[i] * 2, i * 2) for i in range(4)] + [((i ^ 1) * 2 + 1, i * 2 + 1) for i in range(4)],
     )
     column = [own] + [lax.ppermute(own, "y", [((i + d) % 4, i) for i in range(4)]) for d in (2, 1, 3)]
+    def ids_scratch(count):
+        return [
+            pltpu.VMEM((count, 8, 128), jnp.int32),
+            pltpu.SMEM((count, 8, 128), jnp.int32),
+            pltpu.SemaphoreType.DMA,
+        ]
+
+    def dense_rows(block):
+        return pl.pallas_call(
+            rows_kernel,
+            out_shape=jax.ShapeDtypeStruct((CHIP, NOB * AUX), jnp.bfloat16),
+            in_specs=[VMEM],
+            out_specs=VMEM,
+            scratch_shapes=ids_scratch(2),
+            compiler_params=params(16),
+            cost_estimate=pl.CostEstimate(flops=1_000_000_000, bytes_accessed=3_000_000, transcendentals=0),
+            name="rows",
+        )(block)
+
     dense = pl.pallas_call(
         column_kernel,
         out_shape=jax.ShapeDtypeStruct((4 * HALF, NOB * AUX), jnp.bfloat16),
         in_specs=[SMEM] + [VMEM] * 4,
         out_specs=VMEM,
-        scratch_shapes=[
-            pltpu.VMEM((4, 8, 128), jnp.int32),
-            pltpu.SMEM((4, 8, 128), jnp.int32),
-            pltpu.SemaphoreType.DMA,
-        ],
+        scratch_shapes=ids_scratch(4),
         compiler_params=params(16),
         cost_estimate=pl.CostEstimate(flops=20_000_000_000, bytes_accessed=6_000_000, transcendentals=0),
         name="column",
@@ -245,15 +263,10 @@
         out_shape=jax.ShapeDtypeStruct((8, CHUNK, HALF), jnp.int16),
         in_specs=[SMEM] + [VMEM] * 4,
         out_specs=VMEM,
-        scratch_shapes=[
-            pltpu.VMEM((TYPES * CHIP, NOB * AUX), jnp.bfloat16),
-            pltpu.VMEM((6, 8, 128), jnp.int32),
-            pltpu.SMEM((6, 8, 128), jnp.int32),
-            pltpu.SemaphoreType.DMA,
-        ],
-        compiler_params=params(24),
+        scratch_shapes=[pltpu.VMEM((CHIP, NOB * AUX), jnp.bfloat16)] + ids_scratch(2),
+        compiler_params=params(16),
         name="pairs",
-    )(place, dense, both, along, swap(along))
+    )(place, dense, dense_rows(both), dense_rows(along), swap(along))
     arrived = lax.all_to_all(tiles, ("x", "c"), 0, 0, tiled=True)
     wide = jax.ShapeDtypeStruct((WIDE, CHIP), jnp.int16)
     messages = pl.pallas_call(

time: 103 us -> 103 us (level)
  local copies, waits for them, and re-layouts: 3.23 us -> 0.01 us
  Pallas kernels: 10.9 us -> 13.6 us
    unnamed x8 -> x2, local copies, waits for them, and re-layouts: 3.23 us -> 0.01 us
    pallas_call x0 -> x2, Pallas kernels: none -> 1.77 us  [dense_rows(): pl.pallas_call(rows_kernel, out_shape=jax.ShapeDtypeStruct((CHIP, NOB * A...]
    pallas_call x1, Pallas kernels: 1.33 us -> 2.91 us  [shards(): pl.pallas_call(contract_kernel, out_shape=jax.ShapeDtypeStruct((PAY, AUX)...]
  transfers between devices with their start and end apart: 8 -> 8, of which waited for: 6 -> 6; matrix products, arithmetic and copies ran while one was open for 0% -> 0% of each run, Pallas kernels for 2% -> 3%
where the time goes in v5:
time: 103 us; the launch traced here: 102 us
  starting transfers between devices  32.8 us (32%)
  waiting for transfers between devices  32.2 us (31%)
  blocking collectives  23.3 us (23%)
  Pallas kernels  13.6 us (13%)
    all_to_all x1, blocking collectives, shards(): arrived = lax.all_to_all(tiles, ('x', 'c'), 0, 0, tiled=True)  20.4 us
    ppermute x2, waiting for transfers between devices, shards(): lax.ppermute(a, AXES, far_round(r))  19.3 us
    ppermute x2, starting transfers between devices, shards(): lax.ppermute(a, AXES, far_round(r))  17.1 us
    ppermute x1, waiting for transfers between devices, shards(): lax.ppermute(both, ('zl', 'c'), [(CROSS[i] * 2, i * 2) for i in range(4)]...  9.03 us
    ppermute x3, starting transfers between devices, shards(): lax.ppermute(own, 'y', [((i + d) % 4, i) for i in range(4)])  7.92 us
    pallas_call x1, Pallas kernels, shards(): pl.pallas_call(pairs_kernel, out_shape=jax.ShapeDtypeStruct((8, CHUNK, HA...  5 us
    ppermute x2, starting transfers between devices, swap(): return lax.ppermute(a, 'c', [(0, 1), (1, 0)])  4.16 us
    ppermute x1, starting transfers between devices, shards(): lax.ppermute(both, ('zl', 'c'), [(CROSS[i] * 2, i * 2) for i in range(4)]...  3.67 us
  transfers between devices with their start and end apart: 8, of which 6 were waited for; matrix products, arithmetic and copies ran while one was open for 0% of the time, Pallas kernels for 3%

profile of v5, /device:TPU:81, one launch (start us, length us, event | category | flops | bytes accessed | tf_op | source)
XLA Modules:
  0.0 102.2 jit_solution(13665858822820483222)
XLA Ops:
  0.0 2.9 %contract.1.refs_0_ = bf16[784,256]{1,0:T(8,128)(2,1)} custom-call(bf16[2,6,64,256]{3,2,1,0:T(8,128)(2,1)} %raw_hbm.1, bf16[256,256]{1,0:T(8,128)(2,1)} %metric_hbm.1, s32[2,6]{1,0:T(2,128)} %sig_ref.1, s32[2]{0:T(128)} %bitcast.7), custom_call_target="tpu_custom_call" | custom-call | tf_op jit(solution)/shard_map/contract/pallas_call | solution.py:208
  2.9 2.9 %all-gather = bf16[1568,256]{1,0:T(8,128)(2,1)S(1)} all-gather(bf16[784,256]{1,0:T(8,128)(2,1)} %contract.1.refs_0_), channel_id=2, replica_groups=mesh['x'=4,'zh'=4,'y'=4,'zl'=4,'c'=2] {'c'}, dimensions={0}, use_global_device_ids=true | all-gather | bytes 1204224 | tf_op jit(solution)/shard_map/all_gather | solution.py:225
  5.8 0.0 copy-start
  5.8 3.7 %collective-permute-start.3 = (bf16[2,784,256]{2,1,0:T(8,128)(2,1)S(1)}, bf16[2,784,256]{2,1,0:T(8,128)(2,1)S(1)}, u32[]{:S(2)}, u32[]{:S(2)}) collective-permute-start(bf16[2,784,256]{2,1,0:T(8,128)(2,1)S(1)} %bitcast.5), channel_id=1, source_target_pairs={{6,0},{4,2},{0,4},{2,6},{3,1},{1,3},{7,5},{5,7},{14,8},{12,10},{8,... | collective-permute-start | bytes 2408456 | tf_op jit(solution)/shard_map/ppermute | solution.py:226
  9.5 2.0 %collective-permute-start = (bf16[784,256]{1,0:T(8,128)(2,1)}, bf16[784,256]{1,0:T(8,128)(2,1)S(1)}, u32[]{:S(2)}, u32[]{:S(2)}) collective-permute-start(bf16[784,256]{1,0:T(8,128)(2,1)} %contract.1.refs_0_), channel_id=1, source_target_pairs={{16,0},{24,8},{0,16},{8,24},{17,1},{25,9},{1,17},{9,25},{18,2},{26... | collective-permute-start | bytes 1204232 | tf_op jit(solution)/shard_map/ppermute | solution.py:231
  11.5 4.0 %collective-permute-start.1 = (bf16[784,256]{1,0:T(8,128)(2,1)}, bf16[784,256]{1,0:T(8,128)(2,1)S(1)}, u32[]{:S(2)}, u32[]{:S(2)}) collective-permute-start(bf16[784,256]{1,0:T(8,128)(2,1)} %contract.1.refs_0_), channel_id=1, source_target_pairs={{8,0},{16,8},{24,16},{0,24},{9,1},{17,9},{25,17},{1,25},{10,2},{18... | collective-permute-start | bytes 1204232 | tf_op jit(solution)/shard_map/ppermute | solution.py:231
  15.5 1.9 %collective-permute-start.2 = (bf16[784,256]{1,0:T(8,128)(2,1)}, bf16[784,256]{1,0:T(8,128)(2,1)S(1)}, u32[]{:S(2)}, u32[]{:S(2)}) collective-permute-start(bf16[784,256]{1,0:T(8,128)(2,1)} %contract.1.refs_0_), channel_id=1, source_target_pairs={{24,0},{0,8},{8,16},{16,24},{25,1},{1,9},{9,17},{17,25},{26,2},{2,... | collective-permute-start | bytes 1204232 | tf_op jit(solution)/shard_map/ppermute | solution.py:231
  17.4 0.9 rows.2.own_rows
  18.3 0.1 pad_add_fusion.place_ref
  18.4 9.0 %collective-permute-done.3.src = bf16[2,784,256]{2,1,0:T(8,128)(2,1)S(1)} collective-permute-done((bf16[2,784,256]{2,1,0:T(8,128)(2,1)S(1)}, bf16[2,784,256]{2,1,0:T(8,128)(2,1)S(1)}, u32[]{:S(2)}, u32[]{:S(2)}) %collective-permute-start.3) | collective-permute-done | bytes 802848 | tf_op jit(solution)/shard_map/ppermute | solution.py:226
  27.4 2.2 %collective-permute-start.4 = (bf16[2,784,256]{2,1,0:T(8,128)(2,1)S(1)}, bf16[2,784,256]{2,1,0:T(8,128)(2,1)S(1)}, u32[]{:S(2)}, u32[]{:S(2)}) collective-permute-start(bf16[2,784,256]{2,1,0:T(8,128)(2,1)S(1)} %collective-permute-done.3.src), channel_id=1, source_target_pairs={{0,1},{1,0},{2,3},{3,2},{4,5},{5,4},{6,7},{7,6},{8,9},{9,8},{10,11... | collective-permute-start | bytes 2408456 | tf_op jit(solution)/shard_map/ppermute | solution.py:223
  29.7 0.0 collective-permute-done.refs_1_
  29.7 1.6 %collective-permute-done.1.refs_2_ = bf16[784,256]{1,0:T(8,128)(2,1)S(1)} collective-permute-done((bf16[784,256]{1,0:T(8,128)(2,1)}, bf16[784,256]{1,0:T(8,128)(2,1)S(1)}, u32[]{:S(2)}, u32[]{:S(2)}) %collective-permute-start.1) | collective-permute-done | bytes 401440 | tf_op jit(solution)/shard_map/ppermute | solution.py:231
  31.3 1.0 collective-permute-done.2.refs_3_
  32.3 0.0 copy-done
  32.3 1.8 %column.1.cols = bf16[512,4096]{1,0:T(8,128)(2,1)S(1)} custom-call(s32[3]{0:T(128)S(1)} %pad_add_fusion.place_ref, bf16[784,256]{1,0:T(8,128)(2,1)S(1)} %copy-done, bf16[784,256]{1,0:T(8,128)(2,1)S(1)} %collective-permute-done.refs_1_, bf16[784,256]{1,0:T(8,128)(2,1)S(1)} %collective-permute-done.1.refs_2_, bf16[784,256]{1,0:T(8,128)(2,1)S(1)} %collective-permute-done.2.refs_3_), custom_call_target="tpu_custom_call" | custom-call | flops 20000000000 | bytes 6000000 | tf_op jit(solution)/shard_map/column/pallas_call | solution.py:251
  34.1 0.9 rows.3.first_rows
  35.0 0.0 collective-permute-done.4.src
  35.0 5.0 %pairs.1 = s16[8,528,128]{2,1,0:T(8,128)(2,1)S(1)} custom-call(s32[3]{0:T(128)S(1)} %pad_add_fusion.place_ref, bf16[512,4096]{1,0:T(8,128)(2,1)S(1)} %column.1.cols, bf16[256,4096]{1,0:T(8,128)(2,1)S(1)} %rows.2.own_rows, bf16[256,4096]{1,0:T(8,128)(2,1)S(1)} %rows.3.first_rows, bf16[2,784,256]{2,1,0:T(8,128)(2,1)S(1)} %collective-permute-done.4.src), custom_call_target="tpu_custom_call" | custom-call | tf_op jit(solution)/shard_map/pairs/pallas_call | solution.py:261
  40.0 20.4 %all_to_all.5.in_ref = s16[8,528,128]{2,1,0:T(8,128)(2,1)S(1)} all-to-all(s16[8,528,128]{2,1,0:T(8,128)(2,1)S(1)} %pairs.1), channel_id=1, replica_groups=mesh['x'=4,'zh'=4,'y'=4,'zl'=4,'c'=2] {'x','c'}, dimensions={0} | all-to-all | bytes 2162688 | tf_op jit(solution)/shard_map/all_to_all | solution.py:270
  60.4 0.9 middle.1
  61.3 13.0 %collective-permute-start.5 = (s16[272,256]{1,0:T(8,128)(2,1)S(1)}, s16[272,256]{1,0:T(8,128)(2,1)S(1)}, u32[]{:S(2)}, u32[]{:S(2)}) collective-permute-start(s16[272,256]{1,0:T(8,128)(2,1)S(1)} %get-tuple-element.9), channel_id=1, source_target_pairs={{0,0},{1,6},{2,34},{3,36},{4,68},{5,64},{6,102},{7,98},{8,8},{9,14... | collective-permute-start | bytes 417800 | tf_op jit(solution)/shard_map/ppermute | solution.py:288
  74.3 4.1 %collective-permute-start.6 = (s16[272,256]{1,0:T(8,128)(2,1)S(1)}, s16[272,256]{1,0:T(8,128)(2,1)S(1)}, u32[]{:S(2)}, u32[]{:S(2)}) collective-permute-start(s16[272,256]{1,0:T(8,128)(2,1)S(1)} %get-tuple-element.10), channel_id=1, source_target_pairs={{0,2},{1,96},{2,32},{3,66},{4,70},{5,4},{6,100},{7,38},{8,10},{9,2... | collective-permute-start | bytes 417800 | tf_op jit(solution)/shard_map/ppermute | solution.py:288
  78.4 3.9 %collective-permute-done.5.a_ref = s16[272,256]{1,0:T(8,128)(2,1)S(1)} collective-permute-done((s16[272,256]{1,0:T(8,128)(2,1)S(1)}, s16[272,256]{1,0:T(8,128)(2,1)S(1)}, u32[]{:S(2)}, u32[]{:S(2)}) %collective-permute-start.5) | collective-permute-done | bytes 139296 | tf_op jit(solution)/shard_map/ppermute | solution.py:288
  82.2 15.4 %collective-permute-done.6.b_ref = s16[272,256]{1,0:T(8,128)(2,1)S(1)} collective-permute-done((s16[272,256]{1,0:T(8,128)(2,1)S(1)}, s16[272,256]{1,0:T(8,128)(2,1)S(1)}, u32[]{:S(2)}, u32[]{:S(2)}) %collective-permute-start.6) | collective-permute-done | bytes 139296 | tf_op jit(solution)/shard_map/ppermute | solution.py:288
  97.7 0.6 join.1
  98.3 1.9 %collective-permute-start.7 = (f32[128,256]{1,0:T(8,128)S(1)}, f32[128,256]{1,0:T(8,128)S(1)}, u32[]{:S(2)}, u32[]{:S(2)}) collective-permute-start(f32[128,256]{1,0:T(8,128)S(1)} %get-tuple-element.12), channel_id=1, source_target_pairs={{0,1},{1,0},{2,3},{3,2},{4,5},{5,4},{6,7},{7,6},{8,9},{9,8},{10,11... | collective-permute-start | bytes 393224 | tf_op jit(solution)/shard_map/ppermute | solution.py:223
  100.2 1.3 %collective-permute-done.7.come_ref = f32[128,256]{1,0:T(8,128)S(1)} collective-permute-done((f32[128,256]{1,0:T(8,128)S(1)}, f32[128,256]{1,0:T(8,128)S(1)}, u32[]{:S(2)}, u32[]{:S(2)}) %collective-permute-start.7) | collective-permute-done | bytes 131104 | tf_op jit(solution)/shard_map/ppermute | solution.py:223
  101.5 0.7 last.1
Async XLA Ops:
  5.8 26.5 %copy-start = (bf16[784,256]{1,0:T(8,128)(2,1)S(1)}, bf16[784,256]{1,0:T(8,128)(2,1)}, u32[]{:S(2)}) copy-start(bf16[784,256]{1,0:T(8,128)(2,1)} %contract.1.refs_0_) | copy-start | bytes 1204228
  5.8 21.6 %collective-permute-start.3 = (bf16[2,784,256]{2,1,0:T(8,128)(2,1)S(1)}, bf16[2,784,256]{2,1,0:T(8,128)(2,1)S(1)}, u32[]{:S(2)}, u32[]{:S(2)}) collective-permute-start(bf16[2,784,256]{2,1,0:T(8,128)(2,1)S(1)} %bitcast.5), channel_id=1, source_target_pairs={{6,0},{4,2},{0,4},{2,6},{3,1},{1,3},{7,5},{5,7},{14,8},{12,10},{8,... | collective-permute-start | bytes 2408456 | tf_op jit(solution)/shard_map/ppermute | solution.py:226
  9.5 20.2 %collective-permute-start = (bf16[784,256]{1,0:T(8,128)(2,1)}, bf16[784,256]{1,0:T(8,128)(2,1)S(1)}, u32[]{:S(2)}, u32[]{:S(2)}) collective-permute-start(bf16[784,256]{1,0:T(8,128)(2,1)} %contract.1.refs_0_), channel_id=1, source_target_pairs={{16,0},{24,8},{0,16},{8,24},{17,1},{25,9},{1,17},{9,25},{18,2},{26... | collective-permute-start | bytes 1204232 | tf_op jit(solution)/shard_map/ppermute | solution.py:231
  11.5 19.9 %collective-permute-start.1 = (bf16[784,256]{1,0:T(8,128)(2,1)}, bf16[784,256]{1,0:T(8,128)(2,1)S(1)}, u32[]{:S(2)}, u32[]{:S(2)}) collective-permute-start(bf16[784,256]{1,0:T(8,128)(2,1)} %contract.1.refs_0_), channel_id=1, source_target_pairs={{8,0},{16,8},{24,16},{0,24},{9,1},{17,9},{25,17},{1,25},{10,2},{18... | collective-permute-start | bytes 1204232 | tf_op jit(solution)/shard_map/ppermute | solution.py:231
  15.5 16.8 %collective-permute-start.2 = (bf16[784,256]{1,0:T(8,128)(2,1)}, bf16[784,256]{1,0:T(8,128)(2,1)S(1)}, u32[]{:S(2)}, u32[]{:S(2)}) collective-permute-start(bf16[784,256]{1,0:T(8,128)(2,1)} %contract.1.refs_0_), channel_id=1, source_target_pairs={{24,0},{0,8},{8,16},{16,24},{25,1},{1,9},{9,17},{17,25},{26,2},{2,... | collective-permute-start | bytes 1204232 | tf_op jit(solution)/shard_map/ppermute | solution.py:231
  27.4 7.6 %collective-permute-start.4 = (bf16[2,784,256]{2,1,0:T(8,128)(2,1)S(1)}, bf16[2,784,256]{2,1,0:T(8,128)(2,1)S(1)}, u32[]{:S(2)}, u32[]{:S(2)}) collective-permute-start(bf16[2,784,256]{2,1,0:T(8,128)(2,1)S(1)} %collective-permute-done.3.src), channel_id=1, source_target_pairs={{0,1},{1,0},{2,3},{3,2},{4,5},{5,4},{6,7},{7,6},{8,9},{9,8},{10,11... | collective-permute-start | bytes 2408456 | tf_op jit(solution)/shard_map/ppermute | solution.py:223
  61.3 20.9 %collective-permute-start.5 = (s16[272,256]{1,0:T(8,128)(2,1)S(1)}, s16[272,256]{1,0:T(8,128)(2,1)S(1)}, u32[]{:S(2)}, u32[]{:S(2)}) collective-permute-start(s16[272,256]{1,0:T(8,128)(2,1)S(1)} %get-tuple-element.9), channel_id=1, source_target_pairs={{0,0},{1,6},{2,34},{3,36},{4,68},{5,64},{6,102},{7,98},{8,8},{9,14... | collective-permute-start | bytes 417800 | tf_op jit(solution)/shard_map/ppermute | solution.py:288
  74.3 23.4 %collective-permute-start.6 = (s16[272,256]{1,0:T(8,128)(2,1)S(1)}, s16[272,256]{1,0:T(8,128)(2,1)S(1)}, u32[]{:S(2)}, u32[]{:S(2)}) collective-permute-start(s16[272,256]{1,0:T(8,128)(2,1)S(1)} %get-tuple-element.10), channel_id=1, source_target_pairs={{0,2},{1,96},{2,32},{3,66},{4,70},{5,4},{6,100},{7,38},{8,10},{9,2... | collective-permute-start | bytes 417800 | tf_op jit(solution)/shard_map/ppermute | solution.py:288
  98.3 3.2 %collective-permute-start.7 = (f32[128,256]{1,0:T(8,128)S(1)}, f32[128,256]{1,0:T(8,128)S(1)}, u32[]{:S(2)}, u32[]{:S(2)}) collective-permute-start(f32[128,256]{1,0:T(8,128)S(1)} %get-tuple-element.12), channel_id=1, source_target_pairs={{0,1},{1,0},{2,3},{3,2},{4,5},{5,4},{6,7},{7,6},{8,9},{9,8},{10,11... | collective-permute-start | bytes 393224 | tf_op jit(solution)/shard_map/ppermute | solution.py:223

commit v6 on v5

--- a/solution.py
+++ b/solution.py
@@ -170,17 +170,36 @@
         write(odd_ref, first)
 
 
-def join_kernel(place_ref, a_ref, b_ref, keep_ref, send_ref):
+def join_kernel(place_ref, a_ref, b_ref, keep_ref, mirror_ref, send_ref):
     core = place_ref[1]
-    for ref, half in ((keep_ref, core), (send_ref, 1 - core)):
+    for half, ref in ((core, mirror_ref), (1 - core, send_ref)):
         rows = pl.ds(pl.multiple_of(half * HALF, HALF), HALF)
-        ref[...] = sum(
+        total = sum(
             decode(src[rows, :], src[CHIP:, :].astype(jnp.int32), 0) for src in (a_ref, b_ref)
         )
-
-
-def last_kernel(keep_ref, come_ref, out_ref):
-    out_ref[...] = 0.25 * (keep_ref[...] + come_ref[...])
+        if ref is mirror_ref:
+            keep_ref[...] = total
+        coded, exponent = encode(total)
+        ref[:HALF, :] = coded
+        ref[HALF:, :] = jnp.broadcast_to(exponent, (16, CHIP)).astype(jnp.int16)
+
+
+def cross(z):
+    return jnp.where(z < 2, 3 - z, z - 2)
+
+
+def last_kernel(place_ref, keep_ref, mirror_ref, come_ref, out_ref):
+    come = decode(come_ref[:HALF, :], come_ref[HALF:, :].astype(jnp.int32), 0)
+    mirrored = place_ref[2] == cross(place_ref[3])
+
+    @pl.when(mirrored)
+    def _():
+        kept = decode(mirror_ref[:HALF, :], mirror_ref[HALF:, :].astype(jnp.int32), 0)
+        out_ref[...] = 0.25 * (kept + come)
+
+    @pl.when(jnp.logical_not(mirrored))
+    def _():
+        out_ref[...] = 0.25 * (keep_ref[...] + come)
 
 
 def index_of(x, zh, y, zl, c):
@@ -195,7 +214,7 @@
                 for z in range(4):
                     kinds = (
                         ((x, z, y, z), (x, z, y, z ^ 1)),
-                        ((x, z, y, CROSS[z]), (y, CROSS[z], x, z)),
+                        ((x, z, y, CROSS[z]), (x, CROSS[z], y, z)),
                     )
                     for c in range(2):
                         dest = kinds[c][(s + r) % 2]
@@ -203,8 +222,24 @@
     return pairs
 
 
+def home_round(swap_cores):
+    pairs = []
+    for x in range(4):
+        for zh in range(4):
+            for y in range(4):
+                for z in range(4):
+                    mirrored = zh == CROSS[z]
+                    if not (mirrored or swap_cores):
+                        continue
+                    dest = (y, zh, x, z) if mirrored else (x, zh, y, z)
+                    for c in range(2):
+                        pairs.append((index_of(x, zh, y, z, c), index_of(*dest, c ^ swap_cores)))
+    return pairs
+
+
 def shards(raw_blocks, metric_factor, sig_list, live_count):
-    place = jnp.stack([lax.axis_index("y"), lax.axis_index("c"), lax.axis_index("zh")]).astype(jnp.int32)
+    place = jnp.stack([lax.axis_index("y"), lax.axis_index("c"), lax.axis_index("zh"), lax.axis_index("zl")])
+    place = place.astype(jnp.int32)
     own = pl.pallas_call(
         contract_kernel,
         out_shape=jax.ShapeDtypeStruct((PAY, AUX), jnp.bfloat16),
@@ -278,22 +313,23 @@
         name="middle",
     )(place, arrived)
     half = jax.ShapeDtypeStruct((HALF, CHIP), jnp.float32)
-    keep, send = pl.pallas_call(
+    tile = jax.ShapeDtypeStruct((TILE, CHIP), jnp.int16)
+    keep, mirror, send = pl.pallas_call(
         join_kernel,
-        out_shape=[half] * 2,
+        out_shape=[half, tile, tile],
         in_specs=[SMEM, VMEM, VMEM],
-        out_specs=[VMEM] * 2,
+        out_specs=[VMEM] * 3,
         compiler_params=params(16),
         name="join",
     )(place, *[lax.ppermute(a, AXES, far_round(r)) for r, a in enumerate(messages)])
     return pl.pallas_call(
         last_kernel,
         out_shape=half,
-        in_specs=[VMEM] * 2,
+        in_specs=[SMEM] + [VMEM] * 3,
         out_specs=VMEM,
         compiler_params=params(16),
         name="last",
-    )(keep, swap(send))
+    )(place, keep, lax.ppermute(mirror, AXES, home_round(0)), lax.ppermute(send, AXES, home_round(1)))
 
 
 def solution(mesh):

time: 103 us -> 106 us (1.029)
  the two profiles are of different devices: /device:TPU:81 before, /device:TPU:69 now
where the time goes in v6:
time: 106 us; the launch traced here: 105 us
  starting transfers between devices  40.9 us (39%)
  waiting for transfers between devices  28.8 us (27%)
  blocking collectives  21.1 us (20%)
  Pallas kernels  14.3 us (13%)
    all_to_all x1, blocking collectives, shards(): arrived = lax.all_to_all(tiles, ('x', 'c'), 0, 0, tiled=True)  18.2 us
    ppermute x2, starting transfers between devices, shards(): lax.ppermute(a, AXES, far_round(r))  16.8 us
    ppermute x2, waiting for transfers between devices, shards(): lax.ppermute(a, AXES, far_round(r))  11.6 us
    ppermute x3, starting transfers between devices, shards(): lax.ppermute(own, 'y', [((i + d) % 4, i) for i in range(4)])  10.1 us
    ppermute x1, waiting for transfers between devices, shards(): lax.ppermute(both, ('zl', 'c'), [(CROSS[i] * 2, i * 2) for i in range(4)]...  6.84 us
    ppermute x1, waiting for transfers between devices, shards(): lax.ppermute(send, AXES, home_round(1))  6.76 us
    ppermute x1, starting transfers between devices, shards(): lax.ppermute(mirror, AXES, home_round(0))  6.23 us
    pallas_call x1, Pallas kernels, shards(): pl.pallas_call(pairs_kernel, out_shape=jax.ShapeDtypeStruct((8, CHUNK, HA...  5 us
  transfers between devices with their start and end apart: 9, of which 6 were waited for; matrix products, arithmetic and copies ran while one was open for 0% of the time, Pallas kernels for 3%

profile of v6, /device:TPU:69, one launch (start us, length us, event | category | flops | bytes accessed | tf_op | source)
XLA Modules:
  0.0 105.3 jit_solution(453501565910300348)
XLA Ops:
  0.0 2.9 %contract.1.refs_0_ = bf16[784,256]{1,0:T(8,128)(2,1)} custom-call(bf16[2,6,64,256]{3,2,1,0:T(8,128)(2,1)} %raw_hbm.1, bf16[256,256]{1,0:T(8,128)(2,1)} %metric_hbm.1, s32[2,6]{1,0:T(2,128)} %sig_ref.1, s32[2]{0:T(128)} %bitcast.8), custom_call_target="tpu_custom_call" | custom-call | tf_op jit(solution)/shard_map/contract/pallas_call | solution.py:243
  2.9 2.9 %all-gather = bf16[1568,256]{1,0:T(8,128)(2,1)S(1)} all-gather(bf16[784,256]{1,0:T(8,128)(2,1)} %contract.1.refs_0_), channel_id=2, replica_groups=mesh['x'=4,'zh'=4,'y'=4,'zl'=4,'c'=2] {'c'}, dimensions={0}, use_global_device_ids=true | all-gather | bytes 1204224 | tf_op jit(solution)/shard_map/all_gather | solution.py:260
  5.8 0.0 copy-start
  5.8 3.7 %collective-permute-start.3 = (bf16[2,784,256]{2,1,0:T(8,128)(2,1)S(1)}, bf16[2,784,256]{2,1,0:T(8,128)(2,1)S(1)}, u32[]{:S(2)}, u32[]{:S(2)}) collective-permute-start(bf16[2,784,256]{2,1,0:T(8,128)(2,1)S(1)} %bitcast.6), channel_id=1, source_target_pairs={{6,0},{4,2},{0,4},{2,6},{3,1},{1,3},{7,5},{5,7},{14,8},{12,10},{8,... | collective-permute-start | bytes 2408456 | tf_op jit(solution)/shard_map/ppermute | solution.py:261
  9.5 4.8 %collective-permute-start = (bf16[784,256]{1,0:T(8,128)(2,1)}, bf16[784,256]{1,0:T(8,128)(2,1)S(1)}, u32[]{:S(2)}, u32[]{:S(2)}) collective-permute-start(bf16[784,256]{1,0:T(8,128)(2,1)} %contract.1.refs_0_), channel_id=1, source_target_pairs={{16,0},{24,8},{0,16},{8,24},{17,1},{25,9},{1,17},{9,25},{18,2},{26... | collective-permute-start | bytes 1204232 | tf_op jit(solution)/shard_map/ppermute | solution.py:266
  14.3 2.7 %collective-permute-start.1 = (bf16[784,256]{1,0:T(8,128)(2,1)}, bf16[784,256]{1,0:T(8,128)(2,1)S(1)}, u32[]{:S(2)}, u32[]{:S(2)}) collective-permute-start(bf16[784,256]{1,0:T(8,128)(2,1)} %contract.1.refs_0_), channel_id=1, source_target_pairs={{8,0},{16,8},{24,16},{0,24},{9,1},{17,9},{25,17},{1,25},{10,2},{18... | collective-permute-start | bytes 1204232 | tf_op jit(solution)/shard_map/ppermute | solution.py:266
  17.0 2.6 %collective-permute-start.2 = (bf16[784,256]{1,0:T(8,128)(2,1)}, bf16[784,256]{1,0:T(8,128)(2,1)S(1)}, u32[]{:S(2)}, u32[]{:S(2)}) collective-permute-start(bf16[784,256]{1,0:T(8,128)(2,1)} %contract.1.refs_0_), channel_id=1, source_target_pairs={{24,0},{0,8},{8,16},{16,24},{25,1},{1,9},{9,17},{17,25},{26,2},{2,... | collective-permute-start | bytes 1204232 | tf_op jit(solution)/shard_map/ppermute | solution.py:266
  19.6 0.9 rows.2.own_rows
  20.5 0.1 pad_add_fusion.place_ref
  20.6 6.8 %collective-permute-done.3.src = bf16[2,784,256]{2,1,0:T(8,128)(2,1)S(1)} collective-permute-done((bf16[2,784,256]{2,1,0:T(8,128)(2,1)S(1)}, bf16[2,784,256]{2,1,0:T(8,128)(2,1)S(1)}, u32[]{:S(2)}, u32[]{:S(2)}) %collective-permute-start.3) | collective-permute-done | bytes 802848 | tf_op jit(solution)/shard_map/ppermute | solution.py:261
  27.4 2.2 %collective-permute-start.4 = (bf16[2,784,256]{2,1,0:T(8,128)(2,1)S(1)}, bf16[2,784,256]{2,1,0:T(8,128)(2,1)S(1)}, u32[]{:S(2)}, u32[]{:S(2)}) collective-permute-start(bf16[2,784,256]{2,1,0:T(8,128)(2,1)S(1)} %collective-permute-done.3.src), channel_id=1, source_target_pairs={{0,1},{1,0},{2,3},{3,2},{4,5},{5,4},{6,7},{7,6},{8,9},{9,8},{10,11... | collective-permute-start | bytes 2408456 | tf_op jit(solution)/shard_map/ppermute | solution.py:258
  29.7 0.0 collective-permute-done.refs_1_
  29.7 2.7 %collective-permute-done.1.refs_2_ = bf16[784,256]{1,0:T(8,128)(2,1)S(1)} collective-permute-done((bf16[784,256]{1,0:T(8,128)(2,1)}, bf16[784,256]{1,0:T(8,128)(2,1)S(1)}, u32[]{:S(2)}, u32[]{:S(2)}) %collective-permute-start.1) | collective-permute-done | bytes 401440 | tf_op jit(solution)/shard_map/ppermute | solution.py:266
  32.4 0.0 collective-permute-done.2.refs_3_
  32.4 0.0 copy-done
  32.4 1.8 %column.1.cols = bf16[512,4096]{1,0:T(8,128)(2,1)S(1)} custom-call(s32[4]{0:T(128)S(1)} %pad_add_fusion.place_ref, bf16[784,256]{1,0:T(8,128)(2,1)S(1)} %copy-done, bf16[784,256]{1,0:T(8,128)(2,1)S(1)} %collective-permute-done.refs_1_, bf16[784,256]{1,0:T(8,128)(2,1)S(1)} %collective-permute-done.1.refs_2_, bf16[784,256]{1,0:T(8,128)(2,1)S(1)} %collective-permute-done.2.refs_3_), custom_call_target="tpu_custom_call" | custom-call | flops 20000000000 | bytes 6000000 | tf_op jit(solution)/shard_map/column/pallas_call | solution.py:286
  34.2 0.9 rows.3.first_rows
  35.1 0.0 collective-permute-done.4.src
  35.1 5.0 %pairs.1 = s16[8,528,128]{2,1,0:T(8,128)(2,1)S(1)} custom-call(s32[4]{0:T(128)S(1)} %pad_add_fusion.place_ref, bf16[512,4096]{1,0:T(8,128)(2,1)S(1)} %column.1.cols, bf16[256,4096]{1,0:T(8,128)(2,1)S(1)} %rows.2.own_rows, bf16[256,4096]{1,0:T(8,128)(2,1)S(1)} %rows.3.first_rows, bf16[2,784,256]{2,1,0:T(8,128)(2,1)S(1)} %collective-permute-done.4.src), custom_call_target="tpu_custom_call" | custom-call | tf_op jit(solution)/shard_map/pairs/pallas_call | solution.py:296
  40.1 18.2 %all_to_all.5.in_ref = s16[8,528,128]{2,1,0:T(8,128)(2,1)S(1)} all-to-all(s16[8,528,128]{2,1,0:T(8,128)(2,1)S(1)} %pairs.1), channel_id=1, replica_groups=mesh['x'=4,'zh'=4,'y'=4,'zl'=4,'c'=2] {'x','c'}, dimensions={0} | all-to-all | bytes 2162688 | tf_op jit(solution)/shard_map/all_to_all | solution.py:305
  58.3 0.9 middle.1
  59.2 13.6 %collective-permute-start.5 = (s16[272,256]{1,0:T(8,128)(2,1)S(1)}, s16[272,256]{1,0:T(8,128)(2,1)S(1)}, u32[]{:S(2)}, u32[]{:S(2)}) collective-permute-start(s16[272,256]{1,0:T(8,128)(2,1)S(1)} %get-tuple-element.10), channel_id=1, source_target_pairs={{0,0},{1,6},{2,34},{3,36},{4,68},{5,64},{6,102},{7,98},{8,8},{9,14... | collective-permute-start | bytes 417800 | tf_op jit(solution)/shard_map/ppermute | solution.py:324
  72.7 3.2 %collective-permute-start.6 = (s16[272,256]{1,0:T(8,128)(2,1)S(1)}, s16[272,256]{1,0:T(8,128)(2,1)S(1)}, u32[]{:S(2)}, u32[]{:S(2)}) collective-permute-start(s16[272,256]{1,0:T(8,128)(2,1)S(1)} %get-tuple-element.11), channel_id=1, source_target_pairs={{0,2},{1,96},{2,32},{3,66},{4,70},{5,4},{6,100},{7,38},{8,10},{9,1... | collective-permute-start | bytes 417800 | tf_op jit(solution)/shard_map/ppermute | solution.py:324
  76.0 3.3 %collective-permute-done.5.a_ref = s16[272,256]{1,0:T(8,128)(2,1)S(1)} collective-permute-done((s16[272,256]{1,0:T(8,128)(2,1)S(1)}, s16[272,256]{1,0:T(8,128)(2,1)S(1)}, u32[]{:S(2)}, u32[]{:S(2)}) %collective-permute-start.5) | collective-permute-done | bytes 139296 | tf_op jit(solution)/shard_map/ppermute | solution.py:324
  79.2 8.3 %collective-permute-done.6.b_ref = s16[272,256]{1,0:T(8,128)(2,1)S(1)} collective-permute-done((s16[272,256]{1,0:T(8,128)(2,1)S(1)}, s16[272,256]{1,0:T(8,128)(2,1)S(1)}, u32[]{:S(2)}, u32[]{:S(2)}) %collective-permute-start.6) | collective-permute-done | bytes 139296 | tf_op jit(solution)/shard_map/ppermute | solution.py:324
  87.6 0.7 join.1
  88.2 6.2 %collective-permute-start.7 = (s16[144,256]{1,0:T(8,128)(2,1)S(1)}, s16[144,256]{1,0:T(8,128)(2,1)S(1)}, u32[]{:S(2)}, u32[]{:S(2)}) collective-permute-start(s16[144,256]{1,0:T(8,128)(2,1)S(1)} %get-tuple-element.13), channel_id=1, source_target_pairs={{4,4},{5,5},{12,132},{13,133},{20,260},{21,261},{28,388},{29,389},... | collective-permute-start | bytes 221192 | tf_op jit(solution)/shard_map/ppermute | solution.py:332
  94.5 1.9 %collective-permute-start.8 = (s16[144,256]{1,0:T(8,128)(2,1)S(1)}, s16[144,256]{1,0:T(8,128)(2,1)S(1)}, u32[]{:S(2)}, u32[]{:S(2)}) collective-permute-start(s16[144,256]{1,0:T(8,128)(2,1)S(1)} %get-tuple-element.14), channel_id=1, source_target_pairs={{0,1},{1,0},{2,3},{3,2},{4,5},{5,4},{6,7},{7,6},{8,9},{9,8},{10,11... | collective-permute-start | bytes 221192 | tf_op jit(solution)/shard_map/ppermute | solution.py:332
  96.4 0.9 collective-permute-done.7.mirror_ref
  97.3 6.8 %collective-permute-done.8.come_ref = s16[144,256]{1,0:T(8,128)(2,1)S(1)} collective-permute-done((s16[144,256]{1,0:T(8,128)(2,1)S(1)}, s16[144,256]{1,0:T(8,128)(2,1)S(1)}, u32[]{:S(2)}, u32[]{:S(2)}) %collective-permute-start.8) | collective-permute-done | bytes 73760 | tf_op jit(solution)/shard_map/ppermute | solution.py:332
  104.1 1.2 %last.1 = f32[128,256]{1,0:T(8,128)} custom-call(s32[4]{0:T(128)S(1)} %pad_add_fusion.place_ref, f32[128,256]{1,0:T(8,128)S(1)} %get-tuple-element.12.keep_ref, s16[144,256]{1,0:T(8,128)(2,1)S(1)} %collective-permute-done.7.mirror_ref, s16[144,256]{1,0:T(8,128)(2,1)S(1)} %collective-permute-done.8.come_ref), custom_call_target="tpu_custom_call" | custom-call | tf_op jit(solution)/shard_map/last/pallas_call | solution.py:325
Async XLA Ops:
  5.8 26.6 %copy-start = (bf16[784,256]{1,0:T(8,128)(2,1)S(1)}, bf16[784,256]{1,0:T(8,128)(2,1)}, u32[]{:S(2)}) copy-start(bf16[784,256]{1,0:T(8,128)(2,1)} %contract.1.refs_0_) | copy-start | bytes 1204228
  5.8 21.6 %collective-permute-start.3 = (bf16[2,784,256]{2,1,0:T(8,128)(2,1)S(1)}, bf16[2,784,256]{2,1,0:T(8,128)(2,1)S(1)}, u32[]{:S(2)}, u32[]{:S(2)}) collective-permute-start(bf16[2,784,256]{2,1,0:T(8,128)(2,1)S(1)} %bitcast.6), channel_id=1, source_target_pairs={{6,0},{4,2},{0,4},{2,6},{3,1},{1,3},{7,5},{5,7},{14,8},{12,10},{8,... | collective-permute-start | bytes 2408456 | tf_op jit(solution)/shard_map/ppermute | solution.py:261
  9.5 20.2 %collective-permute-start = (bf16[784,256]{1,0:T(8,128)(2,1)}, bf16[784,256]{1,0:T(8,128)(2,1)S(1)}, u32[]{:S(2)}, u32[]{:S(2)}) collective-permute-start(bf16[784,256]{1,0:T(8,128)(2,1)} %contract.1.refs_0_), channel_id=1, source_target_pairs={{16,0},{24,8},{0,16},{8,24},{17,1},{25,9},{1,17},{9,25},{18,2},{26... | collective-permute-start | bytes 1204232 | tf_op jit(solution)/shard_map/ppermute | solution.py:266
  14.3 18.1 %collective-permute-start.1 = (bf16[784,256]{1,0:T(8,128)(2,1)}, bf16[784,256]{1,0:T(8,128)(2,1)S(1)}, u32[]{:S(2)}, u32[]{:S(2)}) collective-permute-start(bf16[784,256]{1,0:T(8,128)(2,1)} %contract.1.refs_0_), channel_id=1, source_target_pairs={{8,0},{16,8},{24,16},{0,24},{9,1},{17,9},{25,17},{1,25},{10,2},{18... | collective-permute-start | bytes 1204232 | tf_op jit(solution)/shard_map/ppermute | solution.py:266
  17.0 15.4 %collective-permute-start.2 = (bf16[784,256]{1,0:T(8,128)(2,1)}, bf16[784,256]{1,0:T(8,128)(2,1)S(1)}, u32[]{:S(2)}, u32[]{:S(2)}) collective-permute-start(bf16[784,256]{1,0:T(8,128)(2,1)} %contract.1.refs_0_), channel_id=1, source_target_pairs={{24,0},{0,8},{8,16},{16,24},{25,1},{1,9},{9,17},{17,25},{26,2},{2,... | collective-permute-start | bytes 1204232 | tf_op jit(solution)/shard_map/ppermute | solution.py:266
  27.4 7.7 %collective-permute-start.4 = (bf16[2,784,256]{2,1,0:T(8,128)(2,1)S(1)}, bf16[2,784,256]{2,1,0:T(8,128)(2,1)S(1)}, u32[]{:S(2)}, u32[]{:S(2)}) collective-permute-start(bf16[2,784,256]{2,1,0:T(8,128)(2,1)S(1)} %collective-permute-done.3.src), channel_id=1, source_target_pairs={{0,1},{1,0},{2,3},{3,2},{4,5},{5,4},{6,7},{7,6},{8,9},{9,8},{10,11... | collective-permute-start | bytes 2408456 | tf_op jit(solution)/shard_map/ppermute | solution.py:258
  59.2 20.1 %collective-permute-start.5 = (s16[272,256]{1,0:T(8,128)(2,1)S(1)}, s16[272,256]{1,0:T(8,128)(2,1)S(1)}, u32[]{:S(2)}, u32[]{:S(2)}) collective-permute-start(s16[272,256]{1,0:T(8,128)(2,1)S(1)} %get-tuple-element.10), channel_id=1, source_target_pairs={{0,0},{1,6},{2,34},{3,36},{4,68},{5,64},{6,102},{7,98},{8,8},{9,14... | collective-permute-start | bytes 417800 | tf_op jit(solution)/shard_map/ppermute | solution.py:324
  72.7 14.8 %collective-permute-start.6 = (s16[272,256]{1,0:T(8,128)(2,1)S(1)}, s16[272,256]{1,0:T(8,128)(2,1)S(1)}, u32[]{:S(2)}, u32[]{:S(2)}) collective-permute-start(s16[272,256]{1,0:T(8,128)(2,1)S(1)} %get-tuple-element.11), channel_id=1, source_target_pairs={{0,2},{1,96},{2,32},{3,66},{4,70},{5,4},{6,100},{7,38},{8,10},{9,1... | collective-permute-start | bytes 417800 | tf_op jit(solution)/shard_map/ppermute | solution.py:324
  88.2 9.1 %collective-permute-start.7 = (s16[144,256]{1,0:T(8,128)(2,1)S(1)}, s16[144,256]{1,0:T(8,128)(2,1)S(1)}, u32[]{:S(2)}, u32[]{:S(2)}) collective-permute-start(s16[144,256]{1,0:T(8,128)(2,1)S(1)} %get-tuple-element.13), channel_id=1, source_target_pairs={{4,4},{5,5},{12,132},{13,133},{20,260},{21,261},{28,388},{29,389},... | collective-permute-start | bytes 221192 | tf_op jit(solution)/shard_map/ppermute | solution.py:332
  94.5 9.6 %collective-permute-start.8 = (s16[144,256]{1,0:T(8,128)(2,1)S(1)}, s16[144,256]{1,0:T(8,128)(2,1)S(1)}, u32[]{:S(2)}, u32[]{:S(2)}) collective-permute-start(s16[144,256]{1,0:T(8,128)(2,1)S(1)} %get-tuple-element.14), channel_id=1, source_target_pairs={{0,1},{1,0},{2,3},{3,2},{4,5},{5,4},{6,7},{7,6},{8,9},{9,8},{10,11... | collective-permute-start | bytes 221192 | tf_op jit(solution)/shard_map/ppermute | solution.py:332

commit v7 on v5

--- a/solution.py
+++ b/solution.py
@@ -107,35 +107,29 @@
         scatter(column[i], ids, i, out_ref, lax.rem(place_ref[0] + d, 4) * HALF)
 
 
-def rows_kernel(src, out_ref, ids_vmem, ids, sem):
-    halves = [src.at[k] for k in range(2)]
-    copy = load_ids(halves, ids_vmem, ids, sem)
+def rows_kernel(place_ref, mine, other, out_ref, ids_vmem, ids, sem):
+    core = place_ref[1]
+    copy = load_ids([mine, other], ids_vmem, ids, sem)
     copy.start()
     out_ref[...] = jnp.zeros_like(out_ref)
     copy.wait()
-    for k in range(2):
-        scatter(halves[k], ids, k, out_ref, k * HALF)
-
-
-def pairs_kernel(place_ref, cols, own_rows, first_rows, src, out_ref, rows, ids_vmem, ids, sem):
-    core = place_ref[1]
-    rows_kernel(src, rows, ids_vmem, ids, sem)
+    scatter(mine, ids, 0, out_ref, core * HALF)
+    scatter(other, ids, 1, out_ref, (1 - core) * HALF)
+
+
+def pairs_kernel(cols, own_rows, across_rows, near_rows, out_ref):
     exponents = {}
-    places = ((0, 0), (1 - core, core * CHIP), (core, (1 - core) * CHIP))
-    for t, block in enumerate((own_rows, first_rows, rows)):
+    for t, block in enumerate((own_rows, near_rows, across_rows)):
         part = lax.dot_general(block[...], cols[...], NT, preferred_element_type=jnp.float32)
-        chunk, first = places[t]
         for i in range(4):
             coded, exponents[t, i] = encode(part[:, i * HALF : (i + 1) * HALF])
-            at = pl.ds(first if t == 0 else pl.multiple_of(first, CHIP), CHIP)
-            out_ref[i * 2 + chunk, at, :] = coded
-    zero = core == 0
+            first = (t % 2) * CHIP
+            out_ref[i * 2 + t // 2, first : first + CHIP, :] = coded
     for i in range(4):
         out_ref[i * 2 + 1, CHIP : 2 * CHIP, :] = jnp.zeros((CHIP, HALF), jnp.int16)
-        near = jnp.where(zero, exponents[2, i], exponents[1, i])
-        across = jnp.where(zero, exponents[1, i], exponents[2, i])
-        out_ref[i * 2, 2 * CHIP :, :] = pick_rows([exponents[0, i], near], HALF).astype(jnp.int16)
-        out_ref[i * 2 + 1, 2 * CHIP :, :] = pick_rows([across], HALF).astype(jnp.int16)
+        for k in range(2):
+            block = pick_rows([exponents[k * 2, i], exponents[1, i]], HALF)
+            out_ref[i * 2 + k, 2 * CHIP :, :] = block.astype(jnp.int16)
 
 
 def middle_kernel(place_ref, in_ref, even_ref, odd_ref):
@@ -222,12 +216,8 @@
     def swap(a):
         return lax.ppermute(a, "c", [(0, 1), (1, 0)])
 
-    both = lax.all_gather(own, "c")
-    along = lax.ppermute(
-        both,
-        ("zl", "c"),
-        [(CROSS[i] * 2, i * 2) for i in range(4)] + [((i ^ 1) * 2 + 1, i * 2 + 1) for i in range(4)],
-    )
+    across = lax.ppermute(own, "zl", [(CROSS[i], i) for i in range(4)])
+    near = lax.ppermute(own, "zl", [(i ^ 1, i) for i in range(4)])
     column = [own] + [lax.ppermute(own, "y", [((i + d) % 4, i) for i in range(4)]) for d in (2, 1, 3)]
     def ids_scratch(count):
         return [
@@ -236,17 +226,17 @@
             pltpu.SemaphoreType.DMA,
         ]
 
-    def dense_rows(block):
+    def dense_rows(block, flops):
         return pl.pallas_call(
             rows_kernel,
             out_shape=jax.ShapeDtypeStruct((CHIP, NOB * AUX), jnp.bfloat16),
-            in_specs=[VMEM],
+            in_specs=[SMEM, VMEM, VMEM],
             out_specs=VMEM,
             scratch_shapes=ids_scratch(2),
             compiler_params=params(16),
-            cost_estimate=pl.CostEstimate(flops=1_000_000_000, bytes_accessed=3_000_000, transcendentals=0),
+            cost_estimate=pl.CostEstimate(flops=flops, bytes_accessed=3_000_000, transcendentals=0),
             name="rows",
-        )(block)
+        )(place, block, swap(block))
 
     dense = pl.pallas_call(
         column_kernel,
@@ -255,18 +245,22 @@
         out_specs=VMEM,
         scratch_shapes=ids_scratch(4),
         compiler_params=params(16),
-        cost_estimate=pl.CostEstimate(flops=20_000_000_000, bytes_accessed=6_000_000, transcendentals=0),
+        cost_estimate=pl.CostEstimate(flops=12_000_000_000, bytes_accessed=6_000_000, transcendentals=0),
         name="column",
     )(place, *column)
     tiles = pl.pallas_call(
         pairs_kernel,
         out_shape=jax.ShapeDtypeStruct((8, CHUNK, HALF), jnp.int16),
-        in_specs=[SMEM] + [VMEM] * 4,
-        out_specs=VMEM,
-        scratch_shapes=[pltpu.VMEM((CHIP, NOB * AUX), jnp.bfloat16)] + ids_scratch(2),
-        compiler_params=params(16),
+        in_specs=[VMEM] * 4,
+        out_specs=VMEM,
+        compiler_params=params(24),
         name="pairs",
-    )(place, dense, dense_rows(both), dense_rows(along), swap(along))
+    )(
+        dense,
+        dense_rows(own, 1_000_000_000),
+        dense_rows(across, 1_000_000_000),
+        dense_rows(near, 1_000_000_000),
+    )
     arrived = lax.all_to_all(tiles, ("x", "c"), 0, 0, tiled=True)
     wide = jax.ShapeDtypeStruct((WIDE, CHIP), jnp.int16)
     messages = pl.pallas_call(

time: 103 us -> 103 us (level)
  the two profiles are of different devices: /device:TPU:81 before, /device:TPU:71 now
where the time goes in v7:
time: 103 us
  starting transfers between devices  47 us (46%)
  waiting for transfers between devices  21.2 us (21%)
  blocking collectives  18.5 us (18%)
  Pallas kernels  14.8 us (14%)
    ppermute x2, starting transfers between devices, shards(): lax.ppermute(a, AXES, far_round(r))  18.8 us
    all_to_all x1, blocking collectives, shards(): arrived = lax.all_to_all(tiles, ('x', 'c'), 0, 0, tiled=True)  18.5 us
    ppermute x2, waiting for transfers between devices, shards(): lax.ppermute(a, AXES, far_round(r))  15.8 us
    ppermute x4, starting transfers between devices, swap(): return lax.ppermute(a, 'c', [(0, 1), (1, 0)])  12.6 us
    ppermute x3, starting transfers between devices, shards(): lax.ppermute(own, 'y', [((i + d) % 4, i) for i in range(4)])  10.1 us
    pallas_call x3, Pallas kernels, dense_rows(): pl.pallas_call(rows_kernel, out_shape=jax.ShapeDtypeStruct((CHIP, NOB * A...  4.33 us
    ppermute x1, waiting for transfers between devices, shards(): across = lax.ppermute(own, 'zl', [(CROSS[i], i) for i in range(4)])  4.11 us
    pallas_call x1, Pallas kernels, shards(): pl.pallas_call(pairs_kernel, out_shape=jax.ShapeDtypeStruct((8, CHUNK, HA...  3.58 us
  transfers between devices with their start and end apart: 11, of which 4 were waited for; matrix products, arithmetic and copies ran while one was open for 0% of the time, Pallas kernels for 5%

profile of v7, /device:TPU:71, one launch (start us, length us, event | category | flops | bytes accessed | tf_op | source)
XLA Modules:
  0.0 102.8 jit_solution(8875892773472242831)
XLA Ops:
  0.0 2.9 %contract.1.refs_0_.mine = bf16[784,256]{1,0:T(8,128)(2,1)} custom-call(bf16[2,6,64,256]{3,2,1,0:T(8,128)(2,1)} %raw_hbm.1, bf16[256,256]{1,0:T(8,128)(2,1)} %metric_hbm.1, s32[2,6]{1,0:T(2,128)} %sig_ref.1, s32[2]{0:T(128)} %bitcast.4), custom_call_target="tpu_custom_call" | custom-call | tf_op jit(solution)/shard_map/contract/pallas_call | solution.py:202
  2.9 4.8 %collective-permute-start = (bf16[784,256]{1,0:T(8,128)(2,1)}, bf16[784,256]{1,0:T(8,128)(2,1)S(1)}, u32[]{:S(2)}, u32[]{:S(2)}) collective-permute-start(bf16[784,256]{1,0:T(8,128)(2,1)} %contract.1.refs_0_.mine), channel_id=1, source_target_pairs={{16,0},{24,8},{0,16},{8,24},{17,1},{25,9},{1,17},{9,25},{18,2},{26... | collective-permute-start | bytes 1204232 | tf_op jit(solution)/shard_map/ppermute | solution.py:221
  7.7 1.9 %collective-permute-start.4 = (bf16[784,256]{1,0:T(8,128)(2,1)}, bf16[784,256]{1,0:T(8,128)(2,1)S(1)}, u32[]{:S(2)}, u32[]{:S(2)}) collective-permute-start(bf16[784,256]{1,0:T(8,128)(2,1)} %contract.1.refs_0_.mine), channel_id=1, source_target_pairs={{6,0},{4,2},{0,4},{2,6},{7,1},{5,3},{1,5},{3,7},{14,8},{12,10},{8,... | collective-permute-start | bytes 1204232 | tf_op jit(solution)/shard_map/ppermute | solution.py:219
  9.7 3.5 %collective-permute-start.6 = (bf16[784,256]{1,0:T(8,128)(2,1)}, bf16[784,256]{1,0:T(8,128)(2,1)S(1)}, u32[]{:S(2)}, u32[]{:S(2)}) collective-permute-start(bf16[784,256]{1,0:T(8,128)(2,1)} %contract.1.refs_0_.mine), channel_id=1, source_target_pairs={{2,0},{0,2},{6,4},{4,6},{3,1},{1,3},{7,5},{5,7},{10,8},{8,10},{14,... | collective-permute-start | bytes 1204232 | tf_op jit(solution)/shard_map/ppermute | solution.py:220
  13.2 2.7 %collective-permute-start.1 = (bf16[784,256]{1,0:T(8,128)(2,1)}, bf16[784,256]{1,0:T(8,128)(2,1)S(1)}, u32[]{:S(2)}, u32[]{:S(2)}) collective-permute-start(bf16[784,256]{1,0:T(8,128)(2,1)} %contract.1.refs_0_.mine), channel_id=1, source_target_pairs={{8,0},{16,8},{24,16},{0,24},{9,1},{17,9},{25,17},{1,25},{10,2},{18... | collective-permute-start | bytes 1204232 | tf_op jit(solution)/shard_map/ppermute | solution.py:221
  15.9 2.6 %collective-permute-start.2 = (bf16[784,256]{1,0:T(8,128)(2,1)}, bf16[784,256]{1,0:T(8,128)(2,1)S(1)}, u32[]{:S(2)}, u32[]{:S(2)}) collective-permute-start(bf16[784,256]{1,0:T(8,128)(2,1)} %contract.1.refs_0_.mine), channel_id=1, source_target_pairs={{24,0},{0,8},{8,16},{16,24},{25,1},{1,9},{9,17},{17,25},{26,2},{2,... | collective-permute-start | bytes 1204232 | tf_op jit(solution)/shard_map/ppermute | solution.py:221
  18.5 0.1 pad_add_fusion.place_ref
  18.6 0.0 collective-permute-done.refs_1_
  18.6 3.7 %collective-permute-start.3 = (bf16[784,256]{1,0:T(8,128)(2,1)}, bf16[784,256]{1,0:T(8,128)(2,1)S(1)}, u32[]{:S(2)}, u32[]{:S(2)}) collective-permute-start(bf16[784,256]{1,0:T(8,128)(2,1)} %contract.1.refs_0_.mine), channel_id=1, source_target_pairs={{0,1},{1,0},{2,3},{3,2},{4,5},{5,4},{6,7},{7,6},{8,9},{9,8},{10,11... | collective-permute-start | bytes 1204232 | tf_op jit(solution)/shard_map/ppermute | solution.py:217
  22.3 4.1 %collective-permute-done.4.mine = bf16[784,256]{1,0:T(8,128)(2,1)S(1)} collective-permute-done((bf16[784,256]{1,0:T(8,128)(2,1)}, bf16[784,256]{1,0:T(8,128)(2,1)S(1)}, u32[]{:S(2)}, u32[]{:S(2)}) %collective-permute-start.4) | collective-permute-done | bytes 401440 | tf_op jit(solution)/shard_map/ppermute | solution.py:219
  26.4 3.6 %collective-permute-start.5 = (bf16[784,256]{1,0:T(8,128)(2,1)S(1)}, bf16[784,256]{1,0:T(8,128)(2,1)S(1)}, u32[]{:S(2)}, u32[]{:S(2)}) collective-permute-start(bf16[784,256]{1,0:T(8,128)(2,1)S(1)} %collective-permute-done.4.mine), channel_id=1, source_target_pairs={{0,1},{1,0},{2,3},{3,2},{4,5},{5,4},{6,7},{7,6},{8,9},{9,8},{10,11... | collective-permute-start | bytes 1204232 | tf_op jit(solution)/shard_map/ppermute | solution.py:217
  30.0 3.4 %collective-permute-start.7 = (bf16[784,256]{1,0:T(8,128)(2,1)S(1)}, bf16[784,256]{1,0:T(8,128)(2,1)S(1)}, u32[]{:S(2)}, u32[]{:S(2)}) collective-permute-start(bf16[784,256]{1,0:T(8,128)(2,1)S(1)} %collective-permute-done.6.mine), channel_id=1, source_target_pairs={{0,1},{1,0},{2,3},{3,2},{4,5},{5,4},{6,7},{7,6},{8,9},{9,8},{10,11... | collective-permute-start | bytes 1204232 | tf_op jit(solution)/shard_map/ppermute | solution.py:217
  33.4 0.0 collective-permute-done.1.refs_2_
  33.4 0.0 collective-permute-done.2.refs_3_
  33.5 1.0 copy-done
  34.4 1.8 %column.1.cols = bf16[512,4096]{1,0:T(8,128)(2,1)S(1)} custom-call(s32[3]{0:T(128)S(1)} %pad_add_fusion.place_ref, bf16[784,256]{1,0:T(8,128)(2,1)S(1)} %copy-done, bf16[784,256]{1,0:T(8,128)(2,1)S(1)} %collective-permute-done.refs_1_, bf16[784,256]{1,0:T(8,128)(2,1)S(1)} %collective-permute-done.1.refs_2_, bf16[784,256]{1,0:T(8,128)(2,1)S(1)} %collective-permute-done.2.refs_3_), custom_call_target="tpu_custom_call" | custom-call | flops 12000000000 | bytes 6000000 | tf_op jit(solution)/shard_map/column/pallas_call | solution.py:241
  36.2 0.0 collective-permute-done.3.other
  36.2 1.4 %rows.3.own_rows = bf16[256,4096]{1,0:T(8,128)(2,1)S(1)} custom-call(s32[3]{0:T(128)S(1)} %pad_add_fusion.place_ref, bf16[784,256]{1,0:T(8,128)(2,1)S(1)} %copy-done, bf16[784,256]{1,0:T(8,128)(2,1)S(1)} %collective-permute-done.3.other), custom_call_target="tpu_custom_call" | custom-call | flops 1000000000 | bytes 3000000 | tf_op jit(solution)/shard_map/rows/pallas_call | solution.py:230
  37.7 0.0 collective-permute-done.5.other
  37.7 1.4 %rows.4.across_rows = bf16[256,4096]{1,0:T(8,128)(2,1)S(1)} custom-call(s32[3]{0:T(128)S(1)} %pad_add_fusion.place_ref, bf16[784,256]{1,0:T(8,128)(2,1)S(1)} %collective-permute-done.4.mine, bf16[784,256]{1,0:T(8,128)(2,1)S(1)} %collective-permute-done.5.other), custom_call_target="tpu_custom_call" | custom-call | flops 1000000000 | bytes 3000000 | tf_op jit(solution)/shard_map/rows/pallas_call | solution.py:230
  39.2 1.4 %rows.5.near_rows = bf16[256,4096]{1,0:T(8,128)(2,1)S(1)} custom-call(s32[3]{0:T(128)S(1)} %pad_add_fusion.place_ref, bf16[784,256]{1,0:T(8,128)(2,1)S(1)} %collective-permute-done.6.mine, bf16[784,256]{1,0:T(8,128)(2,1)S(1)} %collective-permute-done.7.other), custom_call_target="tpu_custom_call" | custom-call | flops 1000000000 | bytes 3000000 | tf_op jit(solution)/shard_map/rows/pallas_call | solution.py:230
  40.6 3.6 %pairs.1 = s16[8,528,128]{2,1,0:T(8,128)(2,1)S(1)} custom-call(bf16[512,4096]{1,0:T(8,128)(2,1)S(1)} %column.1.cols, bf16[256,4096]{1,0:T(8,128)(2,1)S(1)} %rows.3.own_rows, bf16[256,4096]{1,0:T(8,128)(2,1)S(1)} %rows.4.across_rows, bf16[256,4096]{1,0:T(8,128)(2,1)S(1)} %rows.5.near_rows), custom_call_target="tpu_custom_call" | custom-call | tf_op jit(solution)/shard_map/pairs/pallas_call | solution.py:251
  44.2 18.5 %all_to_all.5.in_ref = s16[8,528,128]{2,1,0:T(8,128)(2,1)S(1)} all-to-all(s16[8,528,128]{2,1,0:T(8,128)(2,1)S(1)} %pairs.1), channel_id=1, replica_groups=mesh['x'=4,'zh'=4,'y'=4,'zl'=4,'c'=2] {'x','c'}, dimensions={0} | all-to-all | bytes 2162688 | tf_op jit(solution)/shard_map/all_to_all | solution.py:264
  62.7 0.9 middle.1
  63.6 13.7 %collective-permute-start.8 = (s16[272,256]{1,0:T(8,128)(2,1)S(1)}, s16[272,256]{1,0:T(8,128)(2,1)S(1)}, u32[]{:S(2)}, u32[]{:S(2)}) collective-permute-start(s16[272,256]{1,0:T(8,128)(2,1)S(1)} %get-tuple-element.9), channel_id=1, source_target_pairs={{0,0},{1,6},{2,34},{3,36},{4,68},{5,64},{6,102},{7,98},{8,8},{9,14... | collective-permute-start | bytes 417800 | tf_op jit(solution)/shard_map/ppermute | solution.py:282
  77.3 5.1 %collective-permute-start.9 = (s16[272,256]{1,0:T(8,128)(2,1)S(1)}, s16[272,256]{1,0:T(8,128)(2,1)S(1)}, u32[]{:S(2)}, u32[]{:S(2)}) collective-permute-start(s16[272,256]{1,0:T(8,128)(2,1)S(1)} %get-tuple-element.10), channel_id=1, source_target_pairs={{0,2},{1,96},{2,32},{3,66},{4,70},{5,4},{6,100},{7,38},{8,10},{9,2... | collective-permute-start | bytes 417800 | tf_op jit(solution)/shard_map/ppermute | solution.py:282
  82.4 2.0 %collective-permute-done.8.a_ref = s16[272,256]{1,0:T(8,128)(2,1)S(1)} collective-permute-done((s16[272,256]{1,0:T(8,128)(2,1)S(1)}, s16[272,256]{1,0:T(8,128)(2,1)S(1)}, u32[]{:S(2)}, u32[]{:S(2)}) %collective-permute-start.8) | collective-permute-done | bytes 139296 | tf_op jit(solution)/shard_map/ppermute | solution.py:282
  84.5 13.8 %collective-permute-done.9.b_ref = s16[272,256]{1,0:T(8,128)(2,1)S(1)} collective-permute-done((s16[272,256]{1,0:T(8,128)(2,1)S(1)}, s16[272,256]{1,0:T(8,128)(2,1)S(1)}, u32[]{:S(2)}, u32[]{:S(2)}) %collective-permute-start.9) | collective-permute-done | bytes 139296 | tf_op jit(solution)/shard_map/ppermute | solution.py:282
  98.2 0.6 join.1
  98.9 1.9 %collective-permute-start.10 = (f32[128,256]{1,0:T(8,128)S(1)}, f32[128,256]{1,0:T(8,128)S(1)}, u32[]{:S(2)}, u32[]{:S(2)}) collective-permute-start(f32[128,256]{1,0:T(8,128)S(1)} %get-tuple-element.12), channel_id=1, source_target_pairs={{0,1},{1,0},{2,3},{3,2},{4,5},{5,4},{6,7},{7,6},{8,9},{9,8},{10,11... | collective-permute-start | bytes 393224 | tf_op jit(solution)/shard_map/ppermute | solution.py:217
  100.8 1.3 %collective-permute-done.10.come_ref = f32[128,256]{1,0:T(8,128)S(1)} collective-permute-done((f32[128,256]{1,0:T(8,128)S(1)}, f32[128,256]{1,0:T(8,128)S(1)}, u32[]{:S(2)}, u32[]{:S(2)}) %collective-permute-start.10) | collective-permute-done | bytes 131104 | tf_op jit(solution)/shard_map/ppermute | solution.py:217
  102.1 0.7 last.1
  (3 shorter events, 0.0 us)
Async XLA Ops:
  2.9 15.7 %collective-permute-start = (bf16[784,256]{1,0:T(8,128)(2,1)}, bf16[784,256]{1,0:T(8,128)(2,1)S(1)}, u32[]{:S(2)}, u32[]{:S(2)}) collective-permute-start(bf16[784,256]{1,0:T(8,128)(2,1)} %contract.1.refs_0_.mine), channel_id=1, source_target_pairs={{16,0},{24,8},{0,16},{8,24},{17,1},{25,9},{1,17},{9,25},{18,2},{26... | collective-permute-start | bytes 1204232 | tf_op jit(solution)/shard_map/ppermute | solution.py:221
  7.7 18.7 %collective-permute-start.4 = (bf16[784,256]{1,0:T(8,128)(2,1)}, bf16[784,256]{1,0:T(8,128)(2,1)S(1)}, u32[]{:S(2)}, u32[]{:S(2)}) collective-permute-start(bf16[784,256]{1,0:T(8,128)(2,1)} %contract.1.refs_0_.mine), channel_id=1, source_target_pairs={{6,0},{4,2},{0,4},{2,6},{7,1},{5,3},{1,5},{3,7},{14,8},{12,10},{8,... | collective-permute-start | bytes 1204232 | tf_op jit(solution)/shard_map/ppermute | solution.py:219
  9.7 20.3 %collective-permute-start.6 = (bf16[784,256]{1,0:T(8,128)(2,1)}, bf16[784,256]{1,0:T(8,128)(2,1)S(1)}, u32[]{:S(2)}, u32[]{:S(2)}) collective-permute-start(bf16[784,256]{1,0:T(8,128)(2,1)} %contract.1.refs_0_.mine), channel_id=1, source_target_pairs={{2,0},{0,2},{6,4},{4,6},{3,1},{1,3},{7,5},{5,7},{10,8},{8,10},{14,... | collective-permute-start | bytes 1204232 | tf_op jit(solution)/shard_map/ppermute | solution.py:220
  13.2 20.2 %collective-permute-start.1 = (bf16[784,256]{1,0:T(8,128)(2,1)}, bf16[784,256]{1,0:T(8,128)(2,1)S(1)}, u32[]{:S(2)}, u32[]{:S(2)}) collective-permute-start(bf16[784,256]{1,0:T(8,128)(2,1)} %contract.1.refs_0_.mine), channel_id=1, source_target_pairs={{8,0},{16,8},{24,16},{0,24},{9,1},{17,9},{25,17},{1,25},{10,2},{18... | collective-permute-start | bytes 1204232 | tf_op jit(solution)/shard_map/ppermute | solution.py:221
  15.9 17.5 %collective-permute-start.2 = (bf16[784,256]{1,0:T(8,128)(2,1)}, bf16[784,256]{1,0:T(8,128)(2,1)S(1)}, u32[]{:S(2)}, u32[]{:S(2)}) collective-permute-start(bf16[784,256]{1,0:T(8,128)(2,1)} %contract.1.refs_0_.mine), channel_id=1, source_target_pairs={{24,0},{0,8},{8,16},{16,24},{25,1},{1,9},{9,17},{17,25},{26,2},{2,... | collective-permute-start | bytes 1204232 | tf_op jit(solution)/shard_map/ppermute | solution.py:221
  18.6 17.6 %collective-permute-start.3 = (bf16[784,256]{1,0:T(8,128)(2,1)}, bf16[784,256]{1,0:T(8,128)(2,1)S(1)}, u32[]{:S(2)}, u32[]{:S(2)}) collective-permute-start(bf16[784,256]{1,0:T(8,128)(2,1)} %contract.1.refs_0_.mine), channel_id=1, source_target_pairs={{0,1},{1,0},{2,3},{3,2},{4,5},{5,4},{6,7},{7,6},{8,9},{9,8},{10,11... | collective-permute-start | bytes 1204232 | tf_op jit(solution)/shard_map/ppermute | solution.py:217
  26.4 11.3 %collective-permute-start.5 = (bf16[784,256]{1,0:T(8,128)(2,1)S(1)}, bf16[784,256]{1,0:T(8,128)(2,1)S(1)}, u32[]{:S(2)}, u32[]{:S(2)}) collective-permute-start(bf16[784,256]{1,0:T(8,128)(2,1)S(1)} %collective-permute-done.4.mine), channel_id=1, source_target_pairs={{0,1},{1,0},{2,3},{3,2},{4,5},{5,4},{6,7},{7,6},{8,9},{9,8},{10,11... | collective-permute-start | bytes 1204232 | tf_op jit(solution)/shard_map/ppermute | solution.py:217
  30.0 9.2 %collective-permute-start.7 = (bf16[784,256]{1,0:T(8,128)(2,1)S(1)}, bf16[784,256]{1,0:T(8,128)(2,1)S(1)}, u32[]{:S(2)}, u32[]{:S(2)}) collective-permute-start(bf16[784,256]{1,0:T(8,128)(2,1)S(1)} %collective-permute-done.6.mine), channel_id=1, source_target_pairs={{0,1},{1,0},{2,3},{3,2},{4,5},{5,4},{6,7},{7,6},{8,9},{9,8},{10,11... | collective-permute-start | bytes 1204232 | tf_op jit(solution)/shard_map/ppermute | solution.py:217
  33.4 1.0 copy-start
  63.6 20.9 %collective-permute-start.8 = (s16[272,256]{1,0:T(8,128)(2,1)S(1)}, s16[272,256]{1,0:T(8,128)(2,1)S(1)}, u32[]{:S(2)}, u32[]{:S(2)}) collective-permute-start(s16[272,256]{1,0:T(8,128)(2,1)S(1)} %get-tuple-element.9), channel_id=1, source_target_pairs={{0,0},{1,6},{2,34},{3,36},{4,68},{5,64},{6,102},{7,98},{8,8},{9,14... | collective-permute-start | bytes 417800 | tf_op jit(solution)/shard_map/ppermute | solution.py:282
  77.3 20.9 %collective-permute-start.9 = (s16[272,256]{1,0:T(8,128)(2,1)S(1)}, s16[272,256]{1,0:T(8,128)(2,1)S(1)}, u32[]{:S(2)}, u32[]{:S(2)}) collective-permute-start(s16[272,256]{1,0:T(8,128)(2,1)S(1)} %get-tuple-element.10), channel_id=1, source_target_pairs={{0,2},{1,96},{2,32},{3,66},{4,70},{5,4},{6,100},{7,38},{8,10},{9,2... | collective-permute-start | bytes 417800 | tf_op jit(solution)/shard_map/ppermute | solution.py:282
  98.9 3.2 %collective-permute-start.10 = (f32[128,256]{1,0:T(8,128)S(1)}, f32[128,256]{1,0:T(8,128)S(1)}, u32[]{:S(2)}, u32[]{:S(2)}) collective-permute-start(f32[128,256]{1,0:T(8,128)S(1)} %get-tuple-element.12), channel_id=1, source_target_pairs={{0,1},{1,0},{2,3},{3,2},{4,5},{5,4},{6,7},{7,6},{8,9},{9,8},{10,11... | collective-permute-start | bytes 393224 | tf_op jit(solution)/shard_map/ppermute | solution.py:217

commit v8 on v5

--- a/solution.py
+++ b/solution.py
@@ -138,7 +138,7 @@
         out_ref[i * 2 + 1, 2 * CHIP :, :] = pick_rows([across], HALF).astype(jnp.int16)
 
 
-def middle_kernel(place_ref, in_ref, even_ref, odd_ref):
+def middle_kernel(place_ref, in_ref, first_ref, second_ref):
     tiles = []
     for u in range(2):
         halves = []
@@ -157,17 +157,20 @@
         ref[:CHIP, :] = pair[0]
         ref[CHIP:, :] = jnp.broadcast_to(pair[1], (16, CHIP)).astype(jnp.int16)
 
-    even = lax.rem(place_ref[2], 2) == 0
-
-    @pl.when(even)
+    z = place_ref[3]
+    to = jnp.where(place_ref[1] == 0, z, jnp.where(z < 2, 3 - z, z - 2))
+    far = lax.rem(place_ref[2] + 4 - to, 4) >= 2
+    straight = jnp.logical_xor(far, place_ref[1] == 1)
+
+    @pl.when(straight)
     def _():
-        write(even_ref, first)
-        write(odd_ref, second)
-
-    @pl.when(jnp.logical_not(even))
+        write(first_ref, first)
+        write(second_ref, second)
+
+    @pl.when(jnp.logical_not(straight))
     def _():
-        write(even_ref, second)
-        write(odd_ref, first)
+        write(first_ref, second)
+        write(second_ref, first)
 
 
 def join_kernel(place_ref, a_ref, b_ref, keep_ref, send_ref):
@@ -198,13 +201,16 @@
                         ((x, z, y, CROSS[z]), (y, CROSS[z], x, z)),
                     )
                     for c in range(2):
-                        dest = kinds[c][(s + r) % 2]
-                        pairs.append((index_of(x, s, y, z, c), index_of(*dest, s // 2)))
+                        away = (s - (CROSS[z] if c else z)) % 4
+                        straight = (away >= 2) != (c == 1)
+                        dest = kinds[c][r if straight else 1 - r]
+                        pairs.append((index_of(x, s, y, z, c), index_of(*dest, away % 2)))
     return pairs
 
 
 def shards(raw_blocks, metric_factor, sig_list, live_count):
-    place = jnp.stack([lax.axis_index("y"), lax.axis_index("c"), lax.axis_index("zh")]).astype(jnp.int32)
+    place = jnp.stack([lax.axis_index("y"), lax.axis_index("c"), lax.axis_index("zh"), lax.axis_index("zl")])
+    place = place.astype(jnp.int32)
     own = pl.pallas_call(
         contract_kernel,
         out_shape=jax.ShapeDtypeStruct((PAY, AUX), jnp.bfloat16),

time: 103 us -> 96 us (0.932)
  waiting for transfers between devices: 32.2 us -> 25.6 us
    ppermute x2, waiting for transfers between devices: 19.3 us -> 12.6 us  [shards(): lax.ppermute(a, AXES, far_round(r))]
  transfers between devices with their start and end apart: 8 -> 8, of which waited for: 6 -> 6; matrix products, arithmetic and copies ran while one was open for 0% -> 0% of each run, Pallas kernels for 3% -> 4%
where the time goes in v8:
time: 96 us; the launch traced here: 95.5 us
  starting transfers between devices  32.8 us (34%)
  waiting for transfers between devices  25.6 us (27%)
  blocking collectives  23.3 us (24%)
  Pallas kernels  13.6 us (14%)
    all_to_all x1, blocking collectives, shards(): arrived = lax.all_to_all(tiles, ('x', 'c'), 0, 0, tiled=True)  20.4 us
    ppermute x2, starting transfers between devices, shards(): lax.ppermute(a, AXES, far_round(r))  17.1 us
    ppermute x2, waiting for transfers between devices, shards(): lax.ppermute(a, AXES, far_round(r))  12.6 us
    ppermute x1, waiting for transfers between devices, shards(): lax.ppermute(both, ('zl', 'c'), [(CROSS[i] * 2, i * 2) for i in range(4)]...  9.02 us
    ppermute x3, starting transfers between devices, shards(): lax.ppermute(own, 'y', [((i + d) % 4, i) for i in range(4)])  7.92 us
    pallas_call x1, Pallas kernels, shards(): pl.pallas_call(pairs_kernel, out_shape=jax.ShapeDtypeStruct((8, CHUNK, HA...  5 us
    ppermute x2, starting transfers between devices, swap(): return lax.ppermute(a, 'c', [(0, 1), (1, 0)])  4.16 us
    ppermute x1, starting transfers between devices, shards(): lax.ppermute(both, ('zl', 'c'), [(CROSS[i] * 2, i * 2) for i in range(4)]...  3.67 us
  transfers between devices with their start and end apart: 8, of which 6 were waited for; matrix products, arithmetic and copies ran while one was open for 0% of the time, Pallas kernels for 4%

profile of v8, /device:TPU:81, one launch (start us, length us, event | category | flops | bytes accessed | tf_op | source)
XLA Modules:
  0.0 95.5 jit_solution(13223928004968023788)
XLA Ops:
  0.0 2.9 %contract.1.refs_0_ = bf16[784,256]{1,0:T(8,128)(2,1)} custom-call(bf16[2,6,64,256]{3,2,1,0:T(8,128)(2,1)} %raw_hbm.1, bf16[256,256]{1,0:T(8,128)(2,1)} %metric_hbm.1, s32[2,6]{1,0:T(2,128)} %sig_ref.1, s32[2]{0:T(128)} %bitcast.8), custom_call_target="tpu_custom_call" | custom-call | tf_op jit(solution)/shard_map/contract/pallas_call | solution.py:214
  2.9 2.9 %all-gather = bf16[1568,256]{1,0:T(8,128)(2,1)S(1)} all-gather(bf16[784,256]{1,0:T(8,128)(2,1)} %contract.1.refs_0_), channel_id=2, replica_groups=mesh['x'=4,'zh'=4,'y'=4,'zl'=4,'c'=2] {'c'}, dimensions={0}, use_global_device_ids=true | all-gather | bytes 1204224 | tf_op jit(solution)/shard_map/all_gather | solution.py:231
  5.8 0.0 copy-start
  5.8 3.7 %collective-permute-start.3 = (bf16[2,784,256]{2,1,0:T(8,128)(2,1)S(1)}, bf16[2,784,256]{2,1,0:T(8,128)(2,1)S(1)}, u32[]{:S(2)}, u32[]{:S(2)}) collective-permute-start(bf16[2,784,256]{2,1,0:T(8,128)(2,1)S(1)} %bitcast.6), channel_id=1, source_target_pairs={{6,0},{4,2},{0,4},{2,6},{3,1},{1,3},{7,5},{5,7},{14,8},{12,10},{8,... | collective-permute-start | bytes 2408456 | tf_op jit(solution)/shard_map/ppermute | solution.py:232
  9.5 2.0 %collective-permute-start = (bf16[784,256]{1,0:T(8,128)(2,1)}, bf16[784,256]{1,0:T(8,128)(2,1)S(1)}, u32[]{:S(2)}, u32[]{:S(2)}) collective-permute-start(bf16[784,256]{1,0:T(8,128)(2,1)} %contract.1.refs_0_), channel_id=1, source_target_pairs={{16,0},{24,8},{0,16},{8,24},{17,1},{25,9},{1,17},{9,25},{18,2},{26... | collective-permute-start | bytes 1204232 | tf_op jit(solution)/shard_map/ppermute | solution.py:237
  11.5 4.0 %collective-permute-start.1 = (bf16[784,256]{1,0:T(8,128)(2,1)}, bf16[784,256]{1,0:T(8,128)(2,1)S(1)}, u32[]{:S(2)}, u32[]{:S(2)}) collective-permute-start(bf16[784,256]{1,0:T(8,128)(2,1)} %contract.1.refs_0_), channel_id=1, source_target_pairs={{8,0},{16,8},{24,16},{0,24},{9,1},{17,9},{25,17},{1,25},{10,2},{18... | collective-permute-start | bytes 1204232 | tf_op jit(solution)/shard_map/ppermute | solution.py:237
  15.5 1.9 %collective-permute-start.2 = (bf16[784,256]{1,0:T(8,128)(2,1)}, bf16[784,256]{1,0:T(8,128)(2,1)S(1)}, u32[]{:S(2)}, u32[]{:S(2)}) collective-permute-start(bf16[784,256]{1,0:T(8,128)(2,1)} %contract.1.refs_0_), channel_id=1, source_target_pairs={{24,0},{0,8},{8,16},{16,24},{25,1},{1,9},{9,17},{17,25},{26,2},{2,... | collective-permute-start | bytes 1204232 | tf_op jit(solution)/shard_map/ppermute | solution.py:237
  17.4 0.9 rows.2.own_rows
  18.3 0.1 pad_add_fusion.place_ref
  18.4 9.0 %collective-permute-done.3.src = bf16[2,784,256]{2,1,0:T(8,128)(2,1)S(1)} collective-permute-done((bf16[2,784,256]{2,1,0:T(8,128)(2,1)S(1)}, bf16[2,784,256]{2,1,0:T(8,128)(2,1)S(1)}, u32[]{:S(2)}, u32[]{:S(2)}) %collective-permute-start.3) | collective-permute-done | bytes 802848 | tf_op jit(solution)/shard_map/ppermute | solution.py:232
  27.4 2.2 %collective-permute-start.4 = (bf16[2,784,256]{2,1,0:T(8,128)(2,1)S(1)}, bf16[2,784,256]{2,1,0:T(8,128)(2,1)S(1)}, u32[]{:S(2)}, u32[]{:S(2)}) collective-permute-start(bf16[2,784,256]{2,1,0:T(8,128)(2,1)S(1)} %collective-permute-done.3.src), channel_id=1, source_target_pairs={{0,1},{1,0},{2,3},{3,2},{4,5},{5,4},{6,7},{7,6},{8,9},{9,8},{10,11... | collective-permute-start | bytes 2408456 | tf_op jit(solution)/shard_map/ppermute | solution.py:229
  29.7 0.0 collective-permute-done.refs_1_
  29.7 1.6 %collective-permute-done.1.refs_2_ = bf16[784,256]{1,0:T(8,128)(2,1)S(1)} collective-permute-done((bf16[784,256]{1,0:T(8,128)(2,1)}, bf16[784,256]{1,0:T(8,128)(2,1)S(1)}, u32[]{:S(2)}, u32[]{:S(2)}) %collective-permute-start.1) | collective-permute-done | bytes 401440 | tf_op jit(solution)/shard_map/ppermute | solution.py:237
  31.3 1.0 %collective-permute-done.2.refs_3_ = bf16[784,256]{1,0:T(8,128)(2,1)S(1)} collective-permute-done((bf16[784,256]{1,0:T(8,128)(2,1)}, bf16[784,256]{1,0:T(8,128)(2,1)S(1)}, u32[]{:S(2)}, u32[]{:S(2)}) %collective-permute-start.2) | collective-permute-done | bytes 401440 | tf_op jit(solution)/shard_map/ppermute | solution.py:237
  32.3 0.0 copy-done
  32.3 1.8 %column.1.cols = bf16[512,4096]{1,0:T(8,128)(2,1)S(1)} custom-call(s32[4]{0:T(128)S(1)} %pad_add_fusion.place_ref, bf16[784,256]{1,0:T(8,128)(2,1)S(1)} %copy-done, bf16[784,256]{1,0:T(8,128)(2,1)S(1)} %collective-permute-done.refs_1_, bf16[784,256]{1,0:T(8,128)(2,1)S(1)} %collective-permute-done.1.refs_2_, bf16[784,256]{1,0:T(8,128)(2,1)S(1)} %collective-permute-done.2.refs_3_), custom_call_target="tpu_custom_call" | custom-call | flops 20000000000 | bytes 6000000 | tf_op jit(solution)/shard_map/column/pallas_call | solution.py:257
  34.1 0.9 rows.3.first_rows
  35.0 0.0 collective-permute-done.4.src
  35.0 5.0 %pairs.1 = s16[8,528,128]{2,1,0:T(8,128)(2,1)S(1)} custom-call(s32[4]{0:T(128)S(1)} %pad_add_fusion.place_ref, bf16[512,4096]{1,0:T(8,128)(2,1)S(1)} %column.1.cols, bf16[256,4096]{1,0:T(8,128)(2,1)S(1)} %rows.2.own_rows, bf16[256,4096]{1,0:T(8,128)(2,1)S(1)} %rows.3.first_rows, bf16[2,784,256]{2,1,0:T(8,128)(2,1)S(1)} %collective-permute-done.4.src), custom_call_target="tpu_custom_call" | custom-call | tf_op jit(solution)/shard_map/pairs/pallas_call | solution.py:267
  40.0 20.4 %all_to_all.5.in_ref = s16[8,528,128]{2,1,0:T(8,128)(2,1)S(1)} all-to-all(s16[8,528,128]{2,1,0:T(8,128)(2,1)S(1)} %pairs.1), channel_id=1, replica_groups=mesh['x'=4,'zh'=4,'y'=4,'zl'=4,'c'=2] {'x','c'}, dimensions={0} | all-to-all | bytes 2162688 | tf_op jit(solution)/shard_map/all_to_all | solution.py:276
  60.4 0.9 middle.1
  61.3 13.0 %collective-permute-start.5 = (s16[272,256]{1,0:T(8,128)(2,1)S(1)}, s16[272,256]{1,0:T(8,128)(2,1)S(1)}, u32[]{:S(2)}, u32[]{:S(2)}) collective-permute-start(s16[272,256]{1,0:T(8,128)(2,1)S(1)} %get-tuple-element.9), channel_id=1, source_target_pairs={{0,2},{1,7},{2,35},{3,66},{4,68},{5,64},{6,101},{7,39},{8,10},{9,1... | collective-permute-start | bytes 417800 | tf_op jit(solution)/shard_map/ppermute | solution.py:294
  74.3 4.1 %collective-permute-start.6 = (s16[272,256]{1,0:T(8,128)(2,1)S(1)}, s16[272,256]{1,0:T(8,128)(2,1)S(1)}, u32[]{:S(2)}, u32[]{:S(2)}) collective-permute-start(s16[272,256]{1,0:T(8,128)(2,1)S(1)} %get-tuple-element.10), channel_id=1, source_target_pairs={{0,0},{1,97},{2,33},{3,36},{4,70},{5,4},{6,103},{7,99},{8,8},{9,22... | collective-permute-start | bytes 417800 | tf_op jit(solution)/shard_map/ppermute | solution.py:294
  78.4 5.7 %collective-permute-done.5.a_ref = s16[272,256]{1,0:T(8,128)(2,1)S(1)} collective-permute-done((s16[272,256]{1,0:T(8,128)(2,1)S(1)}, s16[272,256]{1,0:T(8,128)(2,1)S(1)}, u32[]{:S(2)}, u32[]{:S(2)}) %collective-permute-start.5) | collective-permute-done | bytes 139296 | tf_op jit(solution)/shard_map/ppermute | solution.py:294
  84.1 6.9 %collective-permute-done.6.b_ref = s16[272,256]{1,0:T(8,128)(2,1)S(1)} collective-permute-done((s16[272,256]{1,0:T(8,128)(2,1)S(1)}, s16[272,256]{1,0:T(8,128)(2,1)S(1)}, u32[]{:S(2)}, u32[]{:S(2)}) %collective-permute-start.6) | collective-permute-done | bytes 139296 | tf_op jit(solution)/shard_map/ppermute | solution.py:294
  91.0 0.6 join.1
  91.6 1.9 %collective-permute-start.7 = (f32[128,256]{1,0:T(8,128)S(1)}, f32[128,256]{1,0:T(8,128)S(1)}, u32[]{:S(2)}, u32[]{:S(2)}) collective-permute-start(f32[128,256]{1,0:T(8,128)S(1)} %get-tuple-element.12), channel_id=1, source_target_pairs={{0,1},{1,0},{2,3},{3,2},{4,5},{5,4},{6,7},{7,6},{8,9},{9,8},{10,11... | collective-permute-start | bytes 393224 | tf_op jit(solution)/shard_map/ppermute | solution.py:229
  93.6 1.3 %collective-permute-done.7.come_ref = f32[128,256]{1,0:T(8,128)S(1)} collective-permute-done((f32[128,256]{1,0:T(8,128)S(1)}, f32[128,256]{1,0:T(8,128)S(1)}, u32[]{:S(2)}, u32[]{:S(2)}) %collective-permute-start.7) | collective-permute-done | bytes 131104 | tf_op jit(solution)/shard_map/ppermute | solution.py:229
  94.9 0.7 last.1
Async XLA Ops:
  5.8 26.5 %copy-start = (bf16[784,256]{1,0:T(8,128)(2,1)S(1)}, bf16[784,256]{1,0:T(8,128)(2,1)}, u32[]{:S(2)}) copy-start(bf16[784,256]{1,0:T(8,128)(2,1)} %contract.1.refs_0_) | copy-start | bytes 1204228
  5.8 21.6 %collective-permute-start.3 = (bf16[2,784,256]{2,1,0:T(8,128)(2,1)S(1)}, bf16[2,784,256]{2,1,0:T(8,128)(2,1)S(1)}, u32[]{:S(2)}, u32[]{:S(2)}) collective-permute-start(bf16[2,784,256]{2,1,0:T(8,128)(2,1)S(1)} %bitcast.6), channel_id=1, source_target_pairs={{6,0},{4,2},{0,4},{2,6},{3,1},{1,3},{7,5},{5,7},{14,8},{12,10},{8,... | collective-permute-start | bytes 2408456 | tf_op jit(solution)/shard_map/ppermute | solution.py:232
  9.5 20.2 %collective-permute-start = (bf16[784,256]{1,0:T(8,128)(2,1)}, bf16[784,256]{1,0:T(8,128)(2,1)S(1)}, u32[]{:S(2)}, u32[]{:S(2)}) collective-permute-start(bf16[784,256]{1,0:T(8,128)(2,1)} %contract.1.refs_0_), channel_id=1, source_target_pairs={{16,0},{24,8},{0,16},{8,24},{17,1},{25,9},{1,17},{9,25},{18,2},{26... | collective-permute-start | bytes 1204232 | tf_op jit(solution)/shard_map/ppermute | solution.py:237
  11.5 19.9 %collective-permute-start.1 = (bf16[784,256]{1,0:T(8,128)(2,1)}, bf16[784,256]{1,0:T(8,128)(2,1)S(1)}, u32[]{:S(2)}, u32[]{:S(2)}) collective-permute-start(bf16[784,256]{1,0:T(8,128)(2,1)} %contract.1.refs_0_), channel_id=1, source_target_pairs={{8,0},{16,8},{24,16},{0,24},{9,1},{17,9},{25,17},{1,25},{10,2},{18... | collective-permute-start | bytes 1204232 | tf_op jit(solution)/shard_map/ppermute | solution.py:237
  15.5 16.8 %collective-permute-start.2 = (bf16[784,256]{1,0:T(8,128)(2,1)}, bf16[784,256]{1,0:T(8,128)(2,1)S(1)}, u32[]{:S(2)}, u32[]{:S(2)}) collective-permute-start(bf16[784,256]{1,0:T(8,128)(2,1)} %contract.1.refs_0_), channel_id=1, source_target_pairs={{24,0},{0,8},{8,16},{16,24},{25,1},{1,9},{9,17},{17,25},{26,2},{2,... | collective-permute-start | bytes 1204232 | tf_op jit(solution)/shard_map/ppermute | solution.py:237
  27.4 7.6 %collective-permute-start.4 = (bf16[2,784,256]{2,1,0:T(8,128)(2,1)S(1)}, bf16[2,784,256]{2,1,0:T(8,128)(2,1)S(1)}, u32[]{:S(2)}, u32[]{:S(2)}) collective-permute-start(bf16[2,784,256]{2,1,0:T(8,128)(2,1)S(1)} %collective-permute-done.3.src), channel_id=1, source_target_pairs={{0,1},{1,0},{2,3},{3,2},{4,5},{5,4},{6,7},{7,6},{8,9},{9,8},{10,11... | collective-permute-start | bytes 2408456 | tf_op jit(solution)/shard_map/ppermute | solution.py:229
  61.3 22.8 %collective-permute-start.5 = (s16[272,256]{1,0:T(8,128)(2,1)S(1)}, s16[272,256]{1,0:T(8,128)(2,1)S(1)}, u32[]{:S(2)}, u32[]{:S(2)}) collective-permute-start(s16[272,256]{1,0:T(8,128)(2,1)S(1)} %get-tuple-element.9), channel_id=1, source_target_pairs={{0,2},{1,7},{2,35},{3,66},{4,68},{5,64},{6,101},{7,39},{8,10},{9,1... | collective-permute-start | bytes 417800 | tf_op jit(solution)/shard_map/ppermute | solution.py:294
  74.3 16.7 %collective-permute-start.6 = (s16[272,256]{1,0:T(8,128)(2,1)S(1)}, s16[272,256]{1,0:T(8,128)(2,1)S(1)}, u32[]{:S(2)}, u32[]{:S(2)}) collective-permute-start(s16[272,256]{1,0:T(8,128)(2,1)S(1)} %get-tuple-element.10), channel_id=1, source_target_pairs={{0,0},{1,97},{2,33},{3,36},{4,70},{5,4},{6,103},{7,99},{8,8},{9,22... | collective-permute-start | bytes 417800 | tf_op jit(solution)/shard_map/ppermute | solution.py:294
  91.6 3.2 %collective-permute-start.7 = (f32[128,256]{1,0:T(8,128)S(1)}, f32[128,256]{1,0:T(8,128)S(1)}, u32[]{:S(2)}, u32[]{:S(2)}) collective-permute-start(f32[128,256]{1,0:T(8,128)S(1)} %get-tuple-element.12), channel_id=1, source_target_pairs={{0,1},{1,0},{2,3},{3,2},{4,5},{5,4},{6,7},{7,6},{8,9},{9,8},{10,11... | collective-permute-start | bytes 393224 | tf_op jit(solution)/shard_map/ppermute | solution.py:229

commit v9 on v8

--- a/solution.py
+++ b/solution.py
@@ -98,7 +98,7 @@
 
 
 def column_kernel(place_ref, *refs):
-    column, (out_ref, ids_vmem, ids, sem) = refs[:4], refs[4:]
+    column, (out_ref, ids_vmem, ids, sem) = refs[:4], refs[5:]
     copy = load_ids(column, ids_vmem, ids, sem)
     copy.start()
     out_ref[...] = jnp.zeros_like(out_ref)
@@ -254,16 +254,17 @@
             name="rows",
         )(block)
 
+    first_rows = dense_rows(along)
     dense = pl.pallas_call(
         column_kernel,
         out_shape=jax.ShapeDtypeStruct((4 * HALF, NOB * AUX), jnp.bfloat16),
-        in_specs=[SMEM] + [VMEM] * 4,
+        in_specs=[SMEM] + [VMEM] * 4 + [ANY],
         out_specs=VMEM,
         scratch_shapes=ids_scratch(4),
         compiler_params=params(16),
         cost_estimate=pl.CostEstimate(flops=20_000_000_000, bytes_accessed=6_000_000, transcendentals=0),
         name="column",
-    )(place, *column)
+    )(place, *column, first_rows)
     tiles = pl.pallas_call(
         pairs_kernel,
         out_shape=jax.ShapeDtypeStruct((8, CHUNK, HALF), jnp.int16),
@@ -272,7 +273,7 @@
         scratch_shapes=[pltpu.VMEM((CHIP, NOB * AUX), jnp.bfloat16)] + ids_scratch(2),
         compiler_params=params(16),
         name="pairs",
-    )(place, dense, dense_rows(both), dense_rows(along), swap(along))
+    )(place, dense, dense_rows(both), first_rows, swap(along))
     arrived = lax.all_to_all(tiles, ("x", "c"), 0, 0, tiled=True)
     wide = jax.ShapeDtypeStruct((WIDE, CHIP), jnp.int16)
     messages = pl.pallas_call(

time: 96 us -> 95.4 us (level)
  the two profiles are of different devices: /device:TPU:81 before, /device:TPU:79 now
where the time goes in v9:
time: 95.4 us; the launch traced here: 95.1 us
  starting transfers between devices  36.5 us (38%)
  waiting for transfers between devices  23 us (24%)
  blocking collectives  21.7 us (23%)
  Pallas kernels  13.6 us (14%)
    ppermute x2, starting transfers between devices, shards(): lax.ppermute(a, AXES, far_round(r))  19.6 us
    all_to_all x1, blocking collectives, shards(): arrived = lax.all_to_all(tiles, ('x', 'c'), 0, 0, tiled=True)  18.8 us
    ppermute x2, waiting for transfers between devices, shards(): lax.ppermute(a, AXES, far_round(r))  12.2 us
    ppermute x3, starting transfers between devices, shards(): lax.ppermute(own, 'y', [((i + d) % 4, i) for i in range(4)])  9.21 us
    ppermute x1, waiting for transfers between devices, shards(): lax.ppermute(both, ('zl', 'c'), [(CROSS[i] * 2, i * 2) for i in range(4)]...  7.73 us
    pallas_call x1, Pallas kernels, shards(): pl.pallas_call(pairs_kernel, out_shape=jax.ShapeDtypeStruct((8, CHUNK, HA...  5 us
    ppermute x2, starting transfers between devices, swap(): return lax.ppermute(a, 'c', [(0, 1), (1, 0)])  4.16 us
    ppermute x1, starting transfers between devices, shards(): lax.ppermute(both, ('zl', 'c'), [(CROSS[i] * 2, i * 2) for i in range(4)]...  3.53 us
  transfers between devices with their start and end apart: 8, of which 5 were waited for; matrix products, arithmetic and copies ran while one was open for 0% of the time, Pallas kernels for 4%

profile of v9, /device:TPU:79, one launch (start us, length us, event | category | flops | bytes accessed | tf_op | source)
XLA Modules:
  0.0 95.1 jit_solution(13963439112169562243)
XLA Ops:
  0.0 2.9 %contract.1.refs_0_ = bf16[784,256]{1,0:T(8,128)(2,1)} custom-call(bf16[2,6,64,256]{3,2,1,0:T(8,128)(2,1)} %raw_hbm.1, bf16[256,256]{1,0:T(8,128)(2,1)} %metric_hbm.1, s32[2,6]{1,0:T(2,128)} %sig_ref.1, s32[2]{0:T(128)} %bitcast.8), custom_call_target="tpu_custom_call" | custom-call | tf_op jit(solution)/shard_map/contract/pallas_call | solution.py:214
  2.9 2.9 %all-gather = bf16[1568,256]{1,0:T(8,128)(2,1)S(1)} all-gather(bf16[784,256]{1,0:T(8,128)(2,1)} %contract.1.refs_0_), channel_id=2, replica_groups=mesh['x'=4,'zh'=4,'y'=4,'zl'=4,'c'=2] {'c'}, dimensions={0}, use_global_device_ids=true | all-gather | bytes 1204224 | tf_op jit(solution)/shard_map/all_gather | solution.py:231
  5.8 3.5 %collective-permute-start.3 = (bf16[2,784,256]{2,1,0:T(8,128)(2,1)S(1)}, bf16[2,784,256]{2,1,0:T(8,128)(2,1)S(1)}, u32[]{:S(2)}, u32[]{:S(2)}) collective-permute-start(bf16[2,784,256]{2,1,0:T(8,128)(2,1)S(1)} %bitcast.6), channel_id=1, source_target_pairs={{6,0},{4,2},{0,4},{2,6},{3,1},{1,3},{7,5},{5,7},{14,8},{12,10},{8,... | collective-permute-start | bytes 2408456 | tf_op jit(solution)/shard_map/ppermute | solution.py:232
  9.4 3.9 %collective-permute-start = (bf16[784,256]{1,0:T(8,128)(2,1)}, bf16[784,256]{1,0:T(8,128)(2,1)S(1)}, u32[]{:S(2)}, u32[]{:S(2)}) collective-permute-start(bf16[784,256]{1,0:T(8,128)(2,1)} %contract.1.refs_0_), channel_id=1, source_target_pairs={{16,0},{24,8},{0,16},{8,24},{17,1},{25,9},{1,17},{9,25},{18,2},{26... | collective-permute-start | bytes 1204232 | tf_op jit(solution)/shard_map/ppermute | solution.py:237
  13.3 3.0 %collective-permute-start.1 = (bf16[784,256]{1,0:T(8,128)(2,1)}, bf16[784,256]{1,0:T(8,128)(2,1)S(1)}, u32[]{:S(2)}, u32[]{:S(2)}) collective-permute-start(bf16[784,256]{1,0:T(8,128)(2,1)} %contract.1.refs_0_), channel_id=1, source_target_pairs={{8,0},{16,8},{24,16},{0,24},{9,1},{17,9},{25,17},{1,25},{10,2},{18... | collective-permute-start | bytes 1204232 | tf_op jit(solution)/shard_map/ppermute | solution.py:237
  16.3 2.3 %collective-permute-start.2 = (bf16[784,256]{1,0:T(8,128)(2,1)}, bf16[784,256]{1,0:T(8,128)(2,1)S(1)}, u32[]{:S(2)}, u32[]{:S(2)}) collective-permute-start(bf16[784,256]{1,0:T(8,128)(2,1)} %contract.1.refs_0_), channel_id=1, source_target_pairs={{24,0},{0,8},{8,16},{16,24},{25,1},{1,9},{9,17},{17,25},{26,2},{2,... | collective-permute-start | bytes 1204232 | tf_op jit(solution)/shard_map/ppermute | solution.py:237
  18.6 0.9 rows.3.own_rows
  19.5 0.0 copy-start
  19.5 0.1 pad_add_fusion.place_ref
  19.6 7.7 %collective-permute-done.3.src = bf16[2,784,256]{2,1,0:T(8,128)(2,1)S(1)} collective-permute-done((bf16[2,784,256]{2,1,0:T(8,128)(2,1)S(1)}, bf16[2,784,256]{2,1,0:T(8,128)(2,1)S(1)}, u32[]{:S(2)}, u32[]{:S(2)}) %collective-permute-start.3) | collective-permute-done | bytes 802848 | tf_op jit(solution)/shard_map/ppermute | solution.py:232
  27.3 2.2 %collective-permute-start.4 = (bf16[2,784,256]{2,1,0:T(8,128)(2,1)S(1)}, bf16[2,784,256]{2,1,0:T(8,128)(2,1)S(1)}, u32[]{:S(2)}, u32[]{:S(2)}) collective-permute-start(bf16[2,784,256]{2,1,0:T(8,128)(2,1)S(1)} %collective-permute-done.3.src), channel_id=1, source_target_pairs={{0,1},{1,0},{2,3},{3,2},{4,5},{5,4},{6,7},{7,6},{8,9},{9,8},{10,11... | collective-permute-start | bytes 2408456 | tf_op jit(solution)/shard_map/ppermute | solution.py:229
  29.6 0.9 rows.2.refs_4_.first_rows
  30.4 0.0 collective-permute-done.refs_1_
  30.5 1.7 %collective-permute-done.1.refs_2_ = bf16[784,256]{1,0:T(8,128)(2,1)S(1)} collective-permute-done((bf16[784,256]{1,0:T(8,128)(2,1)}, bf16[784,256]{1,0:T(8,128)(2,1)S(1)}, u32[]{:S(2)}, u32[]{:S(2)}) %collective-permute-start.1) | collective-permute-done | bytes 401440 | tf_op jit(solution)/shard_map/ppermute | solution.py:237
  32.1 0.0 collective-permute-done.2.refs_3_
  32.1 0.0 copy-done
  32.1 1.8 %column.1.cols = bf16[512,4096]{1,0:T(8,128)(2,1)S(1)} custom-call(s32[4]{0:T(128)S(1)} %pad_add_fusion.place_ref, bf16[784,256]{1,0:T(8,128)(2,1)S(1)} %copy-done, bf16[784,256]{1,0:T(8,128)(2,1)S(1)} %collective-permute-done.refs_1_, bf16[784,256]{1,0:T(8,128)(2,1)S(1)} %collective-permute-done.1.refs_2_, ...), custom_call_target="tpu_custom_call" | custom-call | flops 20000000000 | bytes 6000000 | tf_op jit(solution)/shard_map/column/pallas_call | solution.py:258
  33.9 0.0 collective-permute-done.4.src
  34.0 5.0 %pairs.1 = s16[8,528,128]{2,1,0:T(8,128)(2,1)S(1)} custom-call(s32[4]{0:T(128)S(1)} %pad_add_fusion.place_ref, bf16[512,4096]{1,0:T(8,128)(2,1)S(1)} %column.1.cols, bf16[256,4096]{1,0:T(8,128)(2,1)S(1)} %rows.3.own_rows, bf16[256,4096]{1,0:T(8,128)(2,1)S(1)} %rows.2.refs_4_.first_rows, bf16[2,784,256]{2,1,0:T(8,128)(2,1)S(1)} %collective-permute-done.4.src), custom_call_target="tpu_custom_call" | custom-call | tf_op jit(solution)/shard_map/pairs/pallas_call | solution.py:268
  39.0 18.8 %all_to_all.5.in_ref = s16[8,528,128]{2,1,0:T(8,128)(2,1)S(1)} all-to-all(s16[8,528,128]{2,1,0:T(8,128)(2,1)S(1)} %pairs.1), channel_id=1, replica_groups=mesh['x'=4,'zh'=4,'y'=4,'zl'=4,'c'=2] {'x','c'}, dimensions={0} | all-to-all | bytes 2162688 | tf_op jit(solution)/shard_map/all_to_all | solution.py:277
  57.7 0.9 middle.1
  58.6 13.2 %collective-permute-start.5 = (s16[272,256]{1,0:T(8,128)(2,1)S(1)}, s16[272,256]{1,0:T(8,128)(2,1)S(1)}, u32[]{:S(2)}, u32[]{:S(2)}) collective-permute-start(s16[272,256]{1,0:T(8,128)(2,1)S(1)} %get-tuple-element.9), channel_id=1, source_target_pairs={{0,2},{1,7},{2,35},{3,66},{4,68},{5,64},{6,101},{7,39},{8,10},{9,1... | collective-permute-start | bytes 417800 | tf_op jit(solution)/shard_map/ppermute | solution.py:295
  71.8 6.5 %collective-permute-start.6 = (s16[272,256]{1,0:T(8,128)(2,1)S(1)}, s16[272,256]{1,0:T(8,128)(2,1)S(1)}, u32[]{:S(2)}, u32[]{:S(2)}) collective-permute-start(s16[272,256]{1,0:T(8,128)(2,1)S(1)} %get-tuple-element.10), channel_id=1, source_target_pairs={{0,0},{1,97},{2,33},{3,36},{4,70},{5,4},{6,103},{7,99},{8,8},{9,22... | collective-permute-start | bytes 417800 | tf_op jit(solution)/shard_map/ppermute | solution.py:295
  78.3 5.4 %collective-permute-done.5.a_ref = s16[272,256]{1,0:T(8,128)(2,1)S(1)} collective-permute-done((s16[272,256]{1,0:T(8,128)(2,1)S(1)}, s16[272,256]{1,0:T(8,128)(2,1)S(1)}, u32[]{:S(2)}, u32[]{:S(2)}) %collective-permute-start.5) | collective-permute-done | bytes 139296 | tf_op jit(solution)/shard_map/ppermute | solution.py:295
  83.7 6.9 %collective-permute-done.6.b_ref = s16[272,256]{1,0:T(8,128)(2,1)S(1)} collective-permute-done((s16[272,256]{1,0:T(8,128)(2,1)S(1)}, s16[272,256]{1,0:T(8,128)(2,1)S(1)}, u32[]{:S(2)}, u32[]{:S(2)}) %collective-permute-start.6) | collective-permute-done | bytes 139296 | tf_op jit(solution)/shard_map/ppermute | solution.py:295
  90.5 0.6 join.1
  91.2 1.9 %collective-permute-start.7 = (f32[128,256]{1,0:T(8,128)S(1)}, f32[128,256]{1,0:T(8,128)S(1)}, u32[]{:S(2)}, u32[]{:S(2)}) collective-permute-start(f32[128,256]{1,0:T(8,128)S(1)} %get-tuple-element.12), channel_id=1, source_target_pairs={{0,1},{1,0},{2,3},{3,2},{4,5},{5,4},{6,7},{7,6},{8,9},{9,8},{10,11... | collective-permute-start | bytes 393224 | tf_op jit(solution)/shard_map/ppermute | solution.py:229
  93.1 1.3 %collective-permute-done.7.come_ref = f32[128,256]{1,0:T(8,128)S(1)} collective-permute-done((f32[128,256]{1,0:T(8,128)S(1)}, f32[128,256]{1,0:T(8,128)S(1)}, u32[]{:S(2)}, u32[]{:S(2)}) %collective-permute-start.7) | collective-permute-done | bytes 131104 | tf_op jit(solution)/shard_map/ppermute | solution.py:229
  94.4 0.7 last.1
Async XLA Ops:
  5.8 21.5 %collective-permute-start.3 = (bf16[2,784,256]{2,1,0:T(8,128)(2,1)S(1)}, bf16[2,784,256]{2,1,0:T(8,128)(2,1)S(1)}, u32[]{:S(2)}, u32[]{:S(2)}) collective-permute-start(bf16[2,784,256]{2,1,0:T(8,128)(2,1)S(1)} %bitcast.6), channel_id=1, source_target_pairs={{6,0},{4,2},{0,4},{2,6},{3,1},{1,3},{7,5},{5,7},{14,8},{12,10},{8,... | collective-permute-start | bytes 2408456 | tf_op jit(solution)/shard_map/ppermute | solution.py:232
  9.4 21.1 %collective-permute-start = (bf16[784,256]{1,0:T(8,128)(2,1)}, bf16[784,256]{1,0:T(8,128)(2,1)S(1)}, u32[]{:S(2)}, u32[]{:S(2)}) collective-permute-start(bf16[784,256]{1,0:T(8,128)(2,1)} %contract.1.refs_0_), channel_id=1, source_target_pairs={{16,0},{24,8},{0,16},{8,24},{17,1},{25,9},{1,17},{9,25},{18,2},{26... | collective-permute-start | bytes 1204232 | tf_op jit(solution)/shard_map/ppermute | solution.py:237
  13.3 18.9 %collective-permute-start.1 = (bf16[784,256]{1,0:T(8,128)(2,1)}, bf16[784,256]{1,0:T(8,128)(2,1)S(1)}, u32[]{:S(2)}, u32[]{:S(2)}) collective-permute-start(bf16[784,256]{1,0:T(8,128)(2,1)} %contract.1.refs_0_), channel_id=1, source_target_pairs={{8,0},{16,8},{24,16},{0,24},{9,1},{17,9},{25,17},{1,25},{10,2},{18... | collective-permute-start | bytes 1204232 | tf_op jit(solution)/shard_map/ppermute | solution.py:237
  16.3 15.9 %collective-permute-start.2 = (bf16[784,256]{1,0:T(8,128)(2,1)}, bf16[784,256]{1,0:T(8,128)(2,1)S(1)}, u32[]{:S(2)}, u32[]{:S(2)}) collective-permute-start(bf16[784,256]{1,0:T(8,128)(2,1)} %contract.1.refs_0_), channel_id=1, source_target_pairs={{24,0},{0,8},{8,16},{16,24},{25,1},{1,9},{9,17},{17,25},{26,2},{2,... | collective-permute-start | bytes 1204232 | tf_op jit(solution)/shard_map/ppermute | solution.py:237
  19.5 12.7 %copy-start = (bf16[784,256]{1,0:T(8,128)(2,1)S(1)}, bf16[784,256]{1,0:T(8,128)(2,1)}, u32[]{:S(2)}) copy-start(bf16[784,256]{1,0:T(8,128)(2,1)} %contract.1.refs_0_) | copy-start | bytes 1204228
  27.3 6.6 %collective-permute-start.4 = (bf16[2,784,256]{2,1,0:T(8,128)(2,1)S(1)}, bf16[2,784,256]{2,1,0:T(8,128)(2,1)S(1)}, u32[]{:S(2)}, u32[]{:S(2)}) collective-permute-start(bf16[2,784,256]{2,1,0:T(8,128)(2,1)S(1)} %collective-permute-done.3.src), channel_id=1, source_target_pairs={{0,1},{1,0},{2,3},{3,2},{4,5},{5,4},{6,7},{7,6},{8,9},{9,8},{10,11... | collective-permute-start | bytes 2408456 | tf_op jit(solution)/shard_map/ppermute | solution.py:229
  58.6 25.0 %collective-permute-start.5 = (s16[272,256]{1,0:T(8,128)(2,1)S(1)}, s16[272,256]{1,0:T(8,128)(2,1)S(1)}, u32[]{:S(2)}, u32[]{:S(2)}) collective-permute-start(s16[272,256]{1,0:T(8,128)(2,1)S(1)} %get-tuple-element.9), channel_id=1, source_target_pairs={{0,2},{1,7},{2,35},{3,66},{4,68},{5,64},{6,101},{7,39},{8,10},{9,1... | collective-permute-start | bytes 417800 | tf_op jit(solution)/shard_map/ppermute | solution.py:295
  71.8 18.7 %collective-permute-start.6 = (s16[272,256]{1,0:T(8,128)(2,1)S(1)}, s16[272,256]{1,0:T(8,128)(2,1)S(1)}, u32[]{:S(2)}, u32[]{:S(2)}) collective-permute-start(s16[272,256]{1,0:T(8,128)(2,1)S(1)} %get-tuple-element.10), channel_id=1, source_target_pairs={{0,0},{1,97},{2,33},{3,36},{4,70},{5,4},{6,103},{7,99},{8,8},{9,22... | collective-permute-start | bytes 417800 | tf_op jit(solution)/shard_map/ppermute | solution.py:295
  91.2 3.2 %collective-permute-start.7 = (f32[128,256]{1,0:T(8,128)S(1)}, f32[128,256]{1,0:T(8,128)S(1)}, u32[]{:S(2)}, u32[]{:S(2)}) collective-permute-start(f32[128,256]{1,0:T(8,128)S(1)} %get-tuple-element.12), channel_id=1, source_target_pairs={{0,1},{1,0},{2,3},{3,2},{4,5},{5,4},{6,7},{7,6},{8,9},{9,8},{10,11... | collective-permute-start | bytes 393224 | tf_op jit(solution)/shard_map/ppermute | solution.py:229

commit v10 on v9

--- a/solution.py
+++ b/solution.py
@@ -93,7 +93,8 @@
 
 
 TYPES = 3
-CHUNK = 2 * CHIP + 16
+CHUNK = TYPES * CHIP + 16
+PART = 2 * CHIP + 16
 WIDE = CHIP + 16
 
 
@@ -121,34 +122,49 @@
     core = place_ref[1]
     rows_kernel(src, rows, ids_vmem, ids, sem)
     exponents = {}
-    places = ((0, 0), (1 - core, core * CHIP), (core, (1 - core) * CHIP))
+    places = (0, (2 - core) * CHIP, (1 + core) * CHIP)
     for t, block in enumerate((own_rows, first_rows, rows)):
         part = lax.dot_general(block[...], cols[...], NT, preferred_element_type=jnp.float32)
-        chunk, first = places[t]
         for i in range(4):
             coded, exponents[t, i] = encode(part[:, i * HALF : (i + 1) * HALF])
-            at = pl.ds(first if t == 0 else pl.multiple_of(first, CHIP), CHIP)
-            out_ref[i * 2 + chunk, at, :] = coded
+            at = pl.ds(places[t] if t == 0 else pl.multiple_of(places[t], CHIP), CHIP)
+            out_ref[i, at, :] = coded
     zero = core == 0
     for i in range(4):
-        out_ref[i * 2 + 1, CHIP : 2 * CHIP, :] = jnp.zeros((CHIP, HALF), jnp.int16)
         near = jnp.where(zero, exponents[2, i], exponents[1, i])
         across = jnp.where(zero, exponents[1, i], exponents[2, i])
-        out_ref[i * 2, 2 * CHIP :, :] = pick_rows([exponents[0, i], near], HALF).astype(jnp.int16)
-        out_ref[i * 2 + 1, 2 * CHIP :, :] = pick_rows([across], HALF).astype(jnp.int16)
-
-
-def middle_kernel(place_ref, in_ref, first_ref, second_ref):
+        block = pick_rows([exponents[0, i], near, across], HALF)
+        out_ref[i, TYPES * CHIP :, :] = block.astype(jnp.int16)
+
+
+def sum_kernel(place_ref, in_ref, keep_ref, send_ref):
+    totals = []
+    for t in range(TYPES):
+        total = None
+        for x in range(4):
+            exps = in_ref[x, TYPES * CHIP :, :].astype(jnp.int32)
+            value = decode(in_ref[x, t * CHIP : (t + 1) * CHIP, :], exps, t)
+            total = value if total is None else total + value
+        totals.append(total)
+    zero = place_ref[1] == 0
+    keep_ref[:CHIP, :] = jnp.where(zero, totals[0], totals[2])
+    keep_ref[CHIP:, :] = totals[1]
+    exponents = []
+    for u, total in enumerate((jnp.where(zero, totals[2], totals[0]), totals[1])):
+        coded, exponent = encode(total)
+        send_ref[u * CHIP : (u + 1) * CHIP, :] = coded
+        exponents.append(exponent)
+    send_ref[2 * CHIP :, :] = pick_rows(exponents, HALF).astype(jnp.int16)
+
+
+def middle_kernel(place_ref, keep_ref, come_ref, first_ref, second_ref):
     tiles = []
+    zero = place_ref[1] == 0
+    exps = come_ref[2 * CHIP :, :].astype(jnp.int32)
     for u in range(2):
-        halves = []
-        for k in range(2):
-            total = None
-            for x in range(4):
-                exps = in_ref[x * 2 + k, 2 * CHIP :, :].astype(jnp.int32)
-                value = decode(in_ref[x * 2 + k, u * CHIP : (u + 1) * CHIP, :], exps, u)
-                total = value if total is None else total + value
-            halves.append(total)
+        rows = slice(u * CHIP, (u + 1) * CHIP)
+        kept, come = keep_ref[rows, :], decode(come_ref[rows, :], exps, u)
+        halves = [jnp.where(zero, kept, come), jnp.where(zero, come, kept)]
         tiles.append(jnp.concatenate(halves, axis=1))
     first = encode(tiles[0])
     second = encode(jnp.where(place_ref[1] == 0, tiles[1], tiles[0].T))
@@ -267,23 +283,34 @@
     )(place, *column, first_rows)
     tiles = pl.pallas_call(
         pairs_kernel,
-        out_shape=jax.ShapeDtypeStruct((8, CHUNK, HALF), jnp.int16),
+        out_shape=jax.ShapeDtypeStruct((4, CHUNK, HALF), jnp.int16),
         in_specs=[SMEM] + [VMEM] * 4,
         out_specs=VMEM,
         scratch_shapes=[pltpu.VMEM((CHIP, NOB * AUX), jnp.bfloat16)] + ids_scratch(2),
         compiler_params=params(16),
         name="pairs",
     )(place, dense, dense_rows(both), first_rows, swap(along))
-    arrived = lax.all_to_all(tiles, ("x", "c"), 0, 0, tiled=True)
+    arrived = lax.all_to_all(tiles, "x", 0, 0, tiled=True)
+    kept, part = pl.pallas_call(
+        sum_kernel,
+        out_shape=[
+            jax.ShapeDtypeStruct((2 * CHIP, HALF), jnp.float32),
+            jax.ShapeDtypeStruct((PART, HALF), jnp.int16),
+        ],
+        in_specs=[SMEM, VMEM],
+        out_specs=[VMEM] * 2,
+        compiler_params=params(24),
+        name="sum",
+    )(place, arrived)
     wide = jax.ShapeDtypeStruct((WIDE, CHIP), jnp.int16)
     messages = pl.pallas_call(
         middle_kernel,
         out_shape=[wide] * 2,
-        in_specs=[SMEM, VMEM],
+        in_specs=[SMEM, VMEM, VMEM],
         out_specs=[VMEM] * 2,
         compiler_params=params(24),
         name="middle",
-    )(place, arrived)
+    )(place, kept, swap(part))
     half = jax.ShapeDtypeStruct((HALF, CHIP), jnp.float32)
     keep, send = pl.pallas_call(
         join_kernel,

time: 95.4 us -> 96.3 us (level)
  the two profiles are of different devices: /device:TPU:79 before, /device:TPU:41 now
where the time goes in v10:
time: 96.3 us; the launch traced here: 95.9 us
  starting transfers between devices  45.7 us (47%)
  blocking collectives  18.6 us (19%)
  waiting for transfers between devices  17.1 us (18%)
  Pallas kernels  14.3 us (15%)
    ppermute x2, starting transfers between devices, shards(): lax.ppermute(a, AXES, far_round(r))  17.1 us
    all_to_all x1, blocking collectives, shards(): arrived = lax.all_to_all(tiles, 'x', 0, 0, tiled=True)  15.7 us
    ppermute x3, starting transfers between devices, swap(): return lax.ppermute(a, 'c', [(0, 1), (1, 0)])  14.4 us
    ppermute x3, starting transfers between devices, shards(): lax.ppermute(own, 'y', [((i + d) % 4, i) for i in range(4)])  12.3 us
    ppermute x2, waiting for transfers between devices, shards(): lax.ppermute(a, AXES, far_round(r))  10.4 us
    pallas_call x1, Pallas kernels, shards(): pl.pallas_call(pairs_kernel, out_shape=jax.ShapeDtypeStruct((4, CHUNK, HA...  4.95 us
    ppermute x1, waiting for transfers between devices, shards(): lax.ppermute(both, ('zl', 'c'), [(CROSS[i] * 2, i * 2) for i in range(4)]...  4.33 us
    pallas_call x1, Pallas kernels, shards(): pl.pallas_call(contract_kernel, out_shape=jax.ShapeDtypeStruct((PAY, AUX)...  2.91 us
  transfers between devices with their start and end apart: 9, of which 6 were waited for; matrix products, arithmetic and copies ran while one was open for 0% of the time, Pallas kernels for 4%

profile of v10, /device:TPU:41, one launch (start us, length us, event | category | flops | bytes accessed | tf_op | source)
XLA Modules:
  0.0 95.9 jit_solution(12542384370802301178)
XLA Ops:
  0.0 2.9 %contract.1.refs_0_ = bf16[784,256]{1,0:T(8,128)(2,1)} custom-call(bf16[2,6,64,256]{3,2,1,0:T(8,128)(2,1)} %raw_hbm.1, bf16[256,256]{1,0:T(8,128)(2,1)} %metric_hbm.1, s32[2,6]{1,0:T(2,128)} %sig_ref.1, s32[2]{0:T(128)} %bitcast.8), custom_call_target="tpu_custom_call" | custom-call | tf_op jit(solution)/shard_map/contract/pallas_call | solution.py:230
  2.9 2.9 %all-gather = bf16[1568,256]{1,0:T(8,128)(2,1)S(1)} all-gather(bf16[784,256]{1,0:T(8,128)(2,1)} %contract.1.refs_0_), channel_id=2, replica_groups=mesh['x'=4,'zh'=4,'y'=4,'zl'=4,'c'=2] {'c'}, dimensions={0}, use_global_device_ids=true | all-gather | bytes 1204224 | tf_op jit(solution)/shard_map/all_gather | solution.py:247
  5.8 1.9 %collective-permute-start.3 = (bf16[2,784,256]{2,1,0:T(8,128)(2,1)S(1)}, bf16[2,784,256]{2,1,0:T(8,128)(2,1)S(1)}, u32[]{:S(2)}, u32[]{:S(2)}) collective-permute-start(bf16[2,784,256]{2,1,0:T(8,128)(2,1)S(1)} %bitcast.6), channel_id=1, source_target_pairs={{6,0},{4,2},{0,4},{2,6},{3,1},{1,3},{7,5},{5,7},{14,8},{12,10},{8,... | collective-permute-start | bytes 2408456 | tf_op jit(solution)/shard_map/ppermute | solution.py:248
  7.7 3.9 %collective-permute-start = (bf16[784,256]{1,0:T(8,128)(2,1)}, bf16[784,256]{1,0:T(8,128)(2,1)S(1)}, u32[]{:S(2)}, u32[]{:S(2)}) collective-permute-start(bf16[784,256]{1,0:T(8,128)(2,1)} %contract.1.refs_0_), channel_id=1, source_target_pairs={{16,0},{24,8},{0,16},{8,24},{17,1},{25,9},{1,17},{9,25},{18,2},{26... | collective-permute-start | bytes 1204232 | tf_op jit(solution)/shard_map/ppermute | solution.py:253
  11.7 5.3 %collective-permute-start.1 = (bf16[784,256]{1,0:T(8,128)(2,1)}, bf16[784,256]{1,0:T(8,128)(2,1)S(1)}, u32[]{:S(2)}, u32[]{:S(2)}) collective-permute-start(bf16[784,256]{1,0:T(8,128)(2,1)} %contract.1.refs_0_), channel_id=1, source_target_pairs={{8,0},{16,8},{24,16},{0,24},{9,1},{17,9},{25,17},{1,25},{10,2},{18... | collective-permute-start | bytes 1204232 | tf_op jit(solution)/shard_map/ppermute | solution.py:253
  16.9 3.1 %collective-permute-start.2 = (bf16[784,256]{1,0:T(8,128)(2,1)}, bf16[784,256]{1,0:T(8,128)(2,1)S(1)}, u32[]{:S(2)}, u32[]{:S(2)}) collective-permute-start(bf16[784,256]{1,0:T(8,128)(2,1)} %contract.1.refs_0_), channel_id=1, source_target_pairs={{24,0},{0,8},{8,16},{16,24},{25,1},{1,9},{9,17},{17,25},{26,2},{2,... | collective-permute-start | bytes 1204232 | tf_op jit(solution)/shard_map/ppermute | solution.py:253
  20.0 0.9 rows.3.own_rows
  20.9 0.0 copy-start
  20.9 0.1 pad_add_fusion.place_ref
  21.0 4.3 %collective-permute-done.3.src = bf16[2,784,256]{2,1,0:T(8,128)(2,1)S(1)} collective-permute-done((bf16[2,784,256]{2,1,0:T(8,128)(2,1)S(1)}, bf16[2,784,256]{2,1,0:T(8,128)(2,1)S(1)}, u32[]{:S(2)}, u32[]{:S(2)}) %collective-permute-start.3) | collective-permute-done | bytes 802848 | tf_op jit(solution)/shard_map/ppermute | solution.py:248
  25.4 6.0 %collective-permute-start.4 = (bf16[2,784,256]{2,1,0:T(8,128)(2,1)S(1)}, bf16[2,784,256]{2,1,0:T(8,128)(2,1)S(1)}, u32[]{:S(2)}, u32[]{:S(2)}) collective-permute-start(bf16[2,784,256]{2,1,0:T(8,128)(2,1)S(1)} %collective-permute-done.3.src), channel_id=1, source_target_pairs={{0,1},{1,0},{2,3},{3,2},{4,5},{5,4},{6,7},{7,6},{8,9},{9,8},{10,11... | collective-permute-start | bytes 2408456 | tf_op jit(solution)/shard_map/ppermute | solution.py:245
  31.3 0.9 rows.2.refs_4_.first_rows
  32.2 0.0 collective-permute-done.refs_1_
  32.2 0.0 collective-permute-done.1.refs_2_
  32.2 0.4 collective-permute-done.2.refs_3_
  32.6 0.0 copy-done
  32.6 1.8 %column.1.cols = bf16[512,4096]{1,0:T(8,128)(2,1)S(1)} custom-call(s32[4]{0:T(128)S(1)} %pad_add_fusion.place_ref, bf16[784,256]{1,0:T(8,128)(2,1)S(1)} %copy-done, bf16[784,256]{1,0:T(8,128)(2,1)S(1)} %collective-permute-done.refs_1_, bf16[784,256]{1,0:T(8,128)(2,1)S(1)} %collective-permute-done.1.refs_2_, ...), custom_call_target="tpu_custom_call" | custom-call | flops 20000000000 | bytes 6000000 | tf_op jit(solution)/shard_map/column/pallas_call | solution.py:274
  34.4 0.0 collective-permute-done.4.src
  34.4 5.0 %pairs.1 = s16[4,784,128]{2,1,0:T(8,128)(2,1)S(1)} custom-call(s32[4]{0:T(128)S(1)} %pad_add_fusion.place_ref, bf16[512,4096]{1,0:T(8,128)(2,1)S(1)} %column.1.cols, bf16[256,4096]{1,0:T(8,128)(2,1)S(1)} %rows.3.own_rows, bf16[256,4096]{1,0:T(8,128)(2,1)S(1)} %rows.2.refs_4_.first_rows, bf16[2,784,256]{2,1,0:T(8,128)(2,1)S(1)} %collective-permute-done.4.src), custom_call_target="tpu_custom_call" | custom-call | tf_op jit(solution)/shard_map/pairs/pallas_call | solution.py:284
  39.4 15.7 %all_to_all.5.in_ref = s16[4,784,128]{2,1,0:T(8,128)(2,1)S(1)} all-to-all(s16[4,784,128]{2,1,0:T(8,128)(2,1)S(1)} %pairs.1), channel_id=1, replica_groups=mesh['x'=4,'zh'=4,'y'=4,'zl'=4,'c'=2] {'x'}, dimensions={0} | all-to-all | bytes 1605632 | tf_op jit(solution)/shard_map/all_to_all | solution.py:293
  55.1 0.8 sum.1
  55.9 3.1 %collective-permute-start.5 = (s16[528,128]{1,0:T(8,128)(2,1)S(1)}, s16[528,128]{1,0:T(8,128)(2,1)S(1)}, u32[]{:S(2)}, u32[]{:S(2)}) collective-permute-start(s16[528,128]{1,0:T(8,128)(2,1)S(1)} %get-tuple-element.12), channel_id=1, source_target_pairs={{0,1},{1,0},{2,3},{3,2},{4,5},{5,4},{6,7},{7,6},{8,9},{9,8},{10,11... | collective-permute-start | bytes 405512 | tf_op jit(solution)/shard_map/ppermute | solution.py:245
  59.0 1.0 %collective-permute-done.5.come_ref = s16[528,128]{1,0:T(8,128)(2,1)S(1)} collective-permute-done((s16[528,128]{1,0:T(8,128)(2,1)S(1)}, s16[528,128]{1,0:T(8,128)(2,1)S(1)}, u32[]{:S(2)}, u32[]{:S(2)}) %collective-permute-start.5) | collective-permute-done | bytes 135200 | tf_op jit(solution)/shard_map/ppermute | solution.py:245
  60.0 0.8 middle.1
  60.7 14.1 %collective-permute-start.6 = (s16[272,256]{1,0:T(8,128)(2,1)S(1)}, s16[272,256]{1,0:T(8,128)(2,1)S(1)}, u32[]{:S(2)}, u32[]{:S(2)}) collective-permute-start(s16[272,256]{1,0:T(8,128)(2,1)S(1)} %get-tuple-element.13), channel_id=1, source_target_pairs={{0,2},{1,7},{2,35},{3,66},{4,68},{5,64},{6,101},{7,39},{8,10},{9,1... | collective-permute-start | bytes 417800 | tf_op jit(solution)/shard_map/ppermute | solution.py:322
  74.8 3.0 %collective-permute-start.7 = (s16[272,256]{1,0:T(8,128)(2,1)S(1)}, s16[272,256]{1,0:T(8,128)(2,1)S(1)}, u32[]{:S(2)}, u32[]{:S(2)}) collective-permute-start(s16[272,256]{1,0:T(8,128)(2,1)S(1)} %get-tuple-element.14), channel_id=1, source_target_pairs={{0,0},{1,97},{2,33},{3,36},{4,70},{5,4},{6,103},{7,99},{8,8},{9,22... | collective-permute-start | bytes 417800 | tf_op jit(solution)/shard_map/ppermute | solution.py:322
  77.9 0.5 collective-permute-done.6.a_ref
  78.3 9.9 %collective-permute-done.7.b_ref = s16[272,256]{1,0:T(8,128)(2,1)S(1)} collective-permute-done((s16[272,256]{1,0:T(8,128)(2,1)S(1)}, s16[272,256]{1,0:T(8,128)(2,1)S(1)}, u32[]{:S(2)}, u32[]{:S(2)}) %collective-permute-start.7) | collective-permute-done | bytes 139296 | tf_op jit(solution)/shard_map/ppermute | solution.py:322
  88.3 0.6 join.1
  88.9 5.4 %collective-permute-start.8 = (f32[128,256]{1,0:T(8,128)S(1)}, f32[128,256]{1,0:T(8,128)S(1)}, u32[]{:S(2)}, u32[]{:S(2)}) collective-permute-start(f32[128,256]{1,0:T(8,128)S(1)} %get-tuple-element.16), channel_id=1, source_target_pairs={{0,1},{1,0},{2,3},{3,2},{4,5},{5,4},{6,7},{7,6},{8,9},{9,8},{10,11... | collective-permute-start | bytes 393224 | tf_op jit(solution)/shard_map/ppermute | solution.py:245
  94.2 1.0 %collective-permute-done.8.come_ref = f32[128,256]{1,0:T(8,128)S(1)} collective-permute-done((f32[128,256]{1,0:T(8,128)S(1)}, f32[128,256]{1,0:T(8,128)S(1)}, u32[]{:S(2)}, u32[]{:S(2)}) %collective-permute-start.8) | collective-permute-done | bytes 131104 | tf_op jit(solution)/shard_map/ppermute | solution.py:245
  95.2 0.7 last.1
Async XLA Ops:
  5.8 19.5 %collective-permute-start.3 = (bf16[2,784,256]{2,1,0:T(8,128)(2,1)S(1)}, bf16[2,784,256]{2,1,0:T(8,128)(2,1)S(1)}, u32[]{:S(2)}, u32[]{:S(2)}) collective-permute-start(bf16[2,784,256]{2,1,0:T(8,128)(2,1)S(1)} %bitcast.6), channel_id=1, source_target_pairs={{6,0},{4,2},{0,4},{2,6},{3,1},{1,3},{7,5},{5,7},{14,8},{12,10},{8,... | collective-permute-start | bytes 2408456 | tf_op jit(solution)/shard_map/ppermute | solution.py:248
  7.7 24.5 %collective-permute-start = (bf16[784,256]{1,0:T(8,128)(2,1)}, bf16[784,256]{1,0:T(8,128)(2,1)S(1)}, u32[]{:S(2)}, u32[]{:S(2)}) collective-permute-start(bf16[784,256]{1,0:T(8,128)(2,1)} %contract.1.refs_0_), channel_id=1, source_target_pairs={{16,0},{24,8},{0,16},{8,24},{17,1},{25,9},{1,17},{9,25},{18,2},{26... | collective-permute-start | bytes 1204232 | tf_op jit(solution)/shard_map/ppermute | solution.py:253
  11.7 20.6 %collective-permute-start.1 = (bf16[784,256]{1,0:T(8,128)(2,1)}, bf16[784,256]{1,0:T(8,128)(2,1)S(1)}, u32[]{:S(2)}, u32[]{:S(2)}) collective-permute-start(bf16[784,256]{1,0:T(8,128)(2,1)} %contract.1.refs_0_), channel_id=1, source_target_pairs={{8,0},{16,8},{24,16},{0,24},{9,1},{17,9},{25,17},{1,25},{10,2},{18... | collective-permute-start | bytes 1204232 | tf_op jit(solution)/shard_map/ppermute | solution.py:253
  16.9 15.7 %collective-permute-start.2 = (bf16[784,256]{1,0:T(8,128)(2,1)}, bf16[784,256]{1,0:T(8,128)(2,1)S(1)}, u32[]{:S(2)}, u32[]{:S(2)}) collective-permute-start(bf16[784,256]{1,0:T(8,128)(2,1)} %contract.1.refs_0_), channel_id=1, source_target_pairs={{24,0},{0,8},{8,16},{16,24},{25,1},{1,9},{9,17},{17,25},{26,2},{2,... | collective-permute-start | bytes 1204232 | tf_op jit(solution)/shard_map/ppermute | solution.py:253
  20.9 11.7 %copy-start = (bf16[784,256]{1,0:T(8,128)(2,1)S(1)}, bf16[784,256]{1,0:T(8,128)(2,1)}, u32[]{:S(2)}) copy-start(bf16[784,256]{1,0:T(8,128)(2,1)} %contract.1.refs_0_) | copy-start | bytes 1204228
  25.4 9.1 %collective-permute-start.4 = (bf16[2,784,256]{2,1,0:T(8,128)(2,1)S(1)}, bf16[2,784,256]{2,1,0:T(8,128)(2,1)S(1)}, u32[]{:S(2)}, u32[]{:S(2)}) collective-permute-start(bf16[2,784,256]{2,1,0:T(8,128)(2,1)S(1)} %collective-permute-done.3.src), channel_id=1, source_target_pairs={{0,1},{1,0},{2,3},{3,2},{4,5},{5,4},{6,7},{7,6},{8,9},{9,8},{10,11... | collective-permute-start | bytes 2408456 | tf_op jit(solution)/shard_map/ppermute | solution.py:245
  55.9 4.1 %collective-permute-start.5 = (s16[528,128]{1,0:T(8,128)(2,1)S(1)}, s16[528,128]{1,0:T(8,128)(2,1)S(1)}, u32[]{:S(2)}, u32[]{:S(2)}) collective-permute-start(s16[528,128]{1,0:T(8,128)(2,1)S(1)} %get-tuple-element.12), channel_id=1, source_target_pairs={{0,1},{1,0},{2,3},{3,2},{4,5},{5,4},{6,7},{7,6},{8,9},{9,8},{10,11... | collective-permute-start | bytes 405512 | tf_op jit(solution)/shard_map/ppermute | solution.py:245
  60.7 17.6 %collective-permute-start.6 = (s16[272,256]{1,0:T(8,128)(2,1)S(1)}, s16[272,256]{1,0:T(8,128)(2,1)S(1)}, u32[]{:S(2)}, u32[]{:S(2)}) collective-permute-start(s16[272,256]{1,0:T(8,128)(2,1)S(1)} %get-tuple-element.13), channel_id=1, source_target_pairs={{0,2},{1,7},{2,35},{3,66},{4,68},{5,64},{6,101},{7,39},{8,10},{9,1... | collective-permute-start | bytes 417800 | tf_op jit(solution)/shard_map/ppermute | solution.py:322
  74.8 13.4 %collective-permute-start.7 = (s16[272,256]{1,0:T(8,128)(2,1)S(1)}, s16[272,256]{1,0:T(8,128)(2,1)S(1)}, u32[]{:S(2)}, u32[]{:S(2)}) collective-permute-start(s16[272,256]{1,0:T(8,128)(2,1)S(1)} %get-tuple-element.14), channel_id=1, source_target_pairs={{0,0},{1,97},{2,33},{3,36},{4,70},{5,4},{6,103},{7,99},{8,8},{9,22... | collective-permute-start | bytes 417800 | tf_op jit(solution)/shard_map/ppermute | solution.py:322
  88.9 6.3 %collective-permute-start.8 = (f32[128,256]{1,0:T(8,128)S(1)}, f32[128,256]{1,0:T(8,128)S(1)}, u32[]{:S(2)}, u32[]{:S(2)}) collective-permute-start(f32[128,256]{1,0:T(8,128)S(1)} %get-tuple-element.16), channel_id=1, source_target_pairs={{0,1},{1,0},{2,3},{3,2},{4,5},{5,4},{6,7},{7,6},{8,9},{9,8},{10,11... | collective-permute-start | bytes 393224 | tf_op jit(solution)/shard_map/ppermute | solution.py:245

commit v11 on v9

--- a/solution.py
+++ b/solution.py
@@ -103,7 +103,7 @@
     copy.start()
     out_ref[...] = jnp.zeros_like(out_ref)
     copy.wait()
-    for i, d in enumerate((0, 2, 1, 3)):
+    for i, d in enumerate((0, 1, 3, 2)):
         scatter(column[i], ids, i, out_ref, lax.rem(place_ref[0] + d, 4) * HALF)
 
 
@@ -234,7 +234,7 @@
         ("zl", "c"),
         [(CROSS[i] * 2, i * 2) for i in range(4)] + [((i ^ 1) * 2 + 1, i * 2 + 1) for i in range(4)],
     )
-    column = [own] + [lax.ppermute(own, "y", [((i + d) % 4, i) for i in range(4)]) for d in (2, 1, 3)]
+    column = [own] + [lax.ppermute(own, "y", [((i + d) % 4, i) for i in range(4)]) for d in (1, 3, 2)]
     def ids_scratch(count):
         return [
             pltpu.VMEM((count, 8, 128), jnp.int32),

time: 95.4 us -> 98.3 us (1.030)
  the two profiles are of different devices: /device:TPU:79 before, /device:TPU:35 now
where the time goes in v11:
time: 98.3 us; the launch traced here: 97.9 us
  starting transfers between devices  41.3 us (42%)
  blocking collectives  26.4 us (27%)
  waiting for transfers between devices  16.3 us (17%)
  Pallas kernels  13.6 us (14%)
    all_to_all x1, blocking collectives, shards(): arrived = lax.all_to_all(tiles, ('x', 'c'), 0, 0, tiled=True)  23.5 us
    ppermute x2, starting transfers between devices, shards(): lax.ppermute(a, AXES, far_round(r))  17.4 us
    ppermute x2, starting transfers between devices, swap(): return lax.ppermute(a, 'c', [(0, 1), (1, 0)])  11.8 us
    ppermute x3, starting transfers between devices, shards(): lax.ppermute(own, 'y', [((i + d) % 4, i) for i in range(4)])  10.1 us
    ppermute x2, waiting for transfers between devices, shards(): lax.ppermute(a, AXES, far_round(r))  8.87 us
    ppermute x1, waiting for transfers between devices, shards(): lax.ppermute(both, ('zl', 'c'), [(CROSS[i] * 2, i * 2) for i in range(4)]...  6.5 us
    pallas_call x1, Pallas kernels, shards(): pl.pallas_call(pairs_kernel, out_shape=jax.ShapeDtypeStruct((8, CHUNK, HA...  5 us
    pallas_call x1, Pallas kernels, shards(): pl.pallas_call(contract_kernel, out_shape=jax.ShapeDtypeStruct((PAY, AUX)...  2.91 us
  transfers between devices with their start and end apart: 8, of which 3 were waited for; matrix products, arithmetic and copies ran while one was open for 0% of the time, Pallas kernels for 4%

profile of v11, /device:TPU:35, one launch (start us, length us, event | category | flops | bytes accessed | tf_op | source)
XLA Modules:
  0.0 97.9 jit_solution(2655013398182472068)
XLA Ops:
  0.0 2.9 %contract.1.refs_0_ = bf16[784,256]{1,0:T(8,128)(2,1)} custom-call(bf16[2,6,64,256]{3,2,1,0:T(8,128)(2,1)} %raw_hbm.1, bf16[256,256]{1,0:T(8,128)(2,1)} %metric_hbm.1, s32[2,6]{1,0:T(2,128)} %sig_ref.1, s32[2]{0:T(128)} %bitcast.8), custom_call_target="tpu_custom_call" | custom-call | tf_op jit(solution)/shard_map/contract/pallas_call | solution.py:214
  2.9 2.9 %all-gather = bf16[1568,256]{1,0:T(8,128)(2,1)S(1)} all-gather(bf16[784,256]{1,0:T(8,128)(2,1)} %contract.1.refs_0_), channel_id=2, replica_groups=mesh['x'=4,'zh'=4,'y'=4,'zl'=4,'c'=2] {'c'}, dimensions={0}, use_global_device_ids=true | all-gather | bytes 1204224 | tf_op jit(solution)/shard_map/all_gather | solution.py:231
  5.8 1.9 %collective-permute-start.3 = (bf16[2,784,256]{2,1,0:T(8,128)(2,1)S(1)}, bf16[2,784,256]{2,1,0:T(8,128)(2,1)S(1)}, u32[]{:S(2)}, u32[]{:S(2)}) collective-permute-start(bf16[2,784,256]{2,1,0:T(8,128)(2,1)S(1)} %bitcast.6), channel_id=1, source_target_pairs={{6,0},{4,2},{0,4},{2,6},{3,1},{1,3},{7,5},{5,7},{14,8},{12,10},{8,... | collective-permute-start | bytes 2408456 | tf_op jit(solution)/shard_map/ppermute | solution.py:232
  7.7 4.6 %collective-permute-start = (bf16[784,256]{1,0:T(8,128)(2,1)}, bf16[784,256]{1,0:T(8,128)(2,1)S(1)}, u32[]{:S(2)}, u32[]{:S(2)}) collective-permute-start(bf16[784,256]{1,0:T(8,128)(2,1)} %contract.1.refs_0_), channel_id=1, source_target_pairs={{8,0},{16,8},{24,16},{0,24},{9,1},{17,9},{25,17},{1,25},{10,2},{18... | collective-permute-start | bytes 1204232 | tf_op jit(solution)/shard_map/ppermute | solution.py:237
  12.4 1.9 %collective-permute-start.1 = (bf16[784,256]{1,0:T(8,128)(2,1)}, bf16[784,256]{1,0:T(8,128)(2,1)S(1)}, u32[]{:S(2)}, u32[]{:S(2)}) collective-permute-start(bf16[784,256]{1,0:T(8,128)(2,1)} %contract.1.refs_0_), channel_id=1, source_target_pairs={{24,0},{0,8},{8,16},{16,24},{25,1},{1,9},{9,17},{17,25},{26,2},{2,... | collective-permute-start | bytes 1204232 | tf_op jit(solution)/shard_map/ppermute | solution.py:237
  14.3 3.5 %collective-permute-start.2 = (bf16[784,256]{1,0:T(8,128)(2,1)}, bf16[784,256]{1,0:T(8,128)(2,1)S(1)}, u32[]{:S(2)}, u32[]{:S(2)}) collective-permute-start(bf16[784,256]{1,0:T(8,128)(2,1)} %contract.1.refs_0_), channel_id=1, source_target_pairs={{16,0},{24,8},{0,16},{8,24},{17,1},{25,9},{1,17},{9,25},{18,2},{26... | collective-permute-start | bytes 1204232 | tf_op jit(solution)/shard_map/ppermute | solution.py:237
  17.9 0.9 rows.3.own_rows
  18.8 0.0 copy-start
  18.8 0.1 pad_add_fusion.place_ref
  18.8 6.5 %collective-permute-done.3.src = bf16[2,784,256]{2,1,0:T(8,128)(2,1)S(1)} collective-permute-done((bf16[2,784,256]{2,1,0:T(8,128)(2,1)S(1)}, bf16[2,784,256]{2,1,0:T(8,128)(2,1)S(1)}, u32[]{:S(2)}, u32[]{:S(2)}) %collective-permute-start.3) | collective-permute-done | bytes 802848 | tf_op jit(solution)/shard_map/ppermute | solution.py:232
  25.4 6.0 %collective-permute-start.4 = (bf16[2,784,256]{2,1,0:T(8,128)(2,1)S(1)}, bf16[2,784,256]{2,1,0:T(8,128)(2,1)S(1)}, u32[]{:S(2)}, u32[]{:S(2)}) collective-permute-start(bf16[2,784,256]{2,1,0:T(8,128)(2,1)S(1)} %collective-permute-done.3.src), channel_id=1, source_target_pairs={{0,1},{1,0},{2,3},{3,2},{4,5},{5,4},{6,7},{7,6},{8,9},{9,8},{10,11... | collective-permute-start | bytes 2408456 | tf_op jit(solution)/shard_map/ppermute | solution.py:229
  31.3 0.9 rows.2.refs_4_.first_rows
  32.2 0.0 collective-permute-done.refs_1_
  32.2 0.0 collective-permute-done.1.refs_2_
  32.3 0.0 collective-permute-done.2.refs_3_
  32.3 0.0 copy-done
  32.3 1.8 %column.1.cols = bf16[512,4096]{1,0:T(8,128)(2,1)S(1)} custom-call(s32[4]{0:T(128)S(1)} %pad_add_fusion.place_ref, bf16[784,256]{1,0:T(8,128)(2,1)S(1)} %copy-done, bf16[784,256]{1,0:T(8,128)(2,1)S(1)} %collective-permute-done.refs_1_, bf16[784,256]{1,0:T(8,128)(2,1)S(1)} %collective-permute-done.1.refs_2_, ...), custom_call_target="tpu_custom_call" | custom-call | flops 20000000000 | bytes 6000000 | tf_op jit(solution)/shard_map/column/pallas_call | solution.py:258
  34.1 0.0 collective-permute-done.4.src
  34.1 5.0 %pairs.1 = s16[8,528,128]{2,1,0:T(8,128)(2,1)S(1)} custom-call(s32[4]{0:T(128)S(1)} %pad_add_fusion.place_ref, bf16[512,4096]{1,0:T(8,128)(2,1)S(1)} %column.1.cols, bf16[256,4096]{1,0:T(8,128)(2,1)S(1)} %rows.3.own_rows, bf16[256,4096]{1,0:T(8,128)(2,1)S(1)} %rows.2.refs_4_.first_rows, bf16[2,784,256]{2,1,0:T(8,128)(2,1)S(1)} %collective-permute-done.4.src), custom_call_target="tpu_custom_call" | custom-call | tf_op jit(solution)/shard_map/pairs/pallas_call | solution.py:268
  39.1 23.5 %all_to_all.5.in_ref = s16[8,528,128]{2,1,0:T(8,128)(2,1)S(1)} all-to-all(s16[8,528,128]{2,1,0:T(8,128)(2,1)S(1)} %pairs.1), channel_id=1, replica_groups=mesh['x'=4,'zh'=4,'y'=4,'zl'=4,'c'=2] {'x','c'}, dimensions={0} | all-to-all | bytes 2162688 | tf_op jit(solution)/shard_map/all_to_all | solution.py:277
  62.6 0.9 middle.1
  63.5 12.0 %collective-permute-start.5 = (s16[272,256]{1,0:T(8,128)(2,1)S(1)}, s16[272,256]{1,0:T(8,128)(2,1)S(1)}, u32[]{:S(2)}, u32[]{:S(2)}) collective-permute-start(s16[272,256]{1,0:T(8,128)(2,1)S(1)} %get-tuple-element.9), channel_id=1, source_target_pairs={{0,2},{1,7},{2,35},{3,66},{4,68},{5,64},{6,101},{7,39},{8,10},{9,1... | collective-permute-start | bytes 417800 | tf_op jit(solution)/shard_map/ppermute | solution.py:295
  75.5 5.4 %collective-permute-start.6 = (s16[272,256]{1,0:T(8,128)(2,1)S(1)}, s16[272,256]{1,0:T(8,128)(2,1)S(1)}, u32[]{:S(2)}, u32[]{:S(2)}) collective-permute-start(s16[272,256]{1,0:T(8,128)(2,1)S(1)} %get-tuple-element.10), channel_id=1, source_target_pairs={{0,0},{1,97},{2,33},{3,36},{4,70},{5,4},{6,103},{7,99},{8,8},{9,22... | collective-permute-start | bytes 417800 | tf_op jit(solution)/shard_map/ppermute | solution.py:295
  81.0 0.0 collective-permute-done.5.a_ref
  81.0 8.9 %collective-permute-done.6.b_ref = s16[272,256]{1,0:T(8,128)(2,1)S(1)} collective-permute-done((s16[272,256]{1,0:T(8,128)(2,1)S(1)}, s16[272,256]{1,0:T(8,128)(2,1)S(1)}, u32[]{:S(2)}, u32[]{:S(2)}) %collective-permute-start.6) | collective-permute-done | bytes 139296 | tf_op jit(solution)/shard_map/ppermute | solution.py:295
  89.8 0.6 join.1
  90.5 5.8 %collective-permute-start.7 = (f32[128,256]{1,0:T(8,128)S(1)}, f32[128,256]{1,0:T(8,128)S(1)}, u32[]{:S(2)}, u32[]{:S(2)}) collective-permute-start(f32[128,256]{1,0:T(8,128)S(1)} %get-tuple-element.12), channel_id=1, source_target_pairs={{0,1},{1,0},{2,3},{3,2},{4,5},{5,4},{6,7},{7,6},{8,9},{9,8},{10,11... | collective-permute-start | bytes 393224 | tf_op jit(solution)/shard_map/ppermute | solution.py:229
  96.3 1.0 collective-permute-done.7.come_ref
  97.3 0.7 last.1
Async XLA Ops:
  5.8 19.5 %collective-permute-start.3 = (bf16[2,784,256]{2,1,0:T(8,128)(2,1)S(1)}, bf16[2,784,256]{2,1,0:T(8,128)(2,1)S(1)}, u32[]{:S(2)}, u32[]{:S(2)}) collective-permute-start(bf16[2,784,256]{2,1,0:T(8,128)(2,1)S(1)} %bitcast.6), channel_id=1, source_target_pairs={{6,0},{4,2},{0,4},{2,6},{3,1},{1,3},{7,5},{5,7},{14,8},{12,10},{8,... | collective-permute-start | bytes 2408456 | tf_op jit(solution)/shard_map/ppermute | solution.py:232
  7.7 24.5 %collective-permute-start = (bf16[784,256]{1,0:T(8,128)(2,1)}, bf16[784,256]{1,0:T(8,128)(2,1)S(1)}, u32[]{:S(2)}, u32[]{:S(2)}) collective-permute-start(bf16[784,256]{1,0:T(8,128)(2,1)} %contract.1.refs_0_), channel_id=1, source_target_pairs={{8,0},{16,8},{24,16},{0,24},{9,1},{17,9},{25,17},{1,25},{10,2},{18... | collective-permute-start | bytes 1204232 | tf_op jit(solution)/shard_map/ppermute | solution.py:237
  12.4 19.9 %collective-permute-start.1 = (bf16[784,256]{1,0:T(8,128)(2,1)}, bf16[784,256]{1,0:T(8,128)(2,1)S(1)}, u32[]{:S(2)}, u32[]{:S(2)}) collective-permute-start(bf16[784,256]{1,0:T(8,128)(2,1)} %contract.1.refs_0_), channel_id=1, source_target_pairs={{24,0},{0,8},{8,16},{16,24},{25,1},{1,9},{9,17},{17,25},{26,2},{2,... | collective-permute-start | bytes 1204232 | tf_op jit(solution)/shard_map/ppermute | solution.py:237
  14.3 17.9 %collective-permute-start.2 = (bf16[784,256]{1,0:T(8,128)(2,1)}, bf16[784,256]{1,0:T(8,128)(2,1)S(1)}, u32[]{:S(2)}, u32[]{:S(2)}) collective-permute-start(bf16[784,256]{1,0:T(8,128)(2,1)} %contract.1.refs_0_), channel_id=1, source_target_pairs={{16,0},{24,8},{0,16},{8,24},{17,1},{25,9},{1,17},{9,25},{18,2},{26... | collective-permute-start | bytes 1204232 | tf_op jit(solution)/shard_map/ppermute | solution.py:237
  18.8 13.5 %copy-start = (bf16[784,256]{1,0:T(8,128)(2,1)S(1)}, bf16[784,256]{1,0:T(8,128)(2,1)}, u32[]{:S(2)}) copy-start(bf16[784,256]{1,0:T(8,128)(2,1)} %contract.1.refs_0_) | copy-start | bytes 1204228
  25.4 8.7 %collective-permute-start.4 = (bf16[2,784,256]{2,1,0:T(8,128)(2,1)S(1)}, bf16[2,784,256]{2,1,0:T(8,128)(2,1)S(1)}, u32[]{:S(2)}, u32[]{:S(2)}) collective-permute-start(bf16[2,784,256]{2,1,0:T(8,128)(2,1)S(1)} %collective-permute-done.3.src), channel_id=1, source_target_pairs={{0,1},{1,0},{2,3},{3,2},{4,5},{5,4},{6,7},{7,6},{8,9},{9,8},{10,11... | collective-permute-start | bytes 2408456 | tf_op jit(solution)/shard_map/ppermute | solution.py:229
  63.5 17.4 %collective-permute-start.5 = (s16[272,256]{1,0:T(8,128)(2,1)S(1)}, s16[272,256]{1,0:T(8,128)(2,1)S(1)}, u32[]{:S(2)}, u32[]{:S(2)}) collective-permute-start(s16[272,256]{1,0:T(8,128)(2,1)S(1)} %get-tuple-element.9), channel_id=1, source_target_pairs={{0,2},{1,7},{2,35},{3,66},{4,68},{5,64},{6,101},{7,39},{8,10},{9,1... | collective-permute-start | bytes 417800 | tf_op jit(solution)/shard_map/ppermute | solution.py:295
  75.5 14.3 %collective-permute-start.6 = (s16[272,256]{1,0:T(8,128)(2,1)S(1)}, s16[272,256]{1,0:T(8,128)(2,1)S(1)}, u32[]{:S(2)}, u32[]{:S(2)}) collective-permute-start(s16[272,256]{1,0:T(8,128)(2,1)S(1)} %get-tuple-element.10), channel_id=1, source_target_pairs={{0,0},{1,97},{2,33},{3,36},{4,70},{5,4},{6,103},{7,99},{8,8},{9,22... | collective-permute-start | bytes 417800 | tf_op jit(solution)/shard_map/ppermute | solution.py:295
  90.5 6.8 %collective-permute-start.7 = (f32[128,256]{1,0:T(8,128)S(1)}, f32[128,256]{1,0:T(8,128)S(1)}, u32[]{:S(2)}, u32[]{:S(2)}) collective-permute-start(f32[128,256]{1,0:T(8,128)S(1)} %get-tuple-element.12), channel_id=1, source_target_pairs={{0,1},{1,0},{2,3},{3,2},{4,5},{5,4},{6,7},{7,6},{8,9},{9,8},{10,11... | collective-permute-start | bytes 393224 | tf_op jit(solution)/shard_map/ppermute | solution.py:229
